TPU v7x, 32 devices: a whole 2x2x4 slice. The times are simulated.
32 devices in a mesh: parts: 2 (over x), frame: 16 (over z, y, core).
Axes of the slice: x: 2, y: 2, z: 4, core: 2. Of those that a mesh axis runs over, the one named last changes fastest.
Arguments:
- latent: bfloat16 [32, 32, 64, 512], P(('parts', 'frame')), parts along dimension 0, may hold values from -6 to 6
- column_project: bfloat16 [512, 1536], replicated, may hold values from -0.25 to 0.25
- column_output: bfloat16 [512, 512], replicated, may hold values from -0.25 to 0.25
- row_query_key_value: bfloat16 [512, 1536], replicated, may hold values from -0.25 to 0.25
- row_output: bfloat16 [512, 512], replicated, may hold values from -0.25 to 0.25
- frame_project: bfloat16 [512, 1536], replicated, may hold values from -0.25 to 0.25
- frame_output: bfloat16 [512, 512], replicated, may hold values from -0.25 to 0.25
- expand_weight: bfloat16 [512, 2048], replicated, may hold values from -0.25 to 0.25
- contract_weight: bfloat16 [2048, 512], replicated, may hold values from -0.125 to 0.125
Outputs:
- result: bfloat16 [32, 32, 64, 512], P(('parts', 'frame')), parts along dimension 0
There are 2 independent parts, one for each index of `parts`. A program takes and returns all parts, laid end to end along the dimension named above; an argument that names none is the same for every part. Nothing has to cross between parts.
All inputs are finite; a program needn't handle non-finite values.
Results may differ from a plain program's by a relative error of at most 0.014.
Values may be sent and summed in bfloat16 or wider, within the bound.
No kernel may reach another device: no remote copies, remote signals or barrier semaphores. Data moves between devices by JAX's collectives and lax.ppermute only.
A program may use at most 128 MiB of HBM per device.

v0:
```python
import math

import jax
import jax.numpy as jnp
from jax import lax
from jax.sharding import PartitionSpec as P

HEADS = 8


EPS_NORM = 1e-05
EPS_HEAD = 1e-06


def layer_normalize(stream):
    values = stream.astype(jnp.float32)
    centre = values - jnp.mean(values, axis=-1, keepdims=True)
    spread = jnp.mean(centre * centre, axis=-1, keepdims=True)
    return (centre * lax.rsqrt(spread + EPS_NORM)).astype(jnp.bfloat16)


def head_norm(block, heads):
    reshaped_input = block.reshape(block.shape[:-1] + (heads, block.shape[-1] // heads))
    scaled = reshaped_input * lax.rsqrt(
        jnp.mean(reshaped_input * reshaped_input, axis=-1, keepdims=True) + EPS_HEAD
    )
    return scaled.reshape(block.shape).astype(jnp.bfloat16)


def project(normed, weight, heads):
    width = normed.shape[-1]
    joined = jnp.dot(normed.reshape(-1, width), weight, preferred_element_type=jnp.float32)
    joined = joined.reshape(normed.shape[:-1] + (3 * width,))
    queries = head_norm(joined[..., :width], heads)
    key_block = head_norm(joined[..., width : 2 * width], heads)
    value_block = joined[..., 2 * width :].astype(jnp.bfloat16)
    return (queries, key_block, value_block)


def attend_core(queries, key_block, value_block, axis, heads):
    width = queries.shape[-1]
    head_dimension_size = width // heads
    leading = queries.ndim - 1
    letters = "abcdefg"[:leading]
    query_form = letters[:axis] + "i" + letters[axis + 1 :]
    key_form = letters[:axis] + "j" + letters[axis + 1 :]
    others = letters[:axis] + letters[axis + 1 :]

    def split_heads(block):
        return block.reshape(block.shape[:-1] + (heads, head_dimension_size))

    logits_form = query_form + "hp," + key_form + "hp->" + others + "hij"
    attention_logits = jnp.einsum(
        logits_form,
        split_heads(queries),
        split_heads(key_block),
        preferred_element_type=jnp.float32,
    ) / math.sqrt(head_dimension_size)
    expd = jnp.exp(attention_logits)
    attention_weights = (expd / jnp.sum(expd, axis=-1, keepdims=True)).astype(jnp.bfloat16)
    blend_form = others + "hij," + key_form + "hp->" + query_form + "hp"
    blended_values = jnp.einsum(
        blend_form, attention_weights, split_heads(value_block), preferred_element_type=jnp.float32
    ).astype(jnp.bfloat16)
    return blended_values.reshape(blended_values.shape[:-2] + (width,))


def finish(stream, blended_values, weight):
    width = stream.shape[-1]
    added = jnp.dot(blended_values.reshape(-1, width), weight, preferred_element_type=jnp.float32)
    return (stream.astype(jnp.float32) + added.reshape(stream.shape)).astype(jnp.bfloat16)


def sublayer(stream, weight_in, weight_out, axis, heads):
    queries, key_block, value_block = project(layer_normalize(stream), weight_in, heads)
    return finish(stream, attend_core(queries, key_block, value_block, axis, heads), weight_out)


def feed_forward(stream, weight_in, weight_out):
    width = stream.shape[-1]
    normed = layer_normalize(stream).reshape(-1, width)
    hidden = jax.nn.gelu(jnp.dot(normed, weight_in, preferred_element_type=jnp.float32)).astype(
        jnp.bfloat16
    )
    added = jnp.dot(hidden, weight_out, preferred_element_type=jnp.float32)
    return (stream.astype(jnp.float32) + added.reshape(stream.shape)).astype(jnp.bfloat16)


def per_device(
    latent,
    column_project,
    column_output,
    row_query_key_value,
    row_output,
    frame_project,
    frame_output,
    expand_weight,
    contract_weight,
):
    local_frame_count, rows_here, columns_here, width = latent.shape
    owners = lax.axis_size("frame")
    pixel_share = rows_here * columns_here // owners
    stream = sublayer(latent, column_project, column_output, 1, HEADS)
    stream = sublayer(stream, row_query_key_value, row_output, 2, HEADS)
    grouped = stream.reshape(local_frame_count, owners, pixel_share, width)
    queries, key_block, value_block = project(layer_normalize(grouped), frame_project, HEADS)
    blended_values = attend_core(
        lax.all_to_all(queries, "frame", split_axis=1, concat_axis=0, tiled=True),
        lax.all_to_all(key_block, "frame", split_axis=1, concat_axis=0, tiled=True),
        lax.all_to_all(value_block, "frame", split_axis=1, concat_axis=0, tiled=True),
        0,
        HEADS,
    )
    mixed_home = lax.all_to_all(blended_values, "frame", split_axis=0, concat_axis=1, tiled=True)
    grouped = finish(grouped, mixed_home, frame_output)
    grouped = feed_forward(grouped, expand_weight, contract_weight)
    return grouped.reshape(local_frame_count, rows_here, columns_here, width)


def solution(mesh):
    placed = (P(("parts", "frame"), None, None, None), P(), P(), P(), P(), P(), P(), P(), P())
    return jax.shard_map(
        per_device,
        mesh=mesh,
        in_specs=placed,
        out_specs=P(("parts", "frame"), None, None, None),
        check_vma=False,
    )
```

profile of v0, /device:TPU:18, one launch (start us, length us, event | category | flops | bytes accessed | tf_op | source)
XLA Modules:
  0.0 563.0 jit_solution(14715224706167294361)
XLA Ops:
  17.2 7.5 %mul.267 = f32[32,64,8,64]{3,2,1,0:T(8,128)} reshape(f32[1,32,64,512]{3,2,1,0:T(8,128)} %get-tuple-element.15) | data formatting | bytes 8388608 | tf_op jit(solution)/shard_map/mul | solution.py:25
  35.5 7.5 %mul.269 = f32[1,32,64,512]{3,2,1,0:T(8,128)} reshape(f32[32,64,8,64]{3,2,1,0:T(8,128)} %mul.268) | data formatting | bytes 8388608 | tf_op jit(solution)/shard_map/mul | solution.py:24
  43.0 7.0 %mul.272 = f32[32,64,8,64]{3,2,1,0:T(8,128)} reshape(f32[1,32,64,512]{3,2,1,0:T(8,128)} %get-tuple-element.16) | data formatting | bytes 8388608 | tf_op jit(solution)/shard_map/mul | solution.py:25
  60.9 7.5 %mul.274 = f32[1,32,64,512]{3,2,1,0:T(8,128)} reshape(f32[32,64,8,64]{3,2,1,0:T(8,128)} %mul.273) | data formatting | bytes 8388608 | tf_op jit(solution)/shard_map/mul | solution.py:24
  68.4 9.6 %multiply_convert_fusion.6 = (bf16[1,32,64,512]{3,2,1,0:T(8,128)(2,1)}, bf16[1,32,64,512]{3,2,1,0:T(8,128)(2,1)}) fusion(f32[1,32,64,512]{3,2,1,0:T(8,128)} %mul.269, f32[1,32,64,1536]{3,2,1,0:T(8,128)} %copy-done.2, f32[1,32,64,512]{3,2,1,0:T(8,128)} %mul.274), kind=kLoop, calls=%fused_computation.65 | loop fusion | flops 4194304 | bytes 20971520 | tf_op jit(solution)/shard_map/convert_element_type | solution.py:27
  78.0 6.2 %reshape.537 = bf16[32,64,8,64]{3,2,1,0:T(8,128)(2,1)} reshape(bf16[1,32,64,512]{3,2,1,0:T(8,128)(2,1)} %get-tuple-element.13) | data formatting | bytes 4194304 | tf_op jit(solution)/shard_map/reshape.4
  84.2 6.2 %reshape.538 = bf16[32,64,8,64]{3,2,1,0:T(8,128)(2,1)} reshape(bf16[1,32,64,512]{3,2,1,0:T(8,128)(2,1)} %get-tuple-element.14) | data formatting | bytes 4194304 | tf_op jit(solution)/shard_map/reshape.5
  90.4 6.3 %reshape.536 = bf16[32,64,8,64]{3,2,1,0:T(8,128)(2,1)} reshape(bf16[1,32,64,512]{3,2,1,0:T(8,128)(2,1)} %slice.70) | data formatting | bytes 4194304 | tf_op jit(solution)/shard_map/reshape.8
  96.8 13.8 %fusion.10 = (f32[64,8,32]{2,1,0:T(8,128)S(1)}, f32[64,8,32,32]{2,3,1,0:T(8,128)}) fusion(bf16[32,64,8,64]{3,2,1,0:T(8,128)(2,1)} %reshape.538, bf16[32,64,8,64]{3,2,1,0:T(8,128)(2,1)} %reshape.537), kind=kOutput, calls=%fused_computation.14 | convolution fusion | flops 68141056 | bytes 6356992 | tf_op jit(solution)/shard_map/aichp,ajchp->achij/dot_general | solution.py:53
  110.6 9.7 %convert_bitcast_fusion.1 = bf16[1,32,64,8,64]{4,1,3,2,0:T(8,128)(2,1)} fusion(f32[64,8,32,32]{2,3,1,0:T(8,128)} %get-tuple-element.18, f32[64,8,32]{2,1,0:T(8,128)S(1)} %get-tuple-element.17, bf16[32,64,8,64]{3,2,1,0:T(8,128)(2,1)S(1)} %copy-done.9), kind=kOutput, calls=%fused_computation.62 | convolution fusion | flops 69730304 | bytes 6356992 | tf_op jit(solution)/shard_map/achij,ajchp->aichp/dot_general | solution.py:62
  126.2 6.5 %reshape.539 = bf16[32,64,512]{2,1,0:T(8,128)(2,1)} reshape(bf16[1,32,64,8,64]{4,3,2,1,0:T(8,128)(2,1)} %copy.111) | data formatting | bytes 4194304 | tf_op jit(solution)/shard_map/reshape.298
  150.2 7.0 %mul.280 = f32[32,64,8,64]{3,2,1,0:T(8,128)} reshape(f32[1,32,64,512]{3,2,1,0:T(8,128)} %get-tuple-element.11) | data formatting | bytes 8388608 | tf_op jit(solution)/shard_map/mul | solution.py:25
  168.1 7.9 %mul.282 = f32[1,32,64,512]{3,2,1,0:T(8,128)} reshape(f32[32,64,8,64]{3,2,1,0:T(8,128)} %mul.281) | data formatting | bytes 8388608 | tf_op jit(solution)/shard_map/mul | solution.py:24
  176.0 7.0 %mul.285 = f32[32,64,8,64]{3,2,1,0:T(8,128)} reshape(f32[1,32,64,512]{3,2,1,0:T(8,128)} %get-tuple-element.12) | data formatting | bytes 8388608 | tf_op jit(solution)/shard_map/mul | solution.py:25
  194.0 7.5 %mul.287 = f32[1,32,64,512]{3,2,1,0:T(8,128)} reshape(f32[32,64,8,64]{3,2,1,0:T(8,128)} %mul.286) | data formatting | bytes 8388608 | tf_op jit(solution)/shard_map/mul | solution.py:24
  201.4 9.6 %multiply_convert_fusion.4 = (bf16[1,32,64,512]{3,2,1,0:T(8,128)(2,1)}, bf16[1,32,64,512]{3,2,1,0:T(8,128)(2,1)}) fusion(f32[1,32,64,512]{3,2,1,0:T(8,128)} %mul.282, f32[1,32,64,1536]{3,2,1,0:T(8,128)} %copy-done.3, f32[1,32,64,512]{3,2,1,0:T(8,128)} %mul.287), kind=kLoop, calls=%fused_computation.61 | loop fusion | flops 4194304 | bytes 20971520 | tf_op jit(solution)/shard_map/convert_element_type | solution.py:27
  211.0 6.2 %reshape.542 = bf16[32,64,8,64]{3,2,1,0:T(8,128)(2,1)} reshape(bf16[1,32,64,512]{3,2,1,0:T(8,128)(2,1)} %get-tuple-element.9) | data formatting | bytes 4194304 | tf_op jit(solution)/shard_map/reshape.15
  217.2 6.2 %reshape.543 = bf16[32,64,8,64]{3,2,1,0:T(8,128)(2,1)} reshape(bf16[1,32,64,512]{3,2,1,0:T(8,128)(2,1)} %get-tuple-element.10) | data formatting | bytes 4194304 | tf_op jit(solution)/shard_map/reshape.16
  228.4 6.1 %fusion.11 = (f32[32,8,64]{2,1,0:T(8,128)S(1)}, f32[32,8,64,64]{2,3,1,0:T(8,128)S(1)}) fusion(bf16[32,64,8,64]{3,2,1,0:T(8,128)(2,1)} %reshape.543, bf16[32,64,8,64]{3,2,1,0:T(8,128)(2,1)} %reshape.542), kind=kOutput, calls=%fused_computation.15 | convolution fusion | flops 136298496 | bytes 8454144 | tf_op jit(solution)/shard_map/abihp,abjhp->abhij/dot_general | solution.py:53
  289.8 8.7 %fusion.43 = (bf16[1,16,128,512]{3,2,0,1:T(8,128)(2,1)}, bf16[1,16,128,512]{3,2,0,1:T(8,128)(2,1)S(1)}) fusion(f32[1,16,128,512]{3,2,1,0:T(8,128)} %copy.128, f32[1,16,128,1536]{3,2,1,0:T(8,128)} %copy-done.1, f32[1,16,128,512]{3,2,1,0:T(8,128)} %copy.124), kind=kLoop, calls=%fused_computation.76 | loop fusion | flops 4194304 | bytes 20971520 | tf_op jit(solution)/shard_map/convert_element_type | solution.py:27
  298.5 53.7 %all_to_all.16 = bf16[1,16,128,512]{3,2,0,1:T(8,128)(2,1)} all-to-all(bf16[1,16,128,512]{3,2,0,1:T(8,128)(2,1)S(1)} %get-tuple-element.6), channel_id=1, replica_groups=mesh['parts'=2,'frame'=16] {'frame'}, dimensions={1} | all-to-all | bytes 4194304 | tf_op jit(solution)/shard_map/all_to_all | solution.py:108
  360.9 43.9 %all-to-all-done.2 = bf16[1,16,128,512]{3,2,0,1:T(8,128)(2,1)} async-done(((bf16[1,16,128,512]{3,2,0,1:T(8,128)(2,1)}), bf16[1,16,128,512]{3,2,0,1:T(8,128)(2,1)}, u32[]{:S(2)}, u32[]{:S(2)}) %all-to-all-start.2) | async-done | bytes 2097184 | tf_op jit(solution)/shard_map/all_to_all | solution.py:109
  414.0 7.5 %copy.131 = bf16[16,128,8,64]{3,0,2,1:T(8,128)(2,1)} copy(bf16[16,128,8,64]{1,3,2,0:T(8,128)(2,1)} %bitcast.122) | data formatting | bytes 4194304 | tf_op jit(solution)/shard_map/reshape.35
  425.3 7.5 %copy.132 = bf16[16,128,8,64]{3,0,2,1:T(8,128)(2,1)} copy(bf16[16,128,8,64]{1,3,2,0:T(8,128)(2,1)} %bitcast.123) | data formatting | bytes 4194304 | tf_op jit(solution)/shard_map/reshape.72
  432.8 9.0 %fusion.70 = f32[128,8,16,16]{2,3,1,0:T(8,128)} fusion(bf16[16,128,8,64]{3,0,2,1:T(8,128)(2,1)} %copy.131, bf16[16,128,8,64]{3,0,2,1:T(8,128)(2,1)} %copy.132), kind=kOutput, calls=%fused_computation.118 | convolution fusion | flops 33554432 | bytes 5242880 | tf_op jit(solution)/shard_map/ibchp,jbchp->bchij/dot_general | solution.py:53
  441.8 6.8 %copy.133 = f32[128,8,16,16]{0,3,2,1:T(8,128)S(1)} copy(f32[128,8,16,16]{2,3,1,0:T(8,128)} %fusion.70) | data formatting | bytes 2097152 | tf_op jit(solution)/shard_map/ibchp,jbchp->bchij/dot_general | solution.py:53
  449.9 7.3 %copy.135 = bf16[128,8,16,16]{3,2,1,0:T(8,128)(2,1)} copy(bf16[128,8,16,16]{0,3,2,1:T(8,128)(2,1)} %divide_convert_fusion.8) | data formatting | bytes 1048576 | tf_op jit(solution)/shard_map/convert_element_type | solution.py:60
  461.5 7.5 %copy.134 = bf16[16,128,8,64]{3,0,2,1:T(8,128)(2,1)} copy(bf16[16,128,8,64]{1,3,2,0:T(8,128)(2,1)} %bitcast.124) | data formatting | bytes 4194304 | tf_op jit(solution)/shard_map/reshape.75
  469.0 7.8 %convert_bitcast_fusion = bf16[16,1,128,8,64]{4,0,3,2,1:T(8,128)(2,1)} fusion(bf16[128,8,16,16]{3,2,1,0:T(8,128)(2,1)} %copy.135, bf16[16,128,8,64]{3,0,2,1:T(8,128)(2,1)} %copy.134), kind=kOutput, calls=%fused_computation.55 | convolution fusion | flops 34603008 | bytes 4718592 | tf_op jit(solution)/shard_map/bchij,jbchp->ibchp/dot_general | solution.py:62
  476.7 6.6 %copy.136 = bf16[16,1,128,8,64]{2,4,3,0,1:T(8,128)(2,1)} copy(bf16[16,1,128,8,64]{4,0,3,2,1:T(8,128)(2,1)} %convert_bitcast_fusion) | data formatting | bytes 4194304 | tf_op jit(solution)/shard_map/convert_element_type | solution.py:64
  487.4 53.3 %all_to_all.17 = bf16[16,1,128,512]{3,2,1,0:T(8,128)(2,1)S(1)} all-to-all(bf16[16,1,128,512]{3,2,1,0:T(8,128)(2,1)} %copy.137), channel_id=1, replica_groups=mesh['parts'=2,'frame'=16] {'frame'}, dimensions={0} | all-to-all | bytes 4194304 | tf_op jit(solution)/shard_map/all_to_all | solution.py:114
  545.1 12.8 %fusion.8 = f32[2048,512]{1,0:T(8,128)} fusion(bf16[2048,512]{1,0:T(8,128)(2,1)S(1)} %copy-done, bf16[2048,512]{1,0:T(8,128)(2,1)} %bitcast.129, bf16[512,2048]{1,0:T(8,128)(2,1)} %param.16), kind=kOutput, calls=%fused_computation.13 | convolution fusion | flops 8627683328 | bytes 10485760 | tf_op jit(solution)/shard_map/dot_general | solution.py:85
  (103 shorter events, 184.8 us)
Async XLA Ops:
  0.0 545.1 %copy-start = (bf16[2048,512]{1,0:T(8,128)(2,1)S(1)}, bf16[2048,512]{1,0:T(8,128)(2,1)}, u32[]{:S(2)}) copy-start(bf16[2048,512]{1,0:T(8,128)(2,1)} %param.17) | copy-start | bytes 6291460
  0.0 4.7 copy-start.8
  0.0 4.7 copy-start.12
  8.2 7.2 %copy-start.2 = (f32[1,32,64,1536]{3,2,1,0:T(8,128)}, f32[1,32,64,1536]{3,2,1,0:T(8,128)S(1)}, u32[]{:S(2)}) copy-start(f32[1,32,64,1536]{3,2,1,0:T(8,128)S(1)} %convolution_bitcast_fusion.2) | copy-start | bytes 37748740
  96.8 13.8 %copy-start.9 = (bf16[32,64,8,64]{3,2,1,0:T(8,128)(2,1)S(1)}, bf16[32,64,8,64]{3,2,1,0:T(8,128)(2,1)}, u32[]{:S(2)}) copy-start(bf16[32,64,8,64]{3,2,1,0:T(8,128)(2,1)} %reshape.536) | copy-start | bytes 6291460
  126.2 6.5 %copy-start.14 = (bf16[512,512]{1,0:T(8,128)(2,1)S(1)}, bf16[512,512]{1,0:T(8,128)(2,1)}, u32[]{:S(2)}) copy-start(bf16[512,512]{1,0:T(8,128)(2,1)} %param.11) | copy-start | bytes 1572868
  132.7 5.1 copy-start.13
  136.4 1.4 copy-start.6
  141.3 7.2 %copy-start.3 = (f32[1,32,64,1536]{3,2,1,0:T(8,128)}, f32[1,32,64,1536]{3,2,1,0:T(8,128)S(1)}, u32[]{:S(2)}) copy-start(f32[1,32,64,1536]{3,2,1,0:T(8,128)S(1)} %convolution_bitcast_fusion.1) | copy-start | bytes 37748740
  228.4 6.1 %copy-start.10 = (bf16[1,32,64,512]{2,3,1,0:T(8,128)(2,1)S(1)}, bf16[1,32,64,512]{2,3,1,0:T(8,128)(2,1)}, u32[]{:S(2)}) copy-start(bf16[1,32,64,512]{2,3,1,0:T(8,128)(2,1)} %copy.141) | copy-start | bytes 6291460
  234.5 3.5 copy-start.7
  234.5 3.5 copy-start.11
  251.3 7.0 %copy-start.1 = (f32[1,16,128,1536]{3,2,1,0:T(8,128)}, f32[1,16,128,1536]{3,2,1,0:T(8,128)S(1)}, u32[]{:S(2)}) copy-start(f32[1,16,128,1536]{3,2,1,0:T(8,128)S(1)} %convolution_bitcast_fusion) | copy-start | bytes 37748740
  352.2 52.6 %all-to-all-start.2 = ((bf16[1,16,128,512]{3,2,0,1:T(8,128)(2,1)}), bf16[1,16,128,512]{3,2,0,1:T(8,128)(2,1)}, u32[]{:S(2)}, u32[]{:S(2)}) async-start(bf16[1,16,128,512]{3,2,0,1:T(8,128)(2,1)} %get-tuple-element.5), calls=%async_computation.2 | async-start | bytes 4194304 | tf_op jit(solution)/shard_map/all_to_all | solution.py:109
  404.8 52.8 %all-to-all-start = ((bf16[1,16,128,512]{3,2,0,1:T(8,128)(2,1)}), bf16[1,16,128,512]{3,2,0,1:T(8,128)(2,1)}, u32[]{:S(2)}, u32[]{:S(2)}) async-start(bf16[1,16,128,512]{3,2,0,1:T(8,128)(2,1)} %fusion.44), calls=%async_computation | async-start | bytes 4194304 | tf_op jit(solution)/shard_map/all_to_all | solution.py:110
  483.4 57.3 %copy-start.15 = (bf16[512,512]{1,0:T(8,128)(2,1)S(1)}, bf16[512,512]{1,0:T(8,128)(2,1)}, u32[]{:S(2)}) copy-start(bf16[512,512]{1,0:T(8,128)(2,1)} %param.15) | copy-start | bytes 1572868
  487.3 53.4 %copy-start.5 = (bf16[1,32,64,512]{3,2,1,0:T(8,128)(2,1)S(1)}, bf16[1,32,64,512]{3,2,1,0:T(8,128)(2,1)}, u32[]{:S(2)}) copy-start(bf16[1,32,64,512]{3,2,1,0:T(8,128)(2,1)} %get-tuple-element.24) | copy-start | bytes 6291460
  542.1 1.3 copy-start.4
where the time goes:
time: 572 us; the launch traced here: 563 us
  local copies, waits for them, and re-layouts  228 us (40%)
  blocking collectives  107 us (19%)
  other arithmetic  88.1 us (15%)
  matrix products  85.4 us (15%)
  waiting for transfers between devices  44.3 us (8%)
  starting transfers between devices  10.1 us (2%)
    another operation x10, local copies, waits for them, and re-layouts  65 us
    mul x12, local copies, waits for them, and re-layouts, head_norm(): reshaped_input * lax.rsqrt(jnp.mean(reshaped_input * reshaped_input, axis...  63.6 us
    all_to_all x1, blocking collectives, per_device(): lax.all_to_all(queries, 'frame', split_axis=1, concat_axis=0, tiled=True)  53.7 us
    all_to_all x1, blocking collectives, per_device(): lax.all_to_all(blended_values, 'frame', split_axis=0, concat_axis=1, tile...  53.3 us
    all_to_all x1, waiting for transfers between devices, per_device(): lax.all_to_all(key_block, 'frame', split_axis=1, concat_axis=0, tiled=True)  43.9 us
    mul x6, local copies, waits for them, and re-layouts, head_norm(): reshaped_input * reshaped_input  39.1 us
    dot_general x3, matrix products, attend_core(): jnp.einsum(logits_form, split_heads(queries), split_heads(key_block), pre...  28.9 us
    reduce_sum x6, other arithmetic, head_norm(): jnp.mean(reshaped_input * reshaped_input, axis=-1, keepdims=True) + EPS_HEAD  28.3 us
  transfers between devices with their start and end apart: 2, of which 2 were waited for; matrix products, arithmetic and copies ran while one was open for 9% of the time, Pallas kernels for 0%

commit v1 on v0

v1 whole, which is shorter than its diff:
```python
import functools

import jax
import jax.numpy as jnp
from jax import lax
from jax.experimental import pallas as pl
from jax.experimental.pallas import tpu as pltpu
from jax.sharding import PartitionSpec as P

HEADS = 8
EPS_NORM = 1e-05
EPS_HEAD = 1e-06
BF = jnp.bfloat16
F32 = jnp.float32
SIDE = 16
GROUP = 64


def dot(a, b):
    return jnp.dot(a, b, preferred_element_type=F32)


def dot_nt(a, b):
    return lax.dot_general(a, b, (((1,), (1,)), ((), ())), preferred_element_type=F32)


def iota(shape, dim):
    return lax.broadcasted_iota(jnp.int32, shape, dim)


def swap_matrix():
    n = SIDE * SIDE
    r, c = iota((n, n), 0), iota((n, n), 1)
    hit = (r // SIDE == c % SIDE) & (r % SIDE == c // SIDE)
    return jnp.where(hit, 1.0, 0.0).astype(BF)


def head_blocks(head, value):
    n = 4 * head
    same = iota((n, n), 0) // head == iota((n, n), 1) // head
    return jnp.where(same, value, 0.0).astype(BF)


def layer_normalize(x):
    v = x.astype(F32)
    centre = v - jnp.mean(v, axis=-1, keepdims=True)
    spread = jnp.mean(centre * centre, axis=-1, keepdims=True)
    return (centre * lax.rsqrt(spread + EPS_NORM)).astype(BF)


def head_norm(block, averager, scale):
    half = averager.shape[0]
    squares = (block * block).astype(BF)
    out = []
    for c in range(0, block.shape[1], half):
        mean = dot(squares[:, c : c + half], averager)
        out.append((block[:, c : c + half] * (lax.rsqrt(mean + EPS_HEAD) * scale)).astype(BF))
    return out


def spread_heads(block, head):
    lane = iota(block.shape, 1) // head
    zero = jnp.zeros_like(block)
    return jnp.concatenate([jnp.where(lane == h, block, zero) for h in range(4)], axis=0)


def sublayer(x, project_ref, output_ref, line):
    tokens, width = x.shape
    head = width // HEADS
    half = 4 * head
    averager = head_blocks(head, 1.0 / head)
    summer = head_blocks(head, 1.0)
    normed = layer_normalize(x)
    queries = head_norm(dot(normed, project_ref[:, :width]), averager, head**-0.5)
    keys = head_norm(dot(normed, project_ref[:, width : 2 * width]), averager, 1.0)
    values = dot(normed, project_ref[:, 2 * width :]).astype(BF)
    rows = []
    for s in range(0, tokens, GROUP):
        parts = []
        for c in range(width // half):
            q = queries[c][s : s + GROUP]
            k = spread_heads(keys[c][s : s + GROUP], head)
            v = spread_heads(values[s : s + GROUP, c * half : (c + 1) * half], head)
            e = jnp.exp(dot_nt(q, k))
            if line < GROUP:
                own = iota(e.shape, 0) // line == (iota(e.shape, 1) % GROUP) // line
                e = jnp.where(own, e, 0.0)
            e = e.astype(BF)
            parts.append((dot(e, v) / dot(e, summer)).astype(BF))
        rows.append(jnp.concatenate(parts, axis=1))
    mixed = jnp.concatenate(rows, axis=0)
    return (x.astype(F32) + dot(mixed, output_ref[...])).astype(BF)


def to_lines(x, swap):
    length, side, width = x.shape
    parts = []
    for a in range(0, length, SIDE):
        tile = x[a : a + SIDE].reshape(SIDE * side, width)
        parts.append(dot(swap, tile).astype(BF).reshape(side, SIDE, width))
    return jnp.concatenate(parts, axis=1).reshape(side * length, width)


def from_lines(x, swap, length):
    width = x.shape[1]
    x = x.reshape(SIDE, length, width)
    parts = []
    for a in range(0, length, SIDE):
        tile = x[:, a : a + SIDE].reshape(SIDE * SIDE, width)
        parts.append(dot(swap, tile).astype(BF).reshape(SIDE, SIDE, width))
    return jnp.concatenate(parts, axis=0)


def feed_forward(x, expand_ref, contract_ref):
    hidden = expand_ref.shape[1]
    piece = 512
    normed = layer_normalize(x)
    total = x.astype(F32)
    for c in range(0, hidden, piece):
        h = jax.nn.gelu(dot(normed, expand_ref[:, c : c + piece])).astype(BF)
        total = total + dot(h, contract_ref[c : c + piece])
    return total.astype(BF)


def column_row_kernel(x_ref, cp_ref, co_ref, rp_ref, ro_ref, out_ref, mid_ref):
    rows, columns, width = x_ref.shape
    swap = swap_matrix()

    @pl.loop(0, columns // SIDE)
    def _(g):
        at = pl.ds(pl.multiple_of(g * SIDE, SIDE), SIDE)
        x = to_lines(x_ref[:, at, :], swap)
        y = sublayer(x, cp_ref, co_ref, rows)
        mid_ref[:, at, :] = from_lines(y, swap, rows)

    step = 512 // columns

    @pl.loop(0, rows // step)
    def _(g):
        at = pl.ds(g * step, step)
        x = mid_ref[at].reshape(step * columns, width)
        out_ref[at] = sublayer(x, rp_ref, ro_ref, columns).reshape(step, columns, width)


def frame_kernel(x_ref, fp_ref, fo_ref, we_ref, wc_ref, out_ref):
    frames, pixels, width = x_ref.shape
    swap = swap_matrix()

    @pl.loop(0, pixels // SIDE)
    def _(g):
        at = pl.ds(pl.multiple_of(g * SIDE, SIDE), SIDE)
        x = to_lines(x_ref[:, at, :], swap)
        y = sublayer(x, fp_ref, fo_ref, frames)
        y = feed_forward(y, we_ref, wc_ref)
        out_ref[:, at, :] = from_lines(y, swap, frames)


VMEM = pl.BlockSpec(memory_space=pltpu.VMEM)


def local_call(kernel, out_shape, args, flops, scratch=()):
    size = sum(a.size * 2 for a in args)
    return pl.pallas_call(
        kernel,
        out_shape=out_shape,
        in_specs=[VMEM] * len(args),
        out_specs=jax.tree.map(lambda _: VMEM, out_shape),
        scratch_shapes=list(scratch),
        cost_estimate=pl.CostEstimate(flops=flops, bytes_accessed=size, transcendentals=0),
        compiler_params=pltpu.CompilerParams(vmem_limit_bytes=56 * 2**20),
    )(*args)


def per_device(latent, cp, co, rp, ro, fp, fo, we, wc):
    _, rows, columns, width = latent.shape
    owners = lax.axis_size("frame")
    share = rows * columns // owners
    stream = local_call(
        column_row_kernel,
        jax.ShapeDtypeStruct((rows, columns, width), BF),
        (latent[0], cp, co, rp, ro),
        2 * rows * columns * width * width * 8,
        [pltpu.VMEM((rows, columns, width), BF)],
    )
    stream = stream.reshape(owners, share, width)
    stream = lax.all_to_all(stream, "frame", split_axis=0, concat_axis=0, tiled=True)
    stream = local_call(
        frame_kernel,
        jax.ShapeDtypeStruct((owners, share, width), BF),
        (stream, fp, fo, we, wc),
        2 * rows * columns * width * width * 12,
    )
    stream = lax.all_to_all(stream, "frame", split_axis=0, concat_axis=0, tiled=True)
    return stream.reshape(latent.shape)


def solution(mesh):
    placed = (P(("parts", "frame"), None, None, None),) + (P(),) * 8
    return jax.shard_map(
        per_device,
        mesh=mesh,
        in_specs=placed,
        out_specs=P(("parts", "frame"), None, None, None),
        check_vma=False,
    )
```

time: 572 us -> 182 us (0.32); the launches traced: 563 us -> 181 us
  local copies, waits for them, and re-layouts: 228 us -> 1.32 us
  other arithmetic: 88.1 us -> 0 us
  matrix products: 85.4 us -> 0 us
  Pallas kernels: 0 us -> 73 us
  waiting for transfers between devices: 44.3 us -> 0 us
  starting transfers between devices: 10.1 us -> 0 us
    mul x18 -> x0, local copies, waits for them, and re-layouts: 103 us -> none  [the longest x12 63.6 us: head_norm(): reshaped_input * lax.rsqrt(jnp.mean(reshaped_input * reshaped_input, axis...]
    dot_general x13 -> x0, matrix products: 85.4 us -> none  [the longest x3 28.9 us: attend_core(): jnp.einsum(logits_form, split_heads(queries), split_heads(key_block), pre...]
    pallas_call x0 -> x2, Pallas kernels: none -> 73 us  [local_call(): pl.pallas_call(kernel, out_shape=out_shape, in_specs=[VMEM] * len(args),...]
    another operation x10 -> x0, local copies, waits for them, and re-layouts: 65 us -> none
    all_to_all x2 -> x0, waiting for transfers between devices: 44.3 us -> none  [the longest x1 43.9 us: per_device(): lax.all_to_all(key_block, 'frame', split_axis=1, concat_axis=0, tiled=True)]
    reduce_sum x12 -> x0, other arithmetic: 37.7 us -> none  [the longest x6 28.3 us: head_norm(): jnp.mean(reshaped_input * reshaped_input, axis=-1, keepdims=True) + EPS_HEAD]
    convert_element_type x6 -> x0, other arithmetic: 35.5 us -> none  [the longest x3 27.9 us: head_norm(): return scaled.reshape(block.shape).astype(jnp.bfloat16)]
    convert_element_type x3 -> x0, local copies, waits for them, and re-layouts: 19.9 us -> none  [the longest x2 12.6 us: attend_core(): blended_values = jnp.einsum(blend_form, attention_weights, split_heads(va...]
  transfers between devices with their start and end apart: 2 -> 0, of which waited for: 2 -> 0; matrix products, arithmetic and copies ran while one was open for 9% -> 0% of each run, Pallas kernels for 0% -> 0%
where the time goes in v1:
time: 182 us; the launch traced here: 181 us
  blocking collectives  106 us (58%)
  Pallas kernels  73 us (40%)
    all_to_all x2, blocking collectives, per_device(): lax.all_to_all(stream, 'frame', split_axis=0, concat_axis=0, tiled=True)  106 us
    pallas_call x2, Pallas kernels, local_call(): pl.pallas_call(kernel, out_shape=out_shape, in_specs=[VMEM] * len(args),...  73 us

profile of v1, /device:TPU:18, one launch (start us, length us, event | category | flops | bytes accessed | tf_op | source)
XLA Modules:
  0.0 180.7 jit_solution(5265030785181329983)
XLA Ops:
  0.0 32.3 %shard_map.91 = bf16[32,64,512]{2,1,0:T(8,128)(2,1)} custom-call(bf16[32,64,512]{2,1,0:T(8,128)(2,1)} %bitcast.5, bf16[512,1536]{1,0:T(8,128)(2,1)} %cp_ref.1, bf16[512,512]{1,0:T(8,128)(2,1)} %co_ref.1, bf16[512,1536]{1,0:T(8,128)(2,1)} %rp_ref.1, bf16[512,512]{1,0:T(8,128)(2,1)} %ro_ref.1), custom_call_target="tpu_custom_call" | custom-call | flops 8589934592 | bytes 6291456 | tf_op jit(solution)/shard_map/pallas_call | solution.py:163
  32.3 53.9 %all_to_all.10.x_ref = bf16[16,128,512]{2,1,0:T(8,128)(2,1)} all-to-all(bf16[16,128,512]{2,1,0:T(8,128)(2,1)} %bitcast.4), channel_id=1, replica_groups=mesh['parts'=2,'frame'=16] {'frame'}, dimensions={0} | all-to-all | bytes 4194304 | tf_op jit(solution)/shard_map/all_to_all | solution.py:186
  86.2 40.7 %shard_map.92 = bf16[16,128,512]{2,1,0:T(8,128)(2,1)} custom-call(bf16[16,128,512]{2,1,0:T(8,128)(2,1)} %all_to_all.10.x_ref, bf16[512,1536]{1,0:T(8,128)(2,1)} %fp_ref.1, bf16[512,512]{1,0:T(8,128)(2,1)} %fo_ref.1, bf16[512,2048]{1,0:T(8,128)(2,1)} %we_ref.1, bf16[2048,512]{1,0:T(8,128)(2,1)} %wc_ref.1), custom_call_target="tpu_custom_call" | custom-call | flops 12884901888 | bytes 8388608 | tf_op jit(solution)/shard_map/pallas_call | solution.py:163
  126.9 52.4 %all_to_all.11 = bf16[16,128,512]{2,1,0:T(8,128)(2,1)S(1)} all-to-all(bf16[16,128,512]{2,1,0:T(8,128)(2,1)} %shard_map.92), channel_id=1, replica_groups=mesh['parts'=2,'frame'=16] {'frame'}, dimensions={0} | all-to-all | bytes 4194304 | tf_op jit(solution)/shard_map/all_to_all | solution.py:193
  179.4 1.3 copy.11

commit v2 on v1

--- a/solution.py
+++ b/solution.py
@@ -1,4 +1,5 @@
 import functools
+import math
 
 import jax
 import jax.numpy as jnp
@@ -122,28 +123,41 @@
     return total.astype(BF)
 
 
-def column_row_kernel(x_ref, cp_ref, co_ref, rp_ref, ro_ref, out_ref, mid_ref):
-    rows, columns, width = x_ref.shape
+def columns_of(x_ref, project_ref, output_ref, mid_ref):
+    rows, columns, _ = x_ref.shape
     swap = swap_matrix()
 
     @pl.loop(0, columns // SIDE)
     def _(g):
         at = pl.ds(pl.multiple_of(g * SIDE, SIDE), SIDE)
         x = to_lines(x_ref[:, at, :], swap)
-        y = sublayer(x, cp_ref, co_ref, rows)
+        y = sublayer(x, project_ref, output_ref, rows)
         mid_ref[:, at, :] = from_lines(y, swap, rows)
 
-    step = 512 // columns
+
+def rows_of(mid_ref, first, project_ref, output_ref, out_ref):
+    rows, columns, width = out_ref.shape
+    step = math.gcd(rows, 512 // columns)
 
     @pl.loop(0, rows // step)
     def _(g):
-        at = pl.ds(g * step, step)
-        x = mid_ref[at].reshape(step * columns, width)
-        out_ref[at] = sublayer(x, rp_ref, ro_ref, columns).reshape(step, columns, width)
-
-
-def frame_kernel(x_ref, fp_ref, fo_ref, we_ref, wc_ref, out_ref):
-    frames, pixels, width = x_ref.shape
+        x = mid_ref[pl.ds(first + g * step, step)].reshape(step * columns, width)
+        y = sublayer(x, project_ref, output_ref, columns)
+        out_ref[pl.ds(g * step, step)] = y.reshape(step, columns, width)
+
+
+def column_row_kernel(x_ref, cp_ref, co_ref, rp_ref, ro_ref, mid_ref, out_ref):
+    columns_of(x_ref, cp_ref, co_ref, mid_ref)
+    rows_of(mid_ref, 0, rp_ref, ro_ref, out_ref)
+
+
+def row_kernel(first, mid_ref, rp_ref, ro_ref, out_ref):
+    rows_of(mid_ref, first, rp_ref, ro_ref, out_ref)
+
+
+def frame_kernel(x_ref, fp_ref, fo_ref, we_ref, wc_ref, *rest):
+    out_ref = rest[-1]
+    frames, pixels, _ = x_ref.shape
     swap = swap_matrix()
 
     @pl.loop(0, pixels // SIDE)
@@ -158,40 +172,64 @@
 VMEM = pl.BlockSpec(memory_space=pltpu.VMEM)
 
 
-def local_call(kernel, out_shape, args, flops, scratch=()):
+def local_call(kernel, out_shape, args, flops, scratch=(), after=()):
     size = sum(a.size * 2 for a in args)
     return pl.pallas_call(
         kernel,
         out_shape=out_shape,
-        in_specs=[VMEM] * len(args),
+        in_specs=[VMEM] * len(args) + [pl.BlockSpec(memory_space=pl.ANY)] * len(after),
         out_specs=jax.tree.map(lambda _: VMEM, out_shape),
         scratch_shapes=list(scratch),
         cost_estimate=pl.CostEstimate(flops=flops, bytes_accessed=size, transcendentals=0),
         compiler_params=pltpu.CompilerParams(vmem_limit_bytes=56 * 2**20),
-    )(*args)
+    )(*args, *after)
+
+
+def like(*shape):
+    return jax.ShapeDtypeStruct(shape, BF)
+
+
+CHUNKS = 2
+
+
+def exchange(blocks):
+    return lax.all_to_all(blocks, "frame", split_axis=0, concat_axis=0, tiled=True)
 
 
 def per_device(latent, cp, co, rp, ro, fp, fo, we, wc):
     _, rows, columns, width = latent.shape
     owners = lax.axis_size("frame")
-    share = rows * columns // owners
-    stream = local_call(
+    height = rows // CHUNKS
+    share = height * columns // owners
+    unit = 2 * columns * width * width
+    mid, first = local_call(
         column_row_kernel,
-        jax.ShapeDtypeStruct((rows, columns, width), BF),
+        (like(rows, columns, width), like(height, columns, width)),
         (latent[0], cp, co, rp, ro),
-        2 * rows * columns * width * width * 8,
-        [pltpu.VMEM((rows, columns, width), BF)],
+        unit * 4 * (rows + height),
     )
-    stream = stream.reshape(owners, share, width)
-    stream = lax.all_to_all(stream, "frame", split_axis=0, concat_axis=0, tiled=True)
-    stream = local_call(
-        frame_kernel,
-        jax.ShapeDtypeStruct((owners, share, width), BF),
-        (stream, fp, fo, we, wc),
-        2 * rows * columns * width * width * 12,
-    )
-    stream = lax.all_to_all(stream, "frame", split_axis=0, concat_axis=0, tiled=True)
-    return stream.reshape(latent.shape)
+    chunks = [first] + [
+        local_call(
+            functools.partial(row_kernel, i * height),
+            like(height, columns, width),
+            (mid, rp, ro),
+            unit * 4 * height,
+        )
+        for i in range(1, CHUNKS)
+    ]
+    owned = [exchange(chunk.reshape(owners, share, width)) for chunk in chunks]
+    done = [
+        local_call(
+            frame_kernel,
+            like(owners, share, width),
+            (block, fp, fo, we, wc),
+            unit * 12 * height,
+            after=chunks[-1:] if i < CHUNKS - 1 else (),
+        )
+        for i, block in enumerate(owned)
+    ]
+    home = [exchange(block).reshape(height, columns, width) for block in done]
+    return jnp.concatenate(home, axis=0)[None]
 
 
 def solution(mesh):

time: 182 us -> 149 us (0.82)
  blocking collectives: 106 us -> 29.8 us
  waiting for transfers between devices: 0 us -> 21.5 us
  starting transfers between devices: 0 us -> 15.5 us
  Pallas kernels: 73 us -> 79.5 us
    all_to_all x2 -> x1, blocking collectives: 106 us -> 29.8 us  [exchange(): lax.all_to_all(blocks, 'frame', split_axis=0, concat_axis=0, tiled=True)]
    all_to_all x0 -> x3, waiting for transfers between devices: none -> 21.5 us  [exchange(): lax.all_to_all(blocks, 'frame', split_axis=0, concat_axis=0, tiled=True)]
    all_to_all x0 -> x3, starting transfers between devices: none -> 15.5 us  [exchange(): lax.all_to_all(blocks, 'frame', split_axis=0, concat_axis=0, tiled=True)]
    pallas_call x2 -> x4, Pallas kernels: 73 us -> 79.5 us  [local_call(): pl.pallas_call(kernel, out_shape=out_shape, in_specs=[VMEM] * len(args) +...]
  transfers between devices with their start and end apart: 0 -> 3, of which waited for: 0 -> 3; matrix products, arithmetic and copies ran while one was open for 0% -> 0% of each run, Pallas kernels for 0% -> 37%
where the time goes in v2:
time: 149 us; the launch traced here: 148 us
  Pallas kernels  79.5 us (53%)
  blocking collectives  29.8 us (20%)
  waiting for transfers between devices  21.5 us (14%)
  starting transfers between devices  15.5 us (10%)
  other arithmetic  1.5 us (1%)
    pallas_call x4, Pallas kernels, local_call(): pl.pallas_call(kernel, out_shape=out_shape, in_specs=[VMEM] * len(args) +...  79.5 us
    all_to_all x1, blocking collectives, exchange(): lax.all_to_all(blocks, 'frame', split_axis=0, concat_axis=0, tiled=True)  29.8 us
    all_to_all x3, waiting for transfers between devices, exchange(): lax.all_to_all(blocks, 'frame', split_axis=0, concat_axis=0, tiled=True)  21.5 us
    all_to_all x3, starting transfers between devices, exchange(): lax.all_to_all(blocks, 'frame', split_axis=0, concat_axis=0, tiled=True)  15.5 us
  transfers between devices with their start and end apart: 3, of which 3 were waited for; matrix products, arithmetic and copies ran while one was open for 0% of the time, Pallas kernels for 37%

profile of v2, /device:TPU:18, one launch (start us, length us, event | category | flops | bytes accessed | tf_op | source)
XLA Modules:
  0.0 147.7 jit_solution(17123334001411079763)
XLA Ops:
  0.0 25.4 %shard_map.91 = (bf16[32,64,512]{2,1,0:T(8,128)(2,1)}, bf16[16,64,512]{2,1,0:T(8,128)(2,1)}) custom-call(bf16[32,64,512]{2,1,0:T(8,128)(2,1)} %bitcast.3, bf16[512,1536]{1,0:T(8,128)(2,1)} %cp_ref.1, bf16[512,512]{1,0:T(8,128)(2,1)} %co_ref.1, bf16[512,1536]{1,0:T(8,128)(2,1)} %rp_ref.3, bf16[512,512]{1,0:T(8,128)(2,1)} %ro_ref.3), custom_call_target="tpu_custom_call" | custom-call | flops 6442450944 | bytes 6291456 | tf_op jit(solution)/shard_map/pallas_call | solution.py:177
  25.4 6.2 %all-to-all-start = ((bf16[16,64,512]{2,1,0:T(8,128)(2,1)}), bf16[16,64,512]{2,1,0:T(8,128)(2,1)S(1)}, u32[]{:S(2)}, u32[]{:S(2)}) async-start(bf16[16,64,512]{2,1,0:T(8,128)(2,1)} %get-tuple-element.7), calls=%async_computation | async-start | bytes 2097152 | tf_op jit(solution)/shard_map/all_to_all | solution.py:196
  31.6 9.7 %shard_map.92.rest_0_ = bf16[16,64,512]{2,1,0:T(8,128)(2,1)} custom-call(bf16[32,64,512]{2,1,0:T(8,128)(2,1)} %get-tuple-element.8.mid_ref, bf16[512,1536]{1,0:T(8,128)(2,1)} %rp_ref.3, bf16[512,512]{1,0:T(8,128)(2,1)} %ro_ref.3), custom_call_target="tpu_custom_call" | custom-call | flops 2147483648 | bytes 4194304 | tf_op jit(solution)/shard_map/pallas_call | solution.py:177
  41.3 15.5 %all-to-all-done.x_ref = bf16[16,64,512]{2,1,0:T(8,128)(2,1)S(1)} async-done(((bf16[16,64,512]{2,1,0:T(8,128)(2,1)}), bf16[16,64,512]{2,1,0:T(8,128)(2,1)S(1)}, u32[]{:S(2)}, u32[]{:S(2)}) %all-to-all-start) | async-done | bytes 1048608 | tf_op jit(solution)/shard_map/all_to_all | solution.py:196
  56.8 0.0 copy-start
  56.8 4.6 %all-to-all-start.2 = ((bf16[16,64,512]{2,1,0:T(8,128)(2,1)}), bf16[16,64,512]{2,1,0:T(8,128)(2,1)S(1)}, u32[]{:S(2)}, u32[]{:S(2)}) async-start(bf16[16,64,512]{2,1,0:T(8,128)(2,1)} %shard_map.92.rest_0_), calls=%async_computation.2 | async-start | bytes 2097152 | tf_op jit(solution)/shard_map/all_to_all | solution.py:196
  61.4 0.0 copy-done
  61.5 22.2 %shard_map.93 = bf16[16,64,512]{2,1,0:T(8,128)(2,1)} custom-call(bf16[16,64,512]{2,1,0:T(8,128)(2,1)} %copy-done, bf16[512,1536]{1,0:T(8,128)(2,1)} %fp_ref.3, bf16[512,512]{1,0:T(8,128)(2,1)} %fo_ref.3, bf16[512,2048]{1,0:T(8,128)(2,1)} %we_ref.3, bf16[2048,512]{1,0:T(8,128)(2,1)} %wc_ref.3, bf16[16,64,512]{2,1,0:T(8,128)(2,1)} %shard_map.92.rest_0_), custom_call_target="tpu_custom_call" | custom-call | flops 6442450944 | bytes 7340032 | tf_op jit(solution)/shard_map/pallas_call | solution.py:177
  83.7 3.0 %all-to-all-done.2.x_ref = bf16[16,64,512]{2,1,0:T(8,128)(2,1)S(1)} async-done(((bf16[16,64,512]{2,1,0:T(8,128)(2,1)}), bf16[16,64,512]{2,1,0:T(8,128)(2,1)S(1)}, u32[]{:S(2)}, u32[]{:S(2)}) %all-to-all-start.2) | async-done | bytes 1048608 | tf_op jit(solution)/shard_map/all_to_all | solution.py:196
  86.6 0.0 copy-start.1
  86.6 4.6 %all-to-all-start.1 = ((bf16[16,64,512]{2,1,0:T(8,128)(2,1)}), bf16[16,64,512]{2,1,0:T(8,128)(2,1)S(1)}, u32[]{:S(2)}, u32[]{:S(2)}) async-start(bf16[16,64,512]{2,1,0:T(8,128)(2,1)} %shard_map.93), calls=%async_computation.1 | async-start | bytes 2097152 | tf_op jit(solution)/shard_map/all_to_all | solution.py:196
  91.3 0.0 copy-done.1
  91.3 22.2 %shard_map.94 = bf16[16,64,512]{2,1,0:T(8,128)(2,1)} custom-call(bf16[16,64,512]{2,1,0:T(8,128)(2,1)} %copy-done.1, bf16[512,1536]{1,0:T(8,128)(2,1)} %fp_ref.3, bf16[512,512]{1,0:T(8,128)(2,1)} %fo_ref.3, bf16[512,2048]{1,0:T(8,128)(2,1)} %we_ref.3, bf16[2048,512]{1,0:T(8,128)(2,1)} %wc_ref.3), custom_call_target="tpu_custom_call" | custom-call | flops 6442450944 | bytes 7340032 | tf_op jit(solution)/shard_map/pallas_call | solution.py:177
  113.4 3.0 %all-to-all-done.1 = bf16[16,64,512]{2,1,0:T(8,128)(2,1)S(1)} async-done(((bf16[16,64,512]{2,1,0:T(8,128)(2,1)}), bf16[16,64,512]{2,1,0:T(8,128)(2,1)S(1)}, u32[]{:S(2)}, u32[]{:S(2)}) %all-to-all-start.1) | async-done | bytes 1048608 | tf_op jit(solution)/shard_map/all_to_all | solution.py:196
  116.4 29.8 %all_to_all.20 = bf16[16,64,512]{2,1,0:T(8,128)(2,1)S(1)} all-to-all(bf16[16,64,512]{2,1,0:T(8,128)(2,1)} %shard_map.94), channel_id=1, replica_groups=mesh['parts'=2,'frame'=16] {'frame'}, dimensions={0} | all-to-all | bytes 2097152 | tf_op jit(solution)/shard_map/all_to_all | solution.py:196
  146.2 1.5 %maximum_bitcast_fusion = bf16[1,32,64,512]{3,2,1,0:T(8,128)(2,1)} fusion(bf16[16,64,512]{2,1,0:T(8,128)(2,1)S(1)} %all_to_all.20, bf16[16,64,512]{2,1,0:T(8,128)(2,1)S(1)} %all-to-all-done.1), kind=kLoop, calls=%fused_computation | loop fusion | flops 1048576 | bytes 4194304 | tf_op jit(solution)/shard_map/broadcast_in_dim | solution.py:232
Async XLA Ops:
  25.4 31.4 %all-to-all-start = ((bf16[16,64,512]{2,1,0:T(8,128)(2,1)}), bf16[16,64,512]{2,1,0:T(8,128)(2,1)S(1)}, u32[]{:S(2)}, u32[]{:S(2)}) async-start(bf16[16,64,512]{2,1,0:T(8,128)(2,1)} %get-tuple-element.7), calls=%async_computation | async-start | bytes 2097152 | tf_op jit(solution)/shard_map/all_to_all | solution.py:196
  56.8 4.6 %copy-start = (bf16[16,64,512]{2,1,0:T(8,128)(2,1)}, bf16[16,64,512]{2,1,0:T(8,128)(2,1)S(1)}, u32[]{:S(2)}) copy-start(bf16[16,64,512]{2,1,0:T(8,128)(2,1)S(1)} %all-to-all-done.x_ref) | copy-start | bytes 3145732
  56.8 29.8 %all-to-all-start.2 = ((bf16[16,64,512]{2,1,0:T(8,128)(2,1)}), bf16[16,64,512]{2,1,0:T(8,128)(2,1)S(1)}, u32[]{:S(2)}, u32[]{:S(2)}) async-start(bf16[16,64,512]{2,1,0:T(8,128)(2,1)} %shard_map.92.rest_0_), calls=%async_computation.2 | async-start | bytes 2097152 | tf_op jit(solution)/shard_map/all_to_all | solution.py:196
  86.6 4.6 %copy-start.1 = (bf16[16,64,512]{2,1,0:T(8,128)(2,1)}, bf16[16,64,512]{2,1,0:T(8,128)(2,1)S(1)}, u32[]{:S(2)}) copy-start(bf16[16,64,512]{2,1,0:T(8,128)(2,1)S(1)} %all-to-all-done.2.x_ref) | copy-start | bytes 3145732
  86.6 29.8 %all-to-all-start.1 = ((bf16[16,64,512]{2,1,0:T(8,128)(2,1)}), bf16[16,64,512]{2,1,0:T(8,128)(2,1)S(1)}, u32[]{:S(2)}, u32[]{:S(2)}) async-start(bf16[16,64,512]{2,1,0:T(8,128)(2,1)} %shard_map.93), calls=%async_computation.1 | async-start | bytes 2097152 | tf_op jit(solution)/shard_map/all_to_all | solution.py:196

commit v3 on v2

v3 whole, which is shorter than its diff:
```python
import functools
import math

import jax
import jax.numpy as jnp
from jax import lax
from jax.experimental import pallas as pl
from jax.experimental.pallas import tpu as pltpu
from jax.sharding import PartitionSpec as P

HEADS = 8
EPS_NORM = 1e-05
EPS_HEAD = 1e-06
BF = jnp.bfloat16
F32 = jnp.float32
SIDE = 16
SPAN = 128
FIRST = 2


def dot(a, b):
    return jnp.dot(a, b, preferred_element_type=F32)


def dot_nt(a, b):
    return lax.dot_general(a, b, (((1,), (1,)), ((), ())), preferred_element_type=F32)


def iota(shape, dim):
    return lax.broadcasted_iota(jnp.int32, shape, dim)


def swap_matrix():
    n = SIDE * SIDE
    r, c = iota((n, n), 0), iota((n, n), 1)
    hit = (r // SIDE == c % SIDE) & (r % SIDE == c // SIDE)
    return jnp.where(hit, 1.0, 0.0).astype(BF)


def head_blocks(head, value):
    n = 4 * head
    same = iota((n, n), 0) // head == iota((n, n), 1) // head
    return jnp.where(same, value, 0.0).astype(BF)


def layer_normalize(x):
    v = x.astype(F32)
    centre = v - jnp.mean(v, axis=-1, keepdims=True)
    spread = jnp.mean(centre * centre, axis=-1, keepdims=True)
    return (centre * lax.rsqrt(spread + EPS_NORM)).astype(BF)


def head_norm(block, averager, scale):
    half = averager.shape[0]
    squares = (block * block).astype(BF)
    out = []
    for c in range(0, block.shape[1], half):
        mean = dot(squares[:, c : c + half], averager)
        out.append((block[:, c : c + half] * (lax.rsqrt(mean + EPS_HEAD) * scale)).astype(BF))
    return out


def sublayer(x, project_ref, output_ref, line):
    tokens, width = x.shape
    head = width // HEADS
    half = 4 * head
    averager = head_blocks(head, 1.0 / head)
    normed = layer_normalize(x)
    queries = head_norm(dot(normed, project_ref[:, :width]), averager, head**-0.5)
    keys = head_norm(dot(normed, project_ref[:, width : 2 * width]), averager, 1.0)
    values = dot(normed, project_ref[:, 2 * width :]).astype(BF)
    span = SPAN
    pair = 2 * head
    own = iota((span, 2 * span), 0) // line == (iota((span, 2 * span), 1) % span) // line
    first = iota((span, pair), 1) < head
    ones = jnp.where((iota((2 * span, pair), 0) < span) == (iota((2 * span, pair), 1) < head), 1.0, 0.0).astype(BF)

    def spread(block):
        zero = jnp.zeros_like(block)
        return jnp.concatenate([jnp.where(first, block, zero), jnp.where(first, zero, block)], axis=0)

    rows = []
    for s in range(0, tokens, span):
        parts = []
        for h in range(0, width, pair):
            c, o = h // half, h % half
            q = queries[c][s : s + span, o : o + pair]
            k = spread(keys[c][s : s + span, o : o + pair])
            v = spread(values[s : s + span, h : h + pair])
            e = jnp.where(own, jnp.exp(dot_nt(q, k)), 0.0).astype(BF)
            r = dot(e, jnp.concatenate([v, ones], axis=1))
            parts.append((r[:, :pair] / r[:, pair:]).astype(BF))
        rows.append(jnp.concatenate(parts, axis=1))
    mixed = jnp.concatenate(rows, axis=0)
    return (x.astype(F32) + dot(mixed, output_ref[...])).astype(BF)


def to_lines(x, swap):
    length, side, width = x.shape
    parts = []
    for a in range(0, length, SIDE):
        tile = x[a : a + SIDE].reshape(SIDE * side, width)
        parts.append(dot(swap, tile).astype(BF).reshape(side, SIDE, width))
    return jnp.concatenate(parts, axis=1).reshape(side * length, width)


def from_lines(x, swap, length):
    width = x.shape[1]
    x = x.reshape(SIDE, length, width)
    parts = []
    for a in range(0, length, SIDE):
        tile = x[:, a : a + SIDE].reshape(SIDE * SIDE, width)
        parts.append(dot(swap, tile).astype(BF).reshape(SIDE, SIDE, width))
    return jnp.concatenate(parts, axis=0)


def feed_forward(x, expand_ref, contract_ref):
    hidden = expand_ref.shape[1]
    piece = 256
    normed = layer_normalize(x)
    total = x.astype(F32)
    for c in range(0, hidden, piece):
        h = jax.nn.gelu(dot(normed, expand_ref[:, c : c + piece])).astype(BF)
        total = total + dot(h, contract_ref[c : c + piece])
    return total.astype(BF)


def like(*shape):
    return jax.ShapeDtypeStruct(shape, BF)


VMEM = pl.BlockSpec(memory_space=pltpu.VMEM)
ANY = pl.BlockSpec(memory_space=pl.ANY)


def local_call(kernel, out_shape, args, specs, flops, scratch=()):
    size = sum(a.size * 2 for a in args)
    return pl.pallas_call(
        kernel,
        out_shape=out_shape,
        in_specs=specs,
        out_specs=jax.tree.map(lambda _: VMEM, out_shape),
        scratch_shapes=list(scratch),
        cost_estimate=pl.CostEstimate(flops=flops, bytes_accessed=size, transcendentals=0),
        compiler_params=pltpu.CompilerParams(vmem_limit_bytes=56 * 2**20),
    )(*args)


def rows_of(mid_ref, first, project_ref, output_ref, out_ref):
    rows, columns, width = out_ref.shape
    step = math.gcd(rows, 512 // columns)

    @pl.loop(0, rows // step)
    def _(g):
        x = mid_ref[pl.ds(first + g * step, step)].reshape(step * columns, width)
        y = sublayer(x, project_ref, output_ref, columns)
        out_ref[pl.ds(g * step, step)] = y.reshape(step, columns, width)


def column_row_kernel(x_ref, cp_ref, co_ref, rp_ref, ro_ref, mid_ref, out_ref):
    rows, columns, _ = x_ref.shape
    swap = swap_matrix()

    @pl.loop(0, columns // SIDE)
    def _(g):
        at = pl.ds(pl.multiple_of(g * SIDE, SIDE), SIDE)
        x = to_lines(x_ref[:, at, :], swap)
        y = sublayer(x, cp_ref, co_ref, rows)
        mid_ref[:, at, :] = from_lines(y, swap, rows)

    rows_of(mid_ref, 0, rp_ref, ro_ref, out_ref)


def row_kernel(first, mid_ref, rp_ref, ro_ref, out_ref):
    rows_of(mid_ref, first, rp_ref, ro_ref, out_ref)


def frame_kernel(x_ref, fp_ref, fo_ref, we_ref, wc_ref, *rest):
    out_ref = rest[-1]
    frames, pixels, _ = x_ref.shape
    swap = swap_matrix()
    size = frames * SIDE
    tiles = math.gcd(pixels // SIDE, max(1, 512 // size))

    @pl.loop(0, pixels // (tiles * SIDE))
    def _(t):
        at = [pl.ds(pl.multiple_of((t * tiles + i) * SIDE, SIDE), SIDE) for i in range(tiles)]
        x = jnp.concatenate([to_lines(x_ref[:, a, :], swap) for a in at], axis=0)
        y = sublayer(x, fp_ref, fo_ref, frames)
        y = feed_forward(y, we_ref, wc_ref)
        for i, a in enumerate(at):
            out_ref[:, a, :] = from_lines(y[i * size : (i + 1) * size], swap, frames)


def exchange(blocks):
    return lax.all_to_all(blocks, "frame", split_axis=0, concat_axis=0, tiled=True)


def per_device(latent, cp, co, rp, ro, fp, fo, we, wc):
    _, rows, columns, width = latent.shape
    owners = lax.axis_size("frame")
    unit = 2 * columns * width * width
    one = rows // FIRST
    two = rows - one
    mid, chunk_one = local_call(
        column_row_kernel,
        (like(rows, columns, width), like(one, columns, width)),
        (latent[0], cp, co, rp, ro),
        [VMEM] * 5,
        unit * 4 * (rows + one),
    )
    chunk_two = local_call(
        functools.partial(row_kernel, one),
        like(two, columns, width),
        (mid, rp, ro),
        [VMEM] * 3,
        unit * 4 * two,
    )
    home = []
    for chunk, after in ((chunk_one, (chunk_two,)), (chunk_two, ())):
        height = chunk.shape[0]
        share = height * columns // owners
        owned = exchange(chunk.reshape(owners, share, width))
        done = local_call(
            frame_kernel,
            like(owners, share, width),
            (owned, fp, fo, we, wc, *after),
            [VMEM] * 5 + [ANY] * len(after),
            unit * 12 * height,
        )
        home.append(exchange(done).reshape(height, columns, width))
    return jnp.concatenate(home, axis=0)[None]


def solution(mesh):
    placed = (P(("parts", "frame"), None, None, None),) + (P(),) * 8
    return jax.shard_map(
        per_device,
        mesh=mesh,
        in_specs=placed,
        out_specs=P(("parts", "frame"), None, None, None),
        check_vma=False,
    )
```

time: 149 us -> 145 us (0.973)
  Pallas kernels: 79.5 us -> 60.6 us
  waiting for transfers between devices: 21.5 us -> 35.9 us
    pallas_call x4, Pallas kernels: 79.5 us -> 60.6 us  [local_call(): pl.pallas_call(kernel, out_shape=out_shape, in_specs=specs, out_specs=jax...]
    all_to_all x3, waiting for transfers between devices: 21.5 us -> 35.9 us  [exchange(): lax.all_to_all(blocks, 'frame', split_axis=0, concat_axis=0, tiled=True)]
  transfers between devices with their start and end apart: 3 -> 3, of which waited for: 3 -> 3; matrix products, arithmetic and copies ran while one was open for 0% -> 0% of each run, Pallas kernels for 37% -> 28%
where the time goes in v3:
time: 145 us; the launch traced here: 143 us
  Pallas kernels  60.6 us (42%)
  waiting for transfers between devices  35.9 us (25%)
  blocking collectives  29.8 us (21%)
  starting transfers between devices  15.5 us (11%)
  other arithmetic  1.5 us (1%)
    pallas_call x4, Pallas kernels, local_call(): pl.pallas_call(kernel, out_shape=out_shape, in_specs=specs, out_specs=jax...  60.6 us
    all_to_all x3, waiting for transfers between devices, exchange(): lax.all_to_all(blocks, 'frame', split_axis=0, concat_axis=0, tiled=True)  35.9 us
    all_to_all x1, blocking collectives, exchange(): lax.all_to_all(blocks, 'frame', split_axis=0, concat_axis=0, tiled=True)  29.8 us
    all_to_all x3, starting transfers between devices, exchange(): lax.all_to_all(blocks, 'frame', split_axis=0, concat_axis=0, tiled=True)  15.5 us
  transfers between devices with their start and end apart: 3, of which 3 were waited for; matrix products, arithmetic and copies ran while one was open for 0% of the time, Pallas kernels for 28%

profile of v3, /device:TPU:18, one launch (start us, length us, event | category | flops | bytes accessed | tf_op | source)
XLA Modules:
  0.0 143.2 jit_solution(14211844176700341486)
XLA Ops:
  0.0 20.9 %shard_map.91 = (bf16[32,64,512]{2,1,0:T(8,128)(2,1)}, bf16[16,64,512]{2,1,0:T(8,128)(2,1)}) custom-call(bf16[32,64,512]{2,1,0:T(8,128)(2,1)} %bitcast.3, bf16[512,1536]{1,0:T(8,128)(2,1)} %cp_ref.1, bf16[512,512]{1,0:T(8,128)(2,1)} %co_ref.1, bf16[512,1536]{1,0:T(8,128)(2,1)} %rp_ref.3, bf16[512,512]{1,0:T(8,128)(2,1)} %ro_ref.3), custom_call_target="tpu_custom_call" | custom-call | flops 6442450944 | bytes 6291456 | tf_op jit(solution)/shard_map/pallas_call | solution.py:138
  20.9 6.2 %all-to-all-start = ((bf16[16,64,512]{2,1,0:T(8,128)(2,1)}), bf16[16,64,512]{2,1,0:T(8,128)(2,1)S(1)}, u32[]{:S(2)}, u32[]{:S(2)}) async-start(bf16[16,64,512]{2,1,0:T(8,128)(2,1)} %get-tuple-element.7), calls=%async_computation | async-start | bytes 2097152 | tf_op jit(solution)/shard_map/all_to_all | solution.py:196
  27.1 8.2 %shard_map.92.rest_0_ = bf16[16,64,512]{2,1,0:T(8,128)(2,1)} custom-call(bf16[32,64,512]{2,1,0:T(8,128)(2,1)} %get-tuple-element.8.mid_ref, bf16[512,1536]{1,0:T(8,128)(2,1)} %rp_ref.3, bf16[512,512]{1,0:T(8,128)(2,1)} %ro_ref.3), custom_call_target="tpu_custom_call" | custom-call | flops 2147483648 | bytes 4194304 | tf_op jit(solution)/shard_map/pallas_call | solution.py:138
  35.3 17.0 %all-to-all-done.x_ref = bf16[16,64,512]{2,1,0:T(8,128)(2,1)S(1)} async-done(((bf16[16,64,512]{2,1,0:T(8,128)(2,1)}), bf16[16,64,512]{2,1,0:T(8,128)(2,1)S(1)}, u32[]{:S(2)}, u32[]{:S(2)}) %all-to-all-start) | async-done | bytes 1048608 | tf_op jit(solution)/shard_map/all_to_all | solution.py:196
  52.3 0.0 copy-start
  52.3 4.6 %all-to-all-start.2 = ((bf16[16,64,512]{2,1,0:T(8,128)(2,1)}), bf16[16,64,512]{2,1,0:T(8,128)(2,1)S(1)}, u32[]{:S(2)}, u32[]{:S(2)}) async-start(bf16[16,64,512]{2,1,0:T(8,128)(2,1)} %shard_map.92.rest_0_), calls=%async_computation.2 | async-start | bytes 2097152 | tf_op jit(solution)/shard_map/all_to_all | solution.py:196
  56.9 0.0 copy-done
  56.9 15.8 %shard_map.93 = bf16[16,64,512]{2,1,0:T(8,128)(2,1)} custom-call(bf16[16,64,512]{2,1,0:T(8,128)(2,1)} %copy-done, bf16[512,1536]{1,0:T(8,128)(2,1)} %fp_ref.3, bf16[512,512]{1,0:T(8,128)(2,1)} %fo_ref.3, bf16[512,2048]{1,0:T(8,128)(2,1)} %we_ref.3, bf16[2048,512]{1,0:T(8,128)(2,1)} %wc_ref.3, bf16[16,64,512]{2,1,0:T(8,128)(2,1)} %shard_map.92.rest_0_), custom_call_target="tpu_custom_call" | custom-call | flops 6442450944 | bytes 8388608 | tf_op jit(solution)/shard_map/pallas_call | solution.py:138
  72.7 9.4 %all-to-all-done.2.x_ref = bf16[16,64,512]{2,1,0:T(8,128)(2,1)S(1)} async-done(((bf16[16,64,512]{2,1,0:T(8,128)(2,1)}), bf16[16,64,512]{2,1,0:T(8,128)(2,1)S(1)}, u32[]{:S(2)}, u32[]{:S(2)}) %all-to-all-start.2) | async-done | bytes 1048608 | tf_op jit(solution)/shard_map/all_to_all | solution.py:196
  82.1 0.0 copy-start.1
  82.1 4.6 %all-to-all-start.1 = ((bf16[16,64,512]{2,1,0:T(8,128)(2,1)}), bf16[16,64,512]{2,1,0:T(8,128)(2,1)S(1)}, u32[]{:S(2)}, u32[]{:S(2)}) async-start(bf16[16,64,512]{2,1,0:T(8,128)(2,1)} %shard_map.93), calls=%async_computation.1 | async-start | bytes 2097152 | tf_op jit(solution)/shard_map/all_to_all | solution.py:196
  86.8 0.0 copy-done.1
  86.8 15.7 %shard_map.94 = bf16[16,64,512]{2,1,0:T(8,128)(2,1)} custom-call(bf16[16,64,512]{2,1,0:T(8,128)(2,1)} %copy-done.1, bf16[512,1536]{1,0:T(8,128)(2,1)} %fp_ref.3, bf16[512,512]{1,0:T(8,128)(2,1)} %fo_ref.3, bf16[512,2048]{1,0:T(8,128)(2,1)} %we_ref.3, bf16[2048,512]{1,0:T(8,128)(2,1)} %wc_ref.3), custom_call_target="tpu_custom_call" | custom-call | flops 6442450944 | bytes 7340032 | tf_op jit(solution)/shard_map/pallas_call | solution.py:138
  102.5 9.5 %all-to-all-done.1 = bf16[16,64,512]{2,1,0:T(8,128)(2,1)S(1)} async-done(((bf16[16,64,512]{2,1,0:T(8,128)(2,1)}), bf16[16,64,512]{2,1,0:T(8,128)(2,1)S(1)}, u32[]{:S(2)}, u32[]{:S(2)}) %all-to-all-start.1) | async-done | bytes 1048608 | tf_op jit(solution)/shard_map/all_to_all | solution.py:196
  111.9 29.8 %all_to_all.20 = bf16[16,64,512]{2,1,0:T(8,128)(2,1)S(1)} all-to-all(bf16[16,64,512]{2,1,0:T(8,128)(2,1)} %shard_map.94), channel_id=1, replica_groups=mesh['parts'=2,'frame'=16] {'frame'}, dimensions={0} | all-to-all | bytes 2097152 | tf_op jit(solution)/shard_map/all_to_all | solution.py:196
  141.7 1.5 %maximum_bitcast_fusion = bf16[1,32,64,512]{3,2,1,0:T(8,128)(2,1)} fusion(bf16[16,64,512]{2,1,0:T(8,128)(2,1)S(1)} %all_to_all.20, bf16[16,64,512]{2,1,0:T(8,128)(2,1)S(1)} %all-to-all-done.1), kind=kLoop, calls=%fused_computation | loop fusion | flops 1048576 | bytes 4194304 | tf_op jit(solution)/shard_map/broadcast_in_dim | solution.py:232
Async XLA Ops:
  20.9 31.4 %all-to-all-start = ((bf16[16,64,512]{2,1,0:T(8,128)(2,1)}), bf16[16,64,512]{2,1,0:T(8,128)(2,1)S(1)}, u32[]{:S(2)}, u32[]{:S(2)}) async-start(bf16[16,64,512]{2,1,0:T(8,128)(2,1)} %get-tuple-element.7), calls=%async_computation | async-start | bytes 2097152 | tf_op jit(solution)/shard_map/all_to_all | solution.py:196
  52.3 4.6 %copy-start = (bf16[16,64,512]{2,1,0:T(8,128)(2,1)}, bf16[16,64,512]{2,1,0:T(8,128)(2,1)S(1)}, u32[]{:S(2)}) copy-start(bf16[16,64,512]{2,1,0:T(8,128)(2,1)S(1)} %all-to-all-done.x_ref) | copy-start | bytes 3145732
  52.3 29.8 %all-to-all-start.2 = ((bf16[16,64,512]{2,1,0:T(8,128)(2,1)}), bf16[16,64,512]{2,1,0:T(8,128)(2,1)S(1)}, u32[]{:S(2)}, u32[]{:S(2)}) async-start(bf16[16,64,512]{2,1,0:T(8,128)(2,1)} %shard_map.92.rest_0_), calls=%async_computation.2 | async-start | bytes 2097152 | tf_op jit(solution)/shard_map/all_to_all | solution.py:196
  82.1 4.6 %copy-start.1 = (bf16[16,64,512]{2,1,0:T(8,128)(2,1)}, bf16[16,64,512]{2,1,0:T(8,128)(2,1)S(1)}, u32[]{:S(2)}) copy-start(bf16[16,64,512]{2,1,0:T(8,128)(2,1)S(1)} %all-to-all-done.2.x_ref) | copy-start | bytes 3145732
  82.1 29.8 %all-to-all-start.1 = ((bf16[16,64,512]{2,1,0:T(8,128)(2,1)}), bf16[16,64,512]{2,1,0:T(8,128)(2,1)S(1)}, u32[]{:S(2)}, u32[]{:S(2)}) async-start(bf16[16,64,512]{2,1,0:T(8,128)(2,1)} %shard_map.93), calls=%async_computation.1 | async-start | bytes 2097152 | tf_op jit(solution)/shard_map/all_to_all | solution.py:196

commit v4 on v3

--- a/solution.py
+++ b/solution.py
@@ -15,7 +15,7 @@
 F32 = jnp.float32
 SIDE = 16
 SPAN = 128
-FIRST = 2
+CHUNKS = 2
 
 
 def dot(a, b):
@@ -50,41 +50,48 @@
     return (centre * lax.rsqrt(spread + EPS_NORM)).astype(BF)
 
 
-def head_norm(block, averager, scale):
+def head_norm(block, averager, eps):
     half = averager.shape[0]
     squares = (block * block).astype(BF)
     out = []
     for c in range(0, block.shape[1], half):
         mean = dot(squares[:, c : c + half], averager)
-        out.append((block[:, c : c + half] * (lax.rsqrt(mean + EPS_HEAD) * scale)).astype(BF))
+        out.append((block[:, c : c + half] * lax.rsqrt(mean + eps)).astype(BF))
     return out
 
 
-def sublayer(x, project_ref, output_ref, line):
+def sublayer(x, project_ref, output_ref, line, first=0, count=None):
     tokens, width = x.shape
+    count = count or line
     head = width // HEADS
     half = 4 * head
-    averager = head_blocks(head, 1.0 / head)
     normed = layer_normalize(x)
-    queries = head_norm(dot(normed, project_ref[:, :width]), averager, head**-0.5)
-    keys = head_norm(dot(normed, project_ref[:, width : 2 * width]), averager, 1.0)
+
+    def picked(block):
+        if count == line:
+            return block
+        return block.reshape(tokens // line, line, width)[:, first : first + count].reshape(-1, width)
+
+    queries = head_norm(dot(picked(normed), project_ref[:, :width]), head_blocks(head, 1.0), head * EPS_HEAD)
+    keys = head_norm(dot(normed, project_ref[:, width : 2 * width]), head_blocks(head, 1.0 / head), EPS_HEAD)
     values = dot(normed, project_ref[:, 2 * width :]).astype(BF)
     span = SPAN
+    asks = span // line * count
     pair = 2 * head
-    own = iota((span, 2 * span), 0) // line == (iota((span, 2 * span), 1) % span) // line
-    first = iota((span, pair), 1) < head
+    own = iota((asks, 2 * span), 0) // count == (iota((asks, 2 * span), 1) % span) // line
+    left = iota((span, pair), 1) < head
     ones = jnp.where((iota((2 * span, pair), 0) < span) == (iota((2 * span, pair), 1) < head), 1.0, 0.0).astype(BF)
 
     def spread(block):
         zero = jnp.zeros_like(block)
-        return jnp.concatenate([jnp.where(first, block, zero), jnp.where(first, zero, block)], axis=0)
+        return jnp.concatenate([jnp.where(left, block, zero), jnp.where(left, zero, block)], axis=0)
 
     rows = []
-    for s in range(0, tokens, span):
+    for i, s in enumerate(range(0, tokens, span)):
         parts = []
         for h in range(0, width, pair):
             c, o = h // half, h % half
-            q = queries[c][s : s + span, o : o + pair]
+            q = queries[c][i * asks : (i + 1) * asks, o : o + pair]
             k = spread(keys[c][s : s + span, o : o + pair])
             v = spread(values[s : s + span, h : h + pair])
             e = jnp.where(own, jnp.exp(dot_nt(q, k)), 0.0).astype(BF)
@@ -92,7 +99,7 @@
             parts.append((r[:, :pair] / r[:, pair:]).astype(BF))
         rows.append(jnp.concatenate(parts, axis=1))
     mixed = jnp.concatenate(rows, axis=0)
-    return (x.astype(F32) + dot(mixed, output_ref[...])).astype(BF)
+    return (picked(x).astype(F32) + dot(mixed, output_ref[...])).astype(BF)
 
 
 def to_lines(x, swap):
@@ -133,46 +140,71 @@
 ANY = pl.BlockSpec(memory_space=pl.ANY)
 
 
-def local_call(kernel, out_shape, args, specs, flops, scratch=()):
+def local_call(kernel, out_shape, args, specs, flops, scratch=(), out_spec=VMEM):
     size = sum(a.size * 2 for a in args)
     return pl.pallas_call(
         kernel,
         out_shape=out_shape,
         in_specs=specs,
-        out_specs=jax.tree.map(lambda _: VMEM, out_shape),
+        out_specs=jax.tree.map(lambda _: out_spec, out_shape),
         scratch_shapes=list(scratch),
         cost_estimate=pl.CostEstimate(flops=flops, bytes_accessed=size, transcendentals=0),
         compiler_params=pltpu.CompilerParams(vmem_limit_bytes=56 * 2**20),
     )(*args)
 
 
-def rows_of(mid_ref, first, project_ref, output_ref, out_ref):
-    rows, columns, width = out_ref.shape
-    step = math.gcd(rows, 512 // columns)
-
-    @pl.loop(0, rows // step)
+def column_row_kernel(first, x_hbm, cp_hbm, co_hbm, rp_hbm, ro_hbm, out_hbm, *scratch):
+    x_ref, cp_ref, co_ref, rp_ref, ro_ref, mid_ref, out_ref, sems = scratch
+    rows, columns, width = x_hbm.shape
+    groups = columns // SIDE
+    count = out_hbm.shape[0]
+    step = math.gcd(count, 512 // columns)
+
+    def at(g):
+        return pl.ds(pl.multiple_of(g * SIDE, SIDE), SIDE)
+
+    def fetch(g):
+        return pltpu.make_async_copy(x_hbm.at[:, at(g), :], x_ref.at[g], sems.at[g])
+
+    pairs = ((cp_hbm, cp_ref), (co_hbm, co_ref), (rp_hbm, rp_ref), (ro_hbm, ro_ref))
+    weights = [pltpu.make_async_copy(h, v, sems.at[groups + i]) for i, (h, v) in enumerate(pairs)]
+    fetch(0).start()
+    weights[0].start()
+    weights[1].start()
+    for g in range(1, groups):
+        fetch(g).start()
+    weights[2].start()
+    weights[3].start()
+    swap = swap_matrix()
+    weights[0].wait()
+    weights[1].wait()
+
+    @pl.loop(0, groups)
     def _(g):
-        x = mid_ref[pl.ds(first + g * step, step)].reshape(step * columns, width)
-        y = sublayer(x, project_ref, output_ref, columns)
+        fetch(g).wait()
+        y = sublayer(to_lines(x_ref[g], swap), cp_ref, co_ref, rows, first, count)
+        mid_ref[:, at(g), :] = from_lines(y, swap, count)
+
+    weights[2].wait()
+    weights[3].wait()
+
+    def give(g):
+        part = pl.ds(g * step, step)
+        return pltpu.make_async_copy(out_ref.at[part], out_hbm.at[part], sems.at[groups + 4])
+
+    @pl.loop(0, count // step)
+    def _(g):
+        x = mid_ref[pl.ds(g * step, step)].reshape(step * columns, width)
+        y = sublayer(x, rp_ref, ro_ref, columns)
+
+        @pl.when(g > 0)
+        def _():
+            give(g - 1).wait()
+
         out_ref[pl.ds(g * step, step)] = y.reshape(step, columns, width)
-
-
-def column_row_kernel(x_ref, cp_ref, co_ref, rp_ref, ro_ref, mid_ref, out_ref):
-    rows, columns, _ = x_ref.shape
-    swap = swap_matrix()
-
-    @pl.loop(0, columns // SIDE)
-    def _(g):
-        at = pl.ds(pl.multiple_of(g * SIDE, SIDE), SIDE)
-        x = to_lines(x_ref[:, at, :], swap)
-        y = sublayer(x, cp_ref, co_ref, rows)
-        mid_ref[:, at, :] = from_lines(y, swap, rows)
-
-    rows_of(mid_ref, 0, rp_ref, ro_ref, out_ref)
-
-
-def row_kernel(first, mid_ref, rp_ref, ro_ref, out_ref):
-    rows_of(mid_ref, first, rp_ref, ro_ref, out_ref)
+        give(g).start()
+
+    give(count // step - 1).wait()
 
 
 def frame_kernel(x_ref, fp_ref, fo_ref, we_ref, wc_ref, *rest):
@@ -200,24 +232,24 @@
     _, rows, columns, width = latent.shape
     owners = lax.axis_size("frame")
     unit = 2 * columns * width * width
-    one = rows // FIRST
-    two = rows - one
-    mid, chunk_one = local_call(
-        column_row_kernel,
-        (like(rows, columns, width), like(one, columns, width)),
-        (latent[0], cp, co, rp, ro),
-        [VMEM] * 5,
-        unit * 4 * (rows + one),
-    )
-    chunk_two = local_call(
-        functools.partial(row_kernel, one),
-        like(two, columns, width),
-        (mid, rp, ro),
-        [VMEM] * 3,
-        unit * 4 * two,
-    )
+    count = rows // CHUNKS
+    chunks = [
+        local_call(
+            functools.partial(column_row_kernel, first),
+            like(count, columns, width),
+            (latent[0], cp, co, rp, ro),
+            [ANY] * 5,
+            unit * (2 * rows + 6 * count),
+            [pltpu.VMEM((columns // SIDE, rows, SIDE, width), BF)]
+            + [pltpu.VMEM(w.shape, BF) for w in (cp, co, rp, ro)]
+            + [pltpu.VMEM((count, columns, width), BF)] * 2
+            + [pltpu.SemaphoreType.DMA((columns // SIDE + 5,))],
+            ANY,
+        )
+        for first in range(0, rows, count)
+    ]
     home = []
-    for chunk, after in ((chunk_one, (chunk_two,)), (chunk_two, ())):
+    for chunk, after in zip(chunks, [chunks[1:2]] + [()] * CHUNKS):
         height = chunk.shape[0]
         share = height * columns // owners
         owned = exchange(chunk.reshape(owners, share, width))

time: 145 us -> 142 us (0.979)
  waiting for transfers between devices: 35.9 us -> 26.1 us
  Pallas kernels: 60.6 us -> 67.3 us
    all_to_all x3, waiting for transfers between devices: 35.9 us -> 26.1 us  [exchange(): lax.all_to_all(blocks, 'frame', split_axis=0, concat_axis=0, tiled=True)]
    pallas_call x4, Pallas kernels: 60.6 us -> 67.3 us  [local_call(): pl.pallas_call(kernel, out_shape=out_shape, in_specs=specs, out_specs=jax...]
  transfers between devices with their start and end apart: 3 -> 3, of which waited for: 3 -> 3; matrix products, arithmetic and copies ran while one was open for 0% -> 0% of each run, Pallas kernels for 28% -> 35%
where the time goes in v4:
time: 142 us; the launch traced here: 140 us
  Pallas kernels  67.3 us (47%)
  blocking collectives  29.8 us (21%)
  waiting for transfers between devices  26.1 us (18%)
  starting transfers between devices  15.5 us (11%)
  other arithmetic  1.5 us (1%)
    pallas_call x4, Pallas kernels, local_call(): pl.pallas_call(kernel, out_shape=out_shape, in_specs=specs, out_specs=jax...  67.3 us
    all_to_all x1, blocking collectives, exchange(): lax.all_to_all(blocks, 'frame', split_axis=0, concat_axis=0, tiled=True)  29.8 us
    all_to_all x3, waiting for transfers between devices, exchange(): lax.all_to_all(blocks, 'frame', split_axis=0, concat_axis=0, tiled=True)  26.1 us
    all_to_all x3, starting transfers between devices, exchange(): lax.all_to_all(blocks, 'frame', split_axis=0, concat_axis=0, tiled=True)  15.5 us
  transfers between devices with their start and end apart: 3, of which 3 were waited for; matrix products, arithmetic and copies ran while one was open for 0% of the time, Pallas kernels for 35%

profile of v4, /device:TPU:18, one launch (start us, length us, event | category | flops | bytes accessed | tf_op | source)
XLA Modules:
  0.0 140.2 jit_solution(14582717423329876761)
XLA Ops:
  0.0 17.9 %shard_map.91 = bf16[16,64,512]{2,1,0:T(8,128)(2,1)} custom-call(bf16[32,64,512]{2,1,0:T(8,128)(2,1)} %bitcast.3, bf16[512,1536]{1,0:T(8,128)(2,1)} %cp_hbm.3, bf16[512,512]{1,0:T(8,128)(2,1)} %co_hbm.3, bf16[512,1536]{1,0:T(8,128)(2,1)} %rp_hbm.3, bf16[512,512]{1,0:T(8,128)(2,1)} %ro_hbm.3), custom_call_target="tpu_custom_call" | custom-call | flops 5368709120 | bytes 6291456 | tf_op jit(solution)/shard_map/pallas_call | solution.py:145
  17.9 6.2 %all-to-all-start = ((bf16[16,64,512]{2,1,0:T(8,128)(2,1)}), bf16[16,64,512]{2,1,0:T(8,128)(2,1)S(1)}, u32[]{:S(2)}, u32[]{:S(2)}) async-start(bf16[16,64,512]{2,1,0:T(8,128)(2,1)} %shard_map.91), calls=%async_computation | async-start | bytes 2097152 | tf_op jit(solution)/shard_map/all_to_all | solution.py:228
  24.1 18.1 %shard_map.92.rest_0_ = bf16[16,64,512]{2,1,0:T(8,128)(2,1)} custom-call(bf16[32,64,512]{2,1,0:T(8,128)(2,1)} %bitcast.4, bf16[512,1536]{1,0:T(8,128)(2,1)} %cp_hbm.3, bf16[512,512]{1,0:T(8,128)(2,1)} %co_hbm.3, bf16[512,1536]{1,0:T(8,128)(2,1)} %rp_hbm.3, bf16[512,512]{1,0:T(8,128)(2,1)} %ro_hbm.3), custom_call_target="tpu_custom_call" | custom-call | flops 5368709120 | bytes 6291456 | tf_op jit(solution)/shard_map/pallas_call | solution.py:145
  42.2 7.1 %all-to-all-done.x_ref = bf16[16,64,512]{2,1,0:T(8,128)(2,1)S(1)} async-done(((bf16[16,64,512]{2,1,0:T(8,128)(2,1)}), bf16[16,64,512]{2,1,0:T(8,128)(2,1)S(1)}, u32[]{:S(2)}, u32[]{:S(2)}) %all-to-all-start) | async-done | bytes 1048608 | tf_op jit(solution)/shard_map/all_to_all | solution.py:228
  49.3 0.0 copy-start.1
  49.3 4.6 %all-to-all-start.2 = ((bf16[16,64,512]{2,1,0:T(8,128)(2,1)}), bf16[16,64,512]{2,1,0:T(8,128)(2,1)S(1)}, u32[]{:S(2)}, u32[]{:S(2)}) async-start(bf16[16,64,512]{2,1,0:T(8,128)(2,1)} %shard_map.92.rest_0_), calls=%async_computation.2 | async-start | bytes 2097152 | tf_op jit(solution)/shard_map/all_to_all | solution.py:228
  53.9 0.0 copy-done.1
  53.9 15.6 %shard_map.93 = bf16[16,64,512]{2,1,0:T(8,128)(2,1)} custom-call(bf16[16,64,512]{2,1,0:T(8,128)(2,1)} %copy-done.1, bf16[512,1536]{1,0:T(8,128)(2,1)} %fp_ref.3, bf16[512,512]{1,0:T(8,128)(2,1)} %fo_ref.3, bf16[512,2048]{1,0:T(8,128)(2,1)} %we_ref.3, bf16[2048,512]{1,0:T(8,128)(2,1)} %wc_ref.3, bf16[16,64,512]{2,1,0:T(8,128)(2,1)} %shard_map.92.rest_0_), custom_call_target="tpu_custom_call" | custom-call | flops 6442450944 | bytes 8388608 | tf_op jit(solution)/shard_map/pallas_call | solution.py:145
  69.5 9.6 %all-to-all-done.2.x_ref = bf16[16,64,512]{2,1,0:T(8,128)(2,1)S(1)} async-done(((bf16[16,64,512]{2,1,0:T(8,128)(2,1)}), bf16[16,64,512]{2,1,0:T(8,128)(2,1)S(1)}, u32[]{:S(2)}, u32[]{:S(2)}) %all-to-all-start.2) | async-done | bytes 1048608 | tf_op jit(solution)/shard_map/all_to_all | solution.py:228
  79.1 0.0 copy-start
  79.1 4.6 %all-to-all-start.1 = ((bf16[16,64,512]{2,1,0:T(8,128)(2,1)}), bf16[16,64,512]{2,1,0:T(8,128)(2,1)S(1)}, u32[]{:S(2)}, u32[]{:S(2)}) async-start(bf16[16,64,512]{2,1,0:T(8,128)(2,1)} %shard_map.93), calls=%async_computation.1 | async-start | bytes 2097152 | tf_op jit(solution)/shard_map/all_to_all | solution.py:228
  83.7 0.0 copy-done
  83.7 15.7 %shard_map.94 = bf16[16,64,512]{2,1,0:T(8,128)(2,1)} custom-call(bf16[16,64,512]{2,1,0:T(8,128)(2,1)} %copy-done, bf16[512,1536]{1,0:T(8,128)(2,1)} %fp_ref.3, bf16[512,512]{1,0:T(8,128)(2,1)} %fo_ref.3, bf16[512,2048]{1,0:T(8,128)(2,1)} %we_ref.3, bf16[2048,512]{1,0:T(8,128)(2,1)} %wc_ref.3), custom_call_target="tpu_custom_call" | custom-call | flops 6442450944 | bytes 7340032 | tf_op jit(solution)/shard_map/pallas_call | solution.py:145
  99.4 9.5 %all-to-all-done.1 = bf16[16,64,512]{2,1,0:T(8,128)(2,1)S(1)} async-done(((bf16[16,64,512]{2,1,0:T(8,128)(2,1)}), bf16[16,64,512]{2,1,0:T(8,128)(2,1)S(1)}, u32[]{:S(2)}, u32[]{:S(2)}) %all-to-all-start.1) | async-done | bytes 1048608 | tf_op jit(solution)/shard_map/all_to_all | solution.py:228
  108.9 29.8 %all_to_all.20 = bf16[16,64,512]{2,1,0:T(8,128)(2,1)S(1)} all-to-all(bf16[16,64,512]{2,1,0:T(8,128)(2,1)} %shard_map.94), channel_id=1, replica_groups=mesh['parts'=2,'frame'=16] {'frame'}, dimensions={0} | all-to-all | bytes 2097152 | tf_op jit(solution)/shard_map/all_to_all | solution.py:228
  138.7 1.5 %maximum_bitcast_fusion = bf16[1,32,64,512]{3,2,1,0:T(8,128)(2,1)} fusion(bf16[16,64,512]{2,1,0:T(8,128)(2,1)S(1)} %all_to_all.20, bf16[16,64,512]{2,1,0:T(8,128)(2,1)S(1)} %all-to-all-done.1), kind=kLoop, calls=%fused_computation | loop fusion | flops 1048576 | bytes 4194304 | tf_op jit(solution)/shard_map/broadcast_in_dim | solution.py:264
Async XLA Ops:
  17.9 31.4 %all-to-all-start = ((bf16[16,64,512]{2,1,0:T(8,128)(2,1)}), bf16[16,64,512]{2,1,0:T(8,128)(2,1)S(1)}, u32[]{:S(2)}, u32[]{:S(2)}) async-start(bf16[16,64,512]{2,1,0:T(8,128)(2,1)} %shard_map.91), calls=%async_computation | async-start | bytes 2097152 | tf_op jit(solution)/shard_map/all_to_all | solution.py:228
  49.3 4.6 %copy-start.1 = (bf16[16,64,512]{2,1,0:T(8,128)(2,1)}, bf16[16,64,512]{2,1,0:T(8,128)(2,1)S(1)}, u32[]{:S(2)}) copy-start(bf16[16,64,512]{2,1,0:T(8,128)(2,1)S(1)} %all-to-all-done.x_ref) | copy-start | bytes 3145732
  49.3 29.8 %all-to-all-start.2 = ((bf16[16,64,512]{2,1,0:T(8,128)(2,1)}), bf16[16,64,512]{2,1,0:T(8,128)(2,1)S(1)}, u32[]{:S(2)}, u32[]{:S(2)}) async-start(bf16[16,64,512]{2,1,0:T(8,128)(2,1)} %shard_map.92.rest_0_), calls=%async_computation.2 | async-start | bytes 2097152 | tf_op jit(solution)/shard_map/all_to_all | solution.py:228
  79.1 4.6 %copy-start = (bf16[16,64,512]{2,1,0:T(8,128)(2,1)}, bf16[16,64,512]{2,1,0:T(8,128)(2,1)S(1)}, u32[]{:S(2)}) copy-start(bf16[16,64,512]{2,1,0:T(8,128)(2,1)S(1)} %all-to-all-done.2.x_ref) | copy-start | bytes 3145732
  79.1 29.8 %all-to-all-start.1 = ((bf16[16,64,512]{2,1,0:T(8,128)(2,1)}), bf16[16,64,512]{2,1,0:T(8,128)(2,1)S(1)}, u32[]{:S(2)}, u32[]{:S(2)}) async-start(bf16[16,64,512]{2,1,0:T(8,128)(2,1)} %shard_map.93), calls=%async_computation.1 | async-start | bytes 2097152 | tf_op jit(solution)/shard_map/all_to_all | solution.py:228

commit v5 on v4

--- a/solution.py
+++ b/solution.py
@@ -138,6 +138,7 @@
 
 VMEM = pl.BlockSpec(memory_space=pltpu.VMEM)
 ANY = pl.BlockSpec(memory_space=pl.ANY)
+SMEM = pl.BlockSpec(memory_space=pltpu.SMEM)
 
 
 def local_call(kernel, out_shape, args, specs, flops, scratch=(), out_spec=VMEM):
@@ -207,8 +208,7 @@
     give(count // step - 1).wait()
 
 
-def frame_kernel(x_ref, fp_ref, fo_ref, we_ref, wc_ref, *rest):
-    out_ref = rest[-1]
+def frame_lines(x_ref, fp_ref, fo_ref, we_ref, wc_ref, store):
     frames, pixels, _ = x_ref.shape
     swap = swap_matrix()
     size = frames * SIDE
@@ -221,7 +221,40 @@
         y = sublayer(x, fp_ref, fo_ref, frames)
         y = feed_forward(y, we_ref, wc_ref)
         for i, a in enumerate(at):
-            out_ref[:, a, :] = from_lines(y[i * size : (i + 1) * size], swap, frames)
+            store(a, from_lines(y[i * size : (i + 1) * size], swap, frames))
+
+
+def frame_kernel(x_ref, fp_ref, fo_ref, we_ref, wc_ref, *rest):
+    out_ref = rest[-1]
+
+    def store(at, z):
+        out_ref[:, at, :] = z
+
+    frame_lines(x_ref, fp_ref, fo_ref, we_ref, wc_ref, store)
+
+
+def frame_sort_kernel(x_ref, fp_ref, fo_ref, we_ref, wc_ref, place_ref, out_ref):
+    def store(at, z):
+        for f in range(z.shape[0]):
+            out_ref[place_ref[f % 2], place_ref[2 + f // 2], at, :] = z[f]
+
+    frame_lines(x_ref, fp_ref, fo_ref, we_ref, wc_ref, store)
+
+
+def gather_kernel(place_ref, head_ref, own_ref, other_ref, *rest):
+    pieces, out_ref, sems = rest[:-2], rest[-2], rest[-1]
+    count, size = head_ref.shape[0], own_ref.shape[0]
+    copies = [pltpu.make_async_copy(head_ref, out_ref.at[pl.ds(0, count)], sems.at[0])]
+    for s in range(len(pieces) + 1):
+        for c in range(2):
+            owner = 2 * place_ref[2 + s] + place_ref[c]
+            to = out_ref.at[pl.ds(pl.multiple_of(count + owner * size, SIDE), size)]
+            source = pieces[s - 1].at[c] if s else (own_ref, other_ref)[c]
+            copies.append(pltpu.make_async_copy(source, to, sems.at[1 + 2 * s + c]))
+    for copy in copies:
+        copy.start()
+    for copy in copies:
+        copy.wait()
 
 
 def exchange(blocks):
@@ -248,20 +281,44 @@
         )
         for first in range(0, rows, count)
     ]
-    home = []
-    for chunk, after in zip(chunks, [chunks[1:2]] + [()] * CHUNKS):
-        height = chunk.shape[0]
-        share = height * columns // owners
-        owned = exchange(chunk.reshape(owners, share, width))
-        done = local_call(
-            frame_kernel,
-            like(owners, share, width),
-            (owned, fp, fo, we, wc, *after),
-            [VMEM] * 5 + [ANY] * len(after),
-            unit * 12 * height,
-        )
-        home.append(exchange(done).reshape(height, columns, width))
-    return jnp.concatenate(home, axis=0)[None]
+    share = count * columns // owners
+    chips = owners // 2
+    me = lax.axis_index("frame")
+    chip, core = me // 2, me % 2
+    place = jnp.stack([core, 1 - core] + [chip ^ s for s in range(chips)]).astype(jnp.int32)
+
+    def hop(block, step):
+        return lax.ppermute(block, "frame", [(i, i ^ step) for i in range(owners)])
+
+    one, two = [exchange(chunk.reshape(owners, share, width)) for chunk in chunks]
+    weights = (fp, fo, we, wc)
+    one = local_call(
+        frame_kernel,
+        like(owners, share, width),
+        (one, *weights, chunks[1]),
+        [VMEM] * 5 + [ANY],
+        unit * 12 * count,
+    )
+    one = exchange(one).reshape(count * columns, width)
+    two = local_call(
+        frame_sort_kernel,
+        like(2, chips, share, width),
+        (two, *weights, place),
+        [VMEM] * 5 + [SMEM],
+        unit * 12 * count,
+    )
+    other = hop(two[1], 1)
+    pieces = [hop(jnp.stack([two[0, s], other[s]]), 2 * s) for s in range(1, chips)]
+    result = local_call(
+        gather_kernel,
+        like(rows * columns, width),
+        (place, one, two[0, 0], other[0], *pieces),
+        [SMEM] + [VMEM] * (chips + 2),
+        unit,
+        [pltpu.SemaphoreType.DMA((2 * chips + 1,))],
+        ANY,
+    )
+    return result.reshape(latent.shape)
 
 
 def solution(mesh):

time: 142 us -> 138 us (0.972)
  blocking collectives: 29.8 us -> 0 us
  waiting for transfers between devices: 26.1 us -> 37.2 us
  starting transfers between devices: 15.5 us -> 24.6 us
  local copies, waits for them, and re-layouts: 0.01 us -> 5.04 us
  Pallas kernels: 67.3 us -> 70.3 us
    all_to_all x1 -> x0, blocking collectives: 29.8 us -> none  [exchange(): lax.all_to_all(blocks, 'frame', split_axis=0, concat_axis=0, tiled=True)]
    ppermute x0 -> x8, waiting for transfers between devices: none -> 21.2 us  [hop(): return lax.ppermute(block, 'frame', [(i, i ^ step) for i in range(owners)])]
    all_to_all x3, waiting for transfers between devices: 26.1 us -> 16 us  [exchange(): lax.all_to_all(blocks, 'frame', split_axis=0, concat_axis=0, tiled=True)]
    ppermute x0 -> x8, starting transfers between devices: none -> 9.14 us  [hop(): return lax.ppermute(block, 'frame', [(i, i ^ step) for i in range(owners)])]
    pallas_call x4 -> x5, Pallas kernels: 67.3 us -> 70.3 us  [local_call(): pl.pallas_call(kernel, out_shape=out_shape, in_specs=specs, out_specs=jax...]
    another operation x0 -> x2, local copies, waits for them, and re-layouts: none -> 2.29 us  [the longest x1 1.72 us: per_device(): jnp.stack([two[0, s], other[s]])]
    broadcast_in_dim x1 -> x0, other arithmetic: 1.5 us -> none  [per_device(): return jnp.concatenate(home, axis=0)[None]]
  transfers between devices with their start and end apart: 3 -> 11, of which waited for: 3 -> 8; matrix products, arithmetic and copies ran while one was open for 0% -> 3% of each run, Pallas kernels for 35% -> 36%
where the time goes in v5:
time: 138 us
  Pallas kernels  70.3 us (51%)
  waiting for transfers between devices  37.2 us (27%)
  starting transfers between devices  24.6 us (18%)
  local copies, waits for them, and re-layouts  5.04 us (4%)
    pallas_call x5, Pallas kernels, local_call(): pl.pallas_call(kernel, out_shape=out_shape, in_specs=specs, out_specs=jax...  70.3 us
    ppermute x8, waiting for transfers between devices, hop(): return lax.ppermute(block, 'frame', [(i, i ^ step) for i in range(owners)])  21.2 us
    all_to_all x3, waiting for transfers between devices, exchange(): lax.all_to_all(blocks, 'frame', split_axis=0, concat_axis=0, tiled=True)  16 us
    all_to_all x3, starting transfers between devices, exchange(): lax.all_to_all(blocks, 'frame', split_axis=0, concat_axis=0, tiled=True)  15.5 us
    ppermute x8, starting transfers between devices, hop(): return lax.ppermute(block, 'frame', [(i, i ^ step) for i in range(owners)])  9.14 us
  transfers between devices with their start and end apart: 11, of which 8 were waited for; matrix products, arithmetic and copies ran while one was open for 3% of the time, Pallas kernels for 36%

profile of v5, /device:TPU:18, one launch (start us, length us, event | category | flops | bytes accessed | tf_op | source)
XLA Modules:
  0.0 137.6 jit_solution(776063265971090159)
XLA Ops:
  0.0 17.9 %shard_map.91 = bf16[16,64,512]{2,1,0:T(8,128)(2,1)} custom-call(bf16[32,64,512]{2,1,0:T(8,128)(2,1)} %bitcast.34, bf16[512,1536]{1,0:T(8,128)(2,1)} %cp_hbm.3, bf16[512,512]{1,0:T(8,128)(2,1)} %co_hbm.3, bf16[512,1536]{1,0:T(8,128)(2,1)} %rp_hbm.3, bf16[512,512]{1,0:T(8,128)(2,1)} %ro_hbm.3), custom_call_target="tpu_custom_call" | custom-call | flops 5368709120 | bytes 6291456 | tf_op jit(solution)/shard_map/pallas_call | solution.py:146
  17.9 6.2 %all-to-all-start = ((bf16[16,64,512]{2,1,0:T(8,128)(2,1)}), bf16[16,64,512]{2,1,0:T(8,128)(2,1)S(1)}, u32[]{:S(2)}, u32[]{:S(2)}) async-start(bf16[16,64,512]{2,1,0:T(8,128)(2,1)} %shard_map.91), calls=%async_computation | async-start | bytes 2097152 | tf_op jit(solution)/shard_map/all_to_all | solution.py:261
  24.1 18.1 %shard_map.92.rest_0_ = bf16[16,64,512]{2,1,0:T(8,128)(2,1)} custom-call(bf16[32,64,512]{2,1,0:T(8,128)(2,1)} %bitcast.35, bf16[512,1536]{1,0:T(8,128)(2,1)} %cp_hbm.3, bf16[512,512]{1,0:T(8,128)(2,1)} %co_hbm.3, bf16[512,1536]{1,0:T(8,128)(2,1)} %rp_hbm.3, bf16[512,512]{1,0:T(8,128)(2,1)} %ro_hbm.3), custom_call_target="tpu_custom_call" | custom-call | flops 5368709120 | bytes 6291456 | tf_op jit(solution)/shard_map/pallas_call | solution.py:146
  42.2 7.0 %all-to-all-done.x_ref = bf16[16,64,512]{2,1,0:T(8,128)(2,1)S(1)} async-done(((bf16[16,64,512]{2,1,0:T(8,128)(2,1)}), bf16[16,64,512]{2,1,0:T(8,128)(2,1)S(1)}, u32[]{:S(2)}, u32[]{:S(2)}) %all-to-all-start) | async-done | bytes 1048608 | tf_op jit(solution)/shard_map/all_to_all | solution.py:261
  49.3 4.6 %all-to-all-start.2 = ((bf16[16,64,512]{2,1,0:T(8,128)(2,1)}), bf16[16,64,512]{2,1,0:T(8,128)(2,1)S(1)}, u32[]{:S(2)}, u32[]{:S(2)}) async-start(bf16[16,64,512]{2,1,0:T(8,128)(2,1)} %shard_map.92.rest_0_), calls=%async_computation.2 | async-start | bytes 2097152 | tf_op jit(solution)/shard_map/all_to_all | solution.py:261
  53.9 0.6 stack.64.place_ref
  54.5 15.6 %shard_map.93 = bf16[16,64,512]{2,1,0:T(8,128)(2,1)} custom-call(bf16[16,64,512]{2,1,0:T(8,128)(2,1)} %copy-done.2, bf16[512,1536]{1,0:T(8,128)(2,1)} %fp_ref.3, bf16[512,512]{1,0:T(8,128)(2,1)} %fo_ref.3, bf16[512,2048]{1,0:T(8,128)(2,1)} %we_ref.3, bf16[2048,512]{1,0:T(8,128)(2,1)} %wc_ref.3, bf16[16,64,512]{2,1,0:T(8,128)(2,1)} %shard_map.92.rest_0_), custom_call_target="tpu_custom_call" | custom-call | flops 6442450944 | bytes 8388608 | tf_op jit(solution)/shard_map/pallas_call | solution.py:146
  70.1 9.0 %all-to-all-done.2.x_ref = bf16[16,64,512]{2,1,0:T(8,128)(2,1)S(1)} async-done(((bf16[16,64,512]{2,1,0:T(8,128)(2,1)}), bf16[16,64,512]{2,1,0:T(8,128)(2,1)S(1)}, u32[]{:S(2)}, u32[]{:S(2)}) %all-to-all-start.2) | async-done | bytes 1048608 | tf_op jit(solution)/shard_map/all_to_all | solution.py:261
  79.1 4.6 %all-to-all-start.1 = ((bf16[16,64,512]{2,1,0:T(8,128)(2,1)}), bf16[16,64,512]{2,1,0:T(8,128)(2,1)S(1)}, u32[]{:S(2)}, u32[]{:S(2)}) async-start(bf16[16,64,512]{2,1,0:T(8,128)(2,1)} %shard_map.93), calls=%async_computation.1 | async-start | bytes 2097152 | tf_op jit(solution)/shard_map/all_to_all | solution.py:261
  83.7 15.7 %shard_map.94 = bf16[2,8,64,512]{3,2,1,0:T(8,128)(2,1)} custom-call(bf16[16,64,512]{2,1,0:T(8,128)(2,1)} %copy-done.1, bf16[512,1536]{1,0:T(8,128)(2,1)} %fp_ref.3, bf16[512,512]{1,0:T(8,128)(2,1)} %fo_ref.3, bf16[512,2048]{1,0:T(8,128)(2,1)} %we_ref.3, bf16[2048,512]{1,0:T(8,128)(2,1)} %wc_ref.3, s32[10]{0:T(128)} %stack.64.place_ref), custom_call_target="tpu_custom_call" | custom-call | flops 6442450944 | bytes 7340052 | tf_op jit(solution)/shard_map/pallas_call | solution.py:146
  99.4 1.1 slice_bitcast_fusion
  100.5 0.2 collective-permute-start
  100.7 1.7 %slice_bitcast_fusion.1 = (bf16[1,64,512]{2,1,0:T(8,128)(2,1)S(1)}, bf16[1,64,512]{2,1,0:T(8,128)(2,1)S(1)}, bf16[1,64,512]{2,1,0:T(8,128)(2,1)S(1)}, bf16[1,64,...) fusion(bf16[2,8,64,512]{3,2,1,0:T(8,128)(2,1)} %shard_map.94), kind=kLoop, calls=%fused_computation.8 | loop fusion | bytes 1048576 | tf_op jit(solution)/shard_map/stack;squeeze | solution.py:311
  102.4 0.0 collective-permute-done
  102.5 0.7 fusion
  103.1 1.5 %collective-permute-start.1 = (bf16[2,64,512]{2,1,0:T(8,128)(2,1)S(1)}, bf16[2,64,512]{2,1,0:T(8,128)(2,1)S(1)}, u32[]{:S(2)}, u32[]{:S(2)}) collective-permute-start(bf16[2,64,512]{2,1,0:T(8,128)(2,1)S(1)} %pad_maximum_fusion), channel_id=1, source_target_pairs={{0,2},{1,3},{2,0},{3,1},{4,6},{5,7},{6,4},{7,5},{8,10},{9,11},{10,... | collective-permute-start | bytes 393224 | tf_op jit(solution)/shard_map/ppermute | solution.py:291
  104.7 1.5 %collective-permute-start.2 = (bf16[2,64,512]{2,1,0:T(8,128)(2,1)S(1)}, bf16[2,64,512]{2,1,0:T(8,128)(2,1)S(1)}, u32[]{:S(2)}, u32[]{:S(2)}) collective-permute-start(bf16[2,64,512]{2,1,0:T(8,128)(2,1)S(1)} %pad_maximum_fusion.1), channel_id=1, source_target_pairs={{0,4},{1,5},{2,6},{3,7},{4,0},{5,1},{6,2},{7,3},{8,12},{9,13},{10,... | collective-permute-start | bytes 393224 | tf_op jit(solution)/shard_map/ppermute | solution.py:291
  106.2 0.6 collective-permute-start.3
  106.9 0.4 collective-permute-start.4
  107.3 3.6 %collective-permute-start.5 = (bf16[2,64,512]{2,1,0:T(8,128)(2,1)S(1)}, bf16[2,64,512]{2,1,0:T(8,128)(2,1)S(1)}, u32[]{:S(2)}, u32[]{:S(2)}) collective-permute-start(bf16[2,64,512]{2,1,0:T(8,128)(2,1)S(1)} %pad_maximum_fusion.4), channel_id=1, source_target_pairs={{0,10},{1,11},{2,8},{3,9},{4,14},{5,15},{6,12},{7,13},{8,2},{9,3},... | collective-permute-start | bytes 393224 | tf_op jit(solution)/shard_map/ppermute | solution.py:291
  110.9 1.7 %collective-permute-done.1.rest_0_ = bf16[2,64,512]{2,1,0:T(8,128)(2,1)S(1)} collective-permute-done((bf16[2,64,512]{2,1,0:T(8,128)(2,1)S(1)}, bf16[2,64,512]{2,1,0:T(8,128)(2,1)S(1)}, u32[]{:S(2)}, u32[]{:S(2)}) %collective-permute-start.1) | collective-permute-done | bytes 131104 | tf_op jit(solution)/shard_map/ppermute | solution.py:291
  112.6 0.3 collective-permute-start.6
  112.9 0.0 collective-permute-done.2.rest_1_
  112.9 1.0 collective-permute-start.7
  113.9 1.8 %collective-permute-done.3.rest_2_ = bf16[2,64,512]{2,1,0:T(8,128)(2,1)S(1)} collective-permute-done((bf16[2,64,512]{2,1,0:T(8,128)(2,1)S(1)}, bf16[2,64,512]{2,1,0:T(8,128)(2,1)S(1)}, u32[]{:S(2)}, u32[]{:S(2)}) %collective-permute-start.3) | collective-permute-done | bytes 131104 | tf_op jit(solution)/shard_map/ppermute | solution.py:291
  115.7 1.1 collective-permute-done.4.rest_3_
  116.8 8.8 %collective-permute-done.5.rest_4_ = bf16[2,64,512]{2,1,0:T(8,128)(2,1)S(1)} collective-permute-done((bf16[2,64,512]{2,1,0:T(8,128)(2,1)S(1)}, bf16[2,64,512]{2,1,0:T(8,128)(2,1)S(1)}, u32[]{:S(2)}, u32[]{:S(2)}) %collective-permute-start.5) | collective-permute-done | bytes 131104 | tf_op jit(solution)/shard_map/ppermute | solution.py:291
  125.6 5.4 %collective-permute-done.6.rest_5_ = bf16[2,64,512]{2,1,0:T(8,128)(2,1)S(1)} collective-permute-done((bf16[2,64,512]{2,1,0:T(8,128)(2,1)S(1)}, bf16[2,64,512]{2,1,0:T(8,128)(2,1)S(1)}, u32[]{:S(2)}, u32[]{:S(2)}) %collective-permute-start.6) | collective-permute-done | bytes 131104 | tf_op jit(solution)/shard_map/ppermute | solution.py:291
  131.0 2.3 %collective-permute-done.7.rest_6_ = bf16[2,64,512]{2,1,0:T(8,128)(2,1)S(1)} collective-permute-done((bf16[2,64,512]{2,1,0:T(8,128)(2,1)S(1)}, bf16[2,64,512]{2,1,0:T(8,128)(2,1)S(1)}, u32[]{:S(2)}, u32[]{:S(2)}) %collective-permute-start.7) | collective-permute-done | bytes 131104 | tf_op jit(solution)/shard_map/ppermute | solution.py:291
  133.4 0.6 copy-done.9
  134.0 0.4 copy-done
  134.4 3.0 %shard_map.95 = bf16[2048,512]{1,0:T(8,128)(2,1)} custom-call(s32[10]{0:T(128)} %stack.64.place_ref, bf16[1024,512]{1,0:T(8,128)(2,1)} %bitcast.33, bf16[64,512]{1,0:T(8,128)(2,1)} %get-tuple-element.12.own_ref, bf16[64,512]{1,0:T(8,128)(2,1)} %get-tuple-element.20.other_ref, bf16[2,64,512]{2,1,0:T(8,128)(2,1)} %copy-done.3, bf16[2,64,512]{2,1,0:T(8,128)(2,1)} %copy-done.4, ...), custom_call_target="tpu_custom_call" | custom-call | flops 33554432 | bytes 2097172 | tf_op jit(solution)/shard_map/pallas_call | solution.py:146
  (26 shorter events, 0.1 us)
Async XLA Ops:
  17.9 31.4 %all-to-all-start = ((bf16[16,64,512]{2,1,0:T(8,128)(2,1)}), bf16[16,64,512]{2,1,0:T(8,128)(2,1)S(1)}, u32[]{:S(2)}, u32[]{:S(2)}) async-start(bf16[16,64,512]{2,1,0:T(8,128)(2,1)} %shard_map.91), calls=%async_computation | async-start | bytes 2097152 | tf_op jit(solution)/shard_map/all_to_all | solution.py:261
  49.3 5.2 %copy-start.2 = (bf16[16,64,512]{2,1,0:T(8,128)(2,1)}, bf16[16,64,512]{2,1,0:T(8,128)(2,1)S(1)}, u32[]{:S(2)}) copy-start(bf16[16,64,512]{2,1,0:T(8,128)(2,1)S(1)} %all-to-all-done.x_ref) | copy-start | bytes 3145732
  49.3 29.8 %all-to-all-start.2 = ((bf16[16,64,512]{2,1,0:T(8,128)(2,1)}), bf16[16,64,512]{2,1,0:T(8,128)(2,1)S(1)}, u32[]{:S(2)}, u32[]{:S(2)}) async-start(bf16[16,64,512]{2,1,0:T(8,128)(2,1)} %shard_map.92.rest_0_), calls=%async_computation.2 | async-start | bytes 2097152 | tf_op jit(solution)/shard_map/all_to_all | solution.py:261
  79.1 4.6 %copy-start.1 = (bf16[16,64,512]{2,1,0:T(8,128)(2,1)}, bf16[16,64,512]{2,1,0:T(8,128)(2,1)S(1)}, u32[]{:S(2)}) copy-start(bf16[16,64,512]{2,1,0:T(8,128)(2,1)S(1)} %all-to-all-done.2.x_ref) | copy-start | bytes 3145732
  79.1 54.3 %all-to-all-start.1 = ((bf16[16,64,512]{2,1,0:T(8,128)(2,1)}), bf16[16,64,512]{2,1,0:T(8,128)(2,1)S(1)}, u32[]{:S(2)}, u32[]{:S(2)}) async-start(bf16[16,64,512]{2,1,0:T(8,128)(2,1)} %shard_map.93), calls=%async_computation.1 | async-start | bytes 2097152 | tf_op jit(solution)/shard_map/all_to_all | solution.py:261
  100.5 2.0 %collective-permute-start = (bf16[8,64,512]{2,1,0:T(8,128)(2,1)S(1)}, bf16[8,64,512]{2,1,0:T(8,128)(2,1)S(1)}, u32[]{:S(2)}, u32[]{:S(2)}) collective-permute-start(bf16[8,64,512]{2,1,0:T(8,128)(2,1)S(1)} %slice_bitcast_fusion), channel_id=1, source_target_pairs={{0,1},{1,0},{2,3},{3,2},{4,5},{5,4},{6,7},{7,6},{8,9},{9,8},{10,11... | collective-permute-start | bytes 1572872 | tf_op jit(solution)/shard_map/ppermute | solution.py:291
  103.1 9.5 %collective-permute-start.1 = (bf16[2,64,512]{2,1,0:T(8,128)(2,1)S(1)}, bf16[2,64,512]{2,1,0:T(8,128)(2,1)S(1)}, u32[]{:S(2)}, u32[]{:S(2)}) collective-permute-start(bf16[2,64,512]{2,1,0:T(8,128)(2,1)S(1)} %pad_maximum_fusion), channel_id=1, source_target_pairs={{0,2},{1,3},{2,0},{3,1},{4,6},{5,7},{6,4},{7,5},{8,10},{9,11},{10,... | collective-permute-start | bytes 393224 | tf_op jit(solution)/shard_map/ppermute | solution.py:291
  104.7 8.2 %collective-permute-start.2 = (bf16[2,64,512]{2,1,0:T(8,128)(2,1)S(1)}, bf16[2,64,512]{2,1,0:T(8,128)(2,1)S(1)}, u32[]{:S(2)}, u32[]{:S(2)}) collective-permute-start(bf16[2,64,512]{2,1,0:T(8,128)(2,1)S(1)} %pad_maximum_fusion.1), channel_id=1, source_target_pairs={{0,4},{1,5},{2,6},{3,7},{4,0},{5,1},{6,2},{7,3},{8,12},{9,13},{10,... | collective-permute-start | bytes 393224 | tf_op jit(solution)/shard_map/ppermute | solution.py:291
  106.2 9.5 %collective-permute-start.3 = (bf16[2,64,512]{2,1,0:T(8,128)(2,1)S(1)}, bf16[2,64,512]{2,1,0:T(8,128)(2,1)S(1)}, u32[]{:S(2)}, u32[]{:S(2)}) collective-permute-start(bf16[2,64,512]{2,1,0:T(8,128)(2,1)S(1)} %pad_maximum_fusion.2), channel_id=1, source_target_pairs={{0,6},{1,7},{2,4},{3,5},{4,2},{5,3},{6,0},{7,1},{8,14},{9,15},{10,... | collective-permute-start | bytes 393224 | tf_op jit(solution)/shard_map/ppermute | solution.py:291
  106.9 10.0 %collective-permute-start.4 = (bf16[2,64,512]{2,1,0:T(8,128)(2,1)S(1)}, bf16[2,64,512]{2,1,0:T(8,128)(2,1)S(1)}, u32[]{:S(2)}, u32[]{:S(2)}) collective-permute-start(bf16[2,64,512]{2,1,0:T(8,128)(2,1)S(1)} %pad_maximum_fusion.3), channel_id=1, source_target_pairs={{0,8},{1,9},{2,10},{3,11},{4,12},{5,13},{6,14},{7,15},{8,0},{9,1},... | collective-permute-start | bytes 393224 | tf_op jit(solution)/shard_map/ppermute | solution.py:291
  107.3 18.3 %collective-permute-start.5 = (bf16[2,64,512]{2,1,0:T(8,128)(2,1)S(1)}, bf16[2,64,512]{2,1,0:T(8,128)(2,1)S(1)}, u32[]{:S(2)}, u32[]{:S(2)}) collective-permute-start(bf16[2,64,512]{2,1,0:T(8,128)(2,1)S(1)} %pad_maximum_fusion.4), channel_id=1, source_target_pairs={{0,10},{1,11},{2,8},{3,9},{4,14},{5,15},{6,12},{7,13},{8,2},{9,3},... | collective-permute-start | bytes 393224 | tf_op jit(solution)/shard_map/ppermute | solution.py:291
  112.6 20.7 %copy-start.3 = (bf16[2,64,512]{2,1,0:T(8,128)(2,1)}, bf16[2,64,512]{2,1,0:T(8,128)(2,1)S(1)}, u32[]{:S(2)}) copy-start(bf16[2,64,512]{2,1,0:T(8,128)(2,1)S(1)} %collective-permute-done.1.rest_0_) | copy-start | bytes 393220
  112.6 18.4 %collective-permute-start.6 = (bf16[2,64,512]{2,1,0:T(8,128)(2,1)S(1)}, bf16[2,64,512]{2,1,0:T(8,128)(2,1)S(1)}, u32[]{:S(2)}, u32[]{:S(2)}) collective-permute-start(bf16[2,64,512]{2,1,0:T(8,128)(2,1)S(1)} %pad_maximum_fusion.5), channel_id=1, source_target_pairs={{0,12},{1,13},{2,14},{3,15},{4,8},{5,9},{6,10},{7,11},{8,4},{9,5},... | collective-permute-start | bytes 393224 | tf_op jit(solution)/shard_map/ppermute | solution.py:291
  112.9 20.4 %copy-start.4 = (bf16[2,64,512]{2,1,0:T(8,128)(2,1)}, bf16[2,64,512]{2,1,0:T(8,128)(2,1)S(1)}, u32[]{:S(2)}) copy-start(bf16[2,64,512]{2,1,0:T(8,128)(2,1)S(1)} %collective-permute-done.2.rest_1_) | copy-start | bytes 393220
  112.9 20.4 %collective-permute-start.7 = (bf16[2,64,512]{2,1,0:T(8,128)(2,1)S(1)}, bf16[2,64,512]{2,1,0:T(8,128)(2,1)S(1)}, u32[]{:S(2)}, u32[]{:S(2)}) collective-permute-start(bf16[2,64,512]{2,1,0:T(8,128)(2,1)S(1)} %pad_maximum_fusion.6), channel_id=1, source_target_pairs={{0,14},{1,15},{2,12},{3,13},{4,10},{5,11},{6,8},{7,9},{8,6},{9,7},... | collective-permute-start | bytes 393224 | tf_op jit(solution)/shard_map/ppermute | solution.py:291
  115.7 17.6 %copy-start.5 = (bf16[2,64,512]{2,1,0:T(8,128)(2,1)}, bf16[2,64,512]{2,1,0:T(8,128)(2,1)S(1)}, u32[]{:S(2)}) copy-start(bf16[2,64,512]{2,1,0:T(8,128)(2,1)S(1)} %collective-permute-done.3.rest_2_) | copy-start | bytes 393220
  116.8 16.5 %copy-start.6 = (bf16[2,64,512]{2,1,0:T(8,128)(2,1)}, bf16[2,64,512]{2,1,0:T(8,128)(2,1)S(1)}, u32[]{:S(2)}) copy-start(bf16[2,64,512]{2,1,0:T(8,128)(2,1)S(1)} %collective-permute-done.4.rest_3_) | copy-start | bytes 393220
  125.6 7.8 %copy-start.7 = (bf16[2,64,512]{2,1,0:T(8,128)(2,1)}, bf16[2,64,512]{2,1,0:T(8,128)(2,1)S(1)}, u32[]{:S(2)}) copy-start(bf16[2,64,512]{2,1,0:T(8,128)(2,1)S(1)} %collective-permute-done.5.rest_4_) | copy-start | bytes 393220
  131.0 2.4 %copy-start.8 = (bf16[2,64,512]{2,1,0:T(8,128)(2,1)}, bf16[2,64,512]{2,1,0:T(8,128)(2,1)S(1)}, u32[]{:S(2)}) copy-start(bf16[2,64,512]{2,1,0:T(8,128)(2,1)S(1)} %collective-permute-done.6.rest_5_) | copy-start | bytes 393220
  133.3 0.7 copy-start.9
  133.3 1.0 copy-start

commit v6 on v5

--- a/solution.py
+++ b/solution.py
@@ -141,7 +141,7 @@
 SMEM = pl.BlockSpec(memory_space=pltpu.SMEM)
 
 
-def local_call(kernel, out_shape, args, specs, flops, scratch=(), out_spec=VMEM):
+def local_call(kernel, out_shape, args, specs, flops, scratch=(), out_spec=VMEM, alias=None):
     size = sum(a.size * 2 for a in args)
     return pl.pallas_call(
         kernel,
@@ -149,6 +149,7 @@
         in_specs=specs,
         out_specs=jax.tree.map(lambda _: out_spec, out_shape),
         scratch_shapes=list(scratch),
+        input_output_aliases=alias or {},
         cost_estimate=pl.CostEstimate(flops=flops, bytes_accessed=size, transcendentals=0),
         compiler_params=pltpu.CompilerParams(vmem_limit_bytes=56 * 2**20),
     )(*args)
@@ -241,16 +242,22 @@
     frame_lines(x_ref, fp_ref, fo_ref, we_ref, wc_ref, store)
 
 
-def gather_kernel(place_ref, head_ref, own_ref, other_ref, *rest):
-    pieces, out_ref, sems = rest[:-2], rest[-2], rest[-1]
-    count, size = head_ref.shape[0], own_ref.shape[0]
-    copies = [pltpu.make_async_copy(head_ref, out_ref.at[pl.ds(0, count)], sems.at[0])]
+def head_kernel(head_ref, out_ref, sem):
+    copy = pltpu.make_async_copy(head_ref, out_ref.at[pl.ds(0, head_ref.shape[0])], sem)
+    copy.start()
+    copy.wait()
+
+
+def gather_kernel(count, place_ref, own_ref, other_ref, *rest):
+    pieces, out_ref, sems = rest[:-3], rest[-2], rest[-1]
+    size = own_ref.shape[0]
+    copies = []
     for s in range(len(pieces) + 1):
         for c in range(2):
             owner = 2 * place_ref[2 + s] + place_ref[c]
             to = out_ref.at[pl.ds(pl.multiple_of(count + owner * size, SIDE), size)]
             source = pieces[s - 1].at[c] if s else (own_ref, other_ref)[c]
-            copies.append(pltpu.make_async_copy(source, to, sems.at[1 + 2 * s + c]))
+            copies.append(pltpu.make_async_copy(source, to, sems.at[2 * s + c]))
     for copy in copies:
         copy.start()
     for copy in copies:
@@ -309,14 +316,17 @@
     )
     other = hop(two[1], 1)
     pieces = [hop(jnp.stack([two[0, s], other[s]]), 2 * s) for s in range(1, chips)]
+    whole = like(rows * columns, width)
+    result = local_call(head_kernel, whole, (one,), [VMEM], unit, [pltpu.SemaphoreType.DMA], ANY)
     result = local_call(
-        gather_kernel,
-        like(rows * columns, width),
-        (place, one, two[0, 0], other[0], *pieces),
-        [SMEM] + [VMEM] * (chips + 2),
+        functools.partial(gather_kernel, count * columns),
+        whole,
+        (place, two[0, 0], other[0], *pieces, result),
+        [SMEM] + [VMEM] * (chips + 1) + [ANY],
         unit,
-        [pltpu.SemaphoreType.DMA((2 * chips + 1,))],
+        [pltpu.SemaphoreType.DMA((2 * chips,))],
         ANY,
+        {chips + 2: 0},
     )
     return result.reshape(latent.shape)
 

time: 138 us -> 137 us (level)
  waiting for transfers between devices: 37.2 us -> 33.9 us
  Pallas kernels: 70.3 us -> 71.9 us
    ppermute x8, waiting for transfers between devices: 21.2 us -> 17.9 us  [hop(): return lax.ppermute(block, 'frame', [(i, i ^ step) for i in range(owners)])]
    pallas_call x5 -> x6, Pallas kernels: 70.3 us -> 71.9 us  [local_call(): pl.pallas_call(kernel, out_shape=out_shape, in_specs=specs, out_specs=jax...]
  transfers between devices with their start and end apart: 11 -> 11, of which waited for: 8 -> 6; matrix products, arithmetic and copies ran while one was open for 3% -> 3% of each run, Pallas kernels for 36% -> 38%
where the time goes in v6:
time: 137 us
  Pallas kernels  71.9 us (52%)
  waiting for transfers between devices  33.9 us (25%)
  starting transfers between devices  24.6 us (18%)
  local copies, waits for them, and re-layouts  5.75 us (4%)
    pallas_call x6, Pallas kernels, local_call(): pl.pallas_call(kernel, out_shape=out_shape, in_specs=specs, out_specs=jax...  71.9 us
    ppermute x8, waiting for transfers between devices, hop(): return lax.ppermute(block, 'frame', [(i, i ^ step) for i in range(owners)])  17.9 us
    all_to_all x3, waiting for transfers between devices, exchange(): lax.all_to_all(blocks, 'frame', split_axis=0, concat_axis=0, tiled=True)  16 us
    all_to_all x3, starting transfers between devices, exchange(): lax.all_to_all(blocks, 'frame', split_axis=0, concat_axis=0, tiled=True)  15.5 us
    ppermute x8, starting transfers between devices, hop(): return lax.ppermute(block, 'frame', [(i, i ^ step) for i in range(owners)])  9.14 us
  transfers between devices with their start and end apart: 11, of which 6 were waited for; matrix products, arithmetic and copies ran while one was open for 3% of the time, Pallas kernels for 38%

profile of v6, /device:TPU:18, one launch (start us, length us, event | category | flops | bytes accessed | tf_op | source)
XLA Modules:
  0.0 136.5 jit_solution(15960119495003096390)
XLA Ops:
  0.0 17.9 %shard_map.93 = bf16[16,64,512]{2,1,0:T(8,128)(2,1)} custom-call(bf16[32,64,512]{2,1,0:T(8,128)(2,1)} %bitcast.34, bf16[512,1536]{1,0:T(8,128)(2,1)} %cp_hbm.3, bf16[512,512]{1,0:T(8,128)(2,1)} %co_hbm.3, bf16[512,1536]{1,0:T(8,128)(2,1)} %rp_hbm.3, bf16[512,512]{1,0:T(8,128)(2,1)} %ro_hbm.3), custom_call_target="tpu_custom_call" | custom-call | flops 5368709120 | bytes 6291456 | tf_op jit(solution)/shard_map/pallas_call | solution.py:146
  17.9 6.2 %all-to-all-start.1 = ((bf16[16,64,512]{2,1,0:T(8,128)(2,1)}), bf16[16,64,512]{2,1,0:T(8,128)(2,1)S(1)}, u32[]{:S(2)}, u32[]{:S(2)}) async-start(bf16[16,64,512]{2,1,0:T(8,128)(2,1)} %shard_map.93), calls=%async_computation.1 | async-start | bytes 2097152 | tf_op jit(solution)/shard_map/all_to_all | solution.py:268
  24.1 18.1 %shard_map.91.rest_0_ = bf16[16,64,512]{2,1,0:T(8,128)(2,1)} custom-call(bf16[32,64,512]{2,1,0:T(8,128)(2,1)} %bitcast.35, bf16[512,1536]{1,0:T(8,128)(2,1)} %cp_hbm.3, bf16[512,512]{1,0:T(8,128)(2,1)} %co_hbm.3, bf16[512,1536]{1,0:T(8,128)(2,1)} %rp_hbm.3, bf16[512,512]{1,0:T(8,128)(2,1)} %ro_hbm.3), custom_call_target="tpu_custom_call" | custom-call | flops 5368709120 | bytes 6291456 | tf_op jit(solution)/shard_map/pallas_call | solution.py:146
  42.2 7.1 %all-to-all-done.1.x_ref = bf16[16,64,512]{2,1,0:T(8,128)(2,1)S(1)} async-done(((bf16[16,64,512]{2,1,0:T(8,128)(2,1)}), bf16[16,64,512]{2,1,0:T(8,128)(2,1)S(1)}, u32[]{:S(2)}, u32[]{:S(2)}) %all-to-all-start.1) | async-done | bytes 1048608 | tf_op jit(solution)/shard_map/all_to_all | solution.py:268
  49.3 4.6 %all-to-all-start = ((bf16[16,64,512]{2,1,0:T(8,128)(2,1)}), bf16[16,64,512]{2,1,0:T(8,128)(2,1)S(1)}, u32[]{:S(2)}, u32[]{:S(2)}) async-start(bf16[16,64,512]{2,1,0:T(8,128)(2,1)} %shard_map.91.rest_0_), calls=%async_computation | async-start | bytes 2097152 | tf_op jit(solution)/shard_map/all_to_all | solution.py:268
  53.9 0.7 stack.64.place_ref
  54.6 15.6 %shard_map.94 = bf16[16,64,512]{2,1,0:T(8,128)(2,1)} custom-call(bf16[16,64,512]{2,1,0:T(8,128)(2,1)} %copy-done.2, bf16[512,1536]{1,0:T(8,128)(2,1)} %fp_ref.3, bf16[512,512]{1,0:T(8,128)(2,1)} %fo_ref.3, bf16[512,2048]{1,0:T(8,128)(2,1)} %we_ref.3, bf16[2048,512]{1,0:T(8,128)(2,1)} %wc_ref.3, bf16[16,64,512]{2,1,0:T(8,128)(2,1)} %shard_map.91.rest_0_), custom_call_target="tpu_custom_call" | custom-call | flops 6442450944 | bytes 8388608 | tf_op jit(solution)/shard_map/pallas_call | solution.py:146
  70.2 8.9 %all-to-all-done.x_ref = bf16[16,64,512]{2,1,0:T(8,128)(2,1)S(1)} async-done(((bf16[16,64,512]{2,1,0:T(8,128)(2,1)}), bf16[16,64,512]{2,1,0:T(8,128)(2,1)S(1)}, u32[]{:S(2)}, u32[]{:S(2)}) %all-to-all-start) | async-done | bytes 1048608 | tf_op jit(solution)/shard_map/all_to_all | solution.py:268
  79.1 4.6 %all-to-all-start.2 = ((bf16[16,64,512]{2,1,0:T(8,128)(2,1)}), bf16[16,64,512]{2,1,0:T(8,128)(2,1)S(1)}, u32[]{:S(2)}, u32[]{:S(2)}) async-start(bf16[16,64,512]{2,1,0:T(8,128)(2,1)} %shard_map.94), calls=%async_computation.2 | async-start | bytes 2097152 | tf_op jit(solution)/shard_map/all_to_all | solution.py:268
  83.7 15.7 %shard_map.92 = bf16[2,8,64,512]{3,2,1,0:T(8,128)(2,1)} custom-call(bf16[16,64,512]{2,1,0:T(8,128)(2,1)} %copy-done.1, bf16[512,1536]{1,0:T(8,128)(2,1)} %fp_ref.3, bf16[512,512]{1,0:T(8,128)(2,1)} %fo_ref.3, bf16[512,2048]{1,0:T(8,128)(2,1)} %we_ref.3, bf16[2048,512]{1,0:T(8,128)(2,1)} %wc_ref.3, s32[10]{0:T(128)} %stack.64.place_ref), custom_call_target="tpu_custom_call" | custom-call | flops 6442450944 | bytes 7340052 | tf_op jit(solution)/shard_map/pallas_call | solution.py:146
  99.4 1.1 slice_bitcast_fusion
  100.5 0.2 collective-permute-start
  100.7 1.7 %slice_bitcast_fusion.1 = (bf16[1,64,512]{2,1,0:T(8,128)(2,1)S(1)}, bf16[1,64,512]{2,1,0:T(8,128)(2,1)S(1)}, bf16[1,64,512]{2,1,0:T(8,128)(2,1)S(1)}, bf16[1,64,...) fusion(bf16[2,8,64,512]{3,2,1,0:T(8,128)(2,1)} %shard_map.92), kind=kLoop, calls=%fused_computation.8 | loop fusion | bytes 1048576 | tf_op jit(solution)/shard_map/stack;squeeze | solution.py:318
  102.4 0.0 collective-permute-done
  102.5 0.7 fusion
  103.2 1.5 %collective-permute-start.1 = (bf16[2,64,512]{2,1,0:T(8,128)(2,1)S(1)}, bf16[2,64,512]{2,1,0:T(8,128)(2,1)S(1)}, u32[]{:S(2)}, u32[]{:S(2)}) collective-permute-start(bf16[2,64,512]{2,1,0:T(8,128)(2,1)S(1)} %pad_maximum_fusion), channel_id=1, source_target_pairs={{0,2},{1,3},{2,0},{3,1},{4,6},{5,7},{6,4},{7,5},{8,10},{9,11},{10,... | collective-permute-start | bytes 393224 | tf_op jit(solution)/shard_map/ppermute | solution.py:298
  104.7 1.5 %collective-permute-start.2 = (bf16[2,64,512]{2,1,0:T(8,128)(2,1)S(1)}, bf16[2,64,512]{2,1,0:T(8,128)(2,1)S(1)}, u32[]{:S(2)}, u32[]{:S(2)}) collective-permute-start(bf16[2,64,512]{2,1,0:T(8,128)(2,1)S(1)} %pad_maximum_fusion.1), channel_id=1, source_target_pairs={{0,4},{1,5},{2,6},{3,7},{4,0},{5,1},{6,2},{7,3},{8,12},{9,13},{10,... | collective-permute-start | bytes 393224 | tf_op jit(solution)/shard_map/ppermute | solution.py:298
  106.2 0.6 collective-permute-start.3
  106.9 0.4 collective-permute-start.4
  107.3 3.6 %collective-permute-start.5 = (bf16[2,64,512]{2,1,0:T(8,128)(2,1)S(1)}, bf16[2,64,512]{2,1,0:T(8,128)(2,1)S(1)}, u32[]{:S(2)}, u32[]{:S(2)}) collective-permute-start(bf16[2,64,512]{2,1,0:T(8,128)(2,1)S(1)} %pad_maximum_fusion.4), channel_id=1, source_target_pairs={{0,10},{1,11},{2,8},{3,9},{4,14},{5,15},{6,12},{7,13},{8,2},{9,3},... | collective-permute-start | bytes 393224 | tf_op jit(solution)/shard_map/ppermute | solution.py:298
  110.9 1.7 %collective-permute-done.1.rest_0_ = bf16[2,64,512]{2,1,0:T(8,128)(2,1)S(1)} collective-permute-done((bf16[2,64,512]{2,1,0:T(8,128)(2,1)S(1)}, bf16[2,64,512]{2,1,0:T(8,128)(2,1)S(1)}, u32[]{:S(2)}, u32[]{:S(2)}) %collective-permute-start.1) | collective-permute-done | bytes 131104 | tf_op jit(solution)/shard_map/ppermute | solution.py:298
  112.6 0.3 collective-permute-start.6
  112.9 0.0 collective-permute-done.2.rest_1_
  112.9 1.0 collective-permute-start.7
  113.9 0.0 all-to-all-done.2
  113.9 1.0 copy-done
  114.9 2.2 %shard_map.95.rest_7_ = bf16[2048,512]{1,0:T(8,128)(2,1)} custom-call(bf16[1024,512]{1,0:T(8,128)(2,1)} %bitcast.33), custom_call_target="tpu_custom_call" | custom-call | flops 33554432 | bytes 1048576 | tf_op jit(solution)/shard_map/pallas_call | solution.py:146
  117.2 8.4 %collective-permute-done.5.rest_4_ = bf16[2,64,512]{2,1,0:T(8,128)(2,1)S(1)} collective-permute-done((bf16[2,64,512]{2,1,0:T(8,128)(2,1)S(1)}, bf16[2,64,512]{2,1,0:T(8,128)(2,1)S(1)}, u32[]{:S(2)}, u32[]{:S(2)}) %collective-permute-start.5) | collective-permute-done | bytes 131104 | tf_op jit(solution)/shard_map/ppermute | solution.py:298
  125.6 5.4 %collective-permute-done.6.rest_5_ = bf16[2,64,512]{2,1,0:T(8,128)(2,1)S(1)} collective-permute-done((bf16[2,64,512]{2,1,0:T(8,128)(2,1)S(1)}, bf16[2,64,512]{2,1,0:T(8,128)(2,1)S(1)}, u32[]{:S(2)}, u32[]{:S(2)}) %collective-permute-start.6) | collective-permute-done | bytes 131104 | tf_op jit(solution)/shard_map/ppermute | solution.py:298
  131.0 2.3 %collective-permute-done.7.rest_6_ = bf16[2,64,512]{2,1,0:T(8,128)(2,1)S(1)} collective-permute-done((bf16[2,64,512]{2,1,0:T(8,128)(2,1)S(1)}, bf16[2,64,512]{2,1,0:T(8,128)(2,1)S(1)}, u32[]{:S(2)}, u32[]{:S(2)}) %collective-permute-start.7) | collective-permute-done | bytes 131104 | tf_op jit(solution)/shard_map/ppermute | solution.py:298
  133.4 0.6 copy-done.9
  134.0 2.4 %shard_map.96 = bf16[2048,512]{1,0:T(8,128)(2,1)} custom-call(s32[10]{0:T(128)} %stack.64.place_ref, bf16[64,512]{1,0:T(8,128)(2,1)} %get-tuple-element.12.own_ref, bf16[64,512]{1,0:T(8,128)(2,1)} %get-tuple-element.20.other_ref, bf16[2,64,512]{2,1,0:T(8,128)(2,1)} %copy-done.3, bf16[2,64,512]{2,1,0:T(8,128)(2,1)} %copy-done.4, ...), custom_call_target="tpu_custom_call", output_to_operand_aliasing={{}: (10, {})} | custom-call | flops 33554432 | bytes 3145748 | tf_op jit(solution)/shard_map/pallas_call | solution.py:146
  (27 shorter events, 0.1 us)
Async XLA Ops:
  17.9 31.4 %all-to-all-start.1 = ((bf16[16,64,512]{2,1,0:T(8,128)(2,1)}), bf16[16,64,512]{2,1,0:T(8,128)(2,1)S(1)}, u32[]{:S(2)}, u32[]{:S(2)}) async-start(bf16[16,64,512]{2,1,0:T(8,128)(2,1)} %shard_map.93), calls=%async_computation.1 | async-start | bytes 2097152 | tf_op jit(solution)/shard_map/all_to_all | solution.py:268
  49.3 5.3 %copy-start.2 = (bf16[16,64,512]{2,1,0:T(8,128)(2,1)}, bf16[16,64,512]{2,1,0:T(8,128)(2,1)S(1)}, u32[]{:S(2)}) copy-start(bf16[16,64,512]{2,1,0:T(8,128)(2,1)S(1)} %all-to-all-done.1.x_ref) | copy-start | bytes 3145732
  49.3 29.8 %all-to-all-start = ((bf16[16,64,512]{2,1,0:T(8,128)(2,1)}), bf16[16,64,512]{2,1,0:T(8,128)(2,1)S(1)}, u32[]{:S(2)}, u32[]{:S(2)}) async-start(bf16[16,64,512]{2,1,0:T(8,128)(2,1)} %shard_map.91.rest_0_), calls=%async_computation | async-start | bytes 2097152 | tf_op jit(solution)/shard_map/all_to_all | solution.py:268
  79.1 4.6 %copy-start.1 = (bf16[16,64,512]{2,1,0:T(8,128)(2,1)}, bf16[16,64,512]{2,1,0:T(8,128)(2,1)S(1)}, u32[]{:S(2)}) copy-start(bf16[16,64,512]{2,1,0:T(8,128)(2,1)S(1)} %all-to-all-done.x_ref) | copy-start | bytes 3145732
  79.1 34.8 %all-to-all-start.2 = ((bf16[16,64,512]{2,1,0:T(8,128)(2,1)}), bf16[16,64,512]{2,1,0:T(8,128)(2,1)S(1)}, u32[]{:S(2)}, u32[]{:S(2)}) async-start(bf16[16,64,512]{2,1,0:T(8,128)(2,1)} %shard_map.94), calls=%async_computation.2 | async-start | bytes 2097152 | tf_op jit(solution)/shard_map/all_to_all | solution.py:268
  100.5 2.0 %collective-permute-start = (bf16[8,64,512]{2,1,0:T(8,128)(2,1)S(1)}, bf16[8,64,512]{2,1,0:T(8,128)(2,1)S(1)}, u32[]{:S(2)}, u32[]{:S(2)}) collective-permute-start(bf16[8,64,512]{2,1,0:T(8,128)(2,1)S(1)} %slice_bitcast_fusion), channel_id=1, source_target_pairs={{0,1},{1,0},{2,3},{3,2},{4,5},{5,4},{6,7},{7,6},{8,9},{9,8},{10,11... | collective-permute-start | bytes 1572872 | tf_op jit(solution)/shard_map/ppermute | solution.py:298
  103.2 9.5 %collective-permute-start.1 = (bf16[2,64,512]{2,1,0:T(8,128)(2,1)S(1)}, bf16[2,64,512]{2,1,0:T(8,128)(2,1)S(1)}, u32[]{:S(2)}, u32[]{:S(2)}) collective-permute-start(bf16[2,64,512]{2,1,0:T(8,128)(2,1)S(1)} %pad_maximum_fusion), channel_id=1, source_target_pairs={{0,2},{1,3},{2,0},{3,1},{4,6},{5,7},{6,4},{7,5},{8,10},{9,11},{10,... | collective-permute-start | bytes 393224 | tf_op jit(solution)/shard_map/ppermute | solution.py:298
  104.7 8.2 %collective-permute-start.2 = (bf16[2,64,512]{2,1,0:T(8,128)(2,1)S(1)}, bf16[2,64,512]{2,1,0:T(8,128)(2,1)S(1)}, u32[]{:S(2)}, u32[]{:S(2)}) collective-permute-start(bf16[2,64,512]{2,1,0:T(8,128)(2,1)S(1)} %pad_maximum_fusion.1), channel_id=1, source_target_pairs={{0,4},{1,5},{2,6},{3,7},{4,0},{5,1},{6,2},{7,3},{8,12},{9,13},{10,... | collective-permute-start | bytes 393224 | tf_op jit(solution)/shard_map/ppermute | solution.py:298
  106.2 10.9 %collective-permute-start.3 = (bf16[2,64,512]{2,1,0:T(8,128)(2,1)S(1)}, bf16[2,64,512]{2,1,0:T(8,128)(2,1)S(1)}, u32[]{:S(2)}, u32[]{:S(2)}) collective-permute-start(bf16[2,64,512]{2,1,0:T(8,128)(2,1)S(1)} %pad_maximum_fusion.2), channel_id=1, source_target_pairs={{0,6},{1,7},{2,4},{3,5},{4,2},{5,3},{6,0},{7,1},{8,14},{9,15},{10,... | collective-permute-start | bytes 393224 | tf_op jit(solution)/shard_map/ppermute | solution.py:298
  106.9 10.3 %collective-permute-start.4 = (bf16[2,64,512]{2,1,0:T(8,128)(2,1)S(1)}, bf16[2,64,512]{2,1,0:T(8,128)(2,1)S(1)}, u32[]{:S(2)}, u32[]{:S(2)}) collective-permute-start(bf16[2,64,512]{2,1,0:T(8,128)(2,1)S(1)} %pad_maximum_fusion.3), channel_id=1, source_target_pairs={{0,8},{1,9},{2,10},{3,11},{4,12},{5,13},{6,14},{7,15},{8,0},{9,1},... | collective-permute-start | bytes 393224 | tf_op jit(solution)/shard_map/ppermute | solution.py:298
  107.3 18.3 %collective-permute-start.5 = (bf16[2,64,512]{2,1,0:T(8,128)(2,1)S(1)}, bf16[2,64,512]{2,1,0:T(8,128)(2,1)S(1)}, u32[]{:S(2)}, u32[]{:S(2)}) collective-permute-start(bf16[2,64,512]{2,1,0:T(8,128)(2,1)S(1)} %pad_maximum_fusion.4), channel_id=1, source_target_pairs={{0,10},{1,11},{2,8},{3,9},{4,14},{5,15},{6,12},{7,13},{8,2},{9,3},... | collective-permute-start | bytes 393224 | tf_op jit(solution)/shard_map/ppermute | solution.py:298
  112.6 20.7 %copy-start.3 = (bf16[2,64,512]{2,1,0:T(8,128)(2,1)}, bf16[2,64,512]{2,1,0:T(8,128)(2,1)S(1)}, u32[]{:S(2)}) copy-start(bf16[2,64,512]{2,1,0:T(8,128)(2,1)S(1)} %collective-permute-done.1.rest_0_) | copy-start | bytes 393220
  112.6 18.4 %collective-permute-start.6 = (bf16[2,64,512]{2,1,0:T(8,128)(2,1)S(1)}, bf16[2,64,512]{2,1,0:T(8,128)(2,1)S(1)}, u32[]{:S(2)}, u32[]{:S(2)}) collective-permute-start(bf16[2,64,512]{2,1,0:T(8,128)(2,1)S(1)} %pad_maximum_fusion.5), channel_id=1, source_target_pairs={{0,12},{1,13},{2,14},{3,15},{4,8},{5,9},{6,10},{7,11},{8,4},{9,5},... | collective-permute-start | bytes 393224 | tf_op jit(solution)/shard_map/ppermute | solution.py:298
  112.9 20.4 %copy-start.4 = (bf16[2,64,512]{2,1,0:T(8,128)(2,1)}, bf16[2,64,512]{2,1,0:T(8,128)(2,1)S(1)}, u32[]{:S(2)}) copy-start(bf16[2,64,512]{2,1,0:T(8,128)(2,1)S(1)} %collective-permute-done.2.rest_1_) | copy-start | bytes 393220
  112.9 20.4 %collective-permute-start.7 = (bf16[2,64,512]{2,1,0:T(8,128)(2,1)S(1)}, bf16[2,64,512]{2,1,0:T(8,128)(2,1)S(1)}, u32[]{:S(2)}, u32[]{:S(2)}) collective-permute-start(bf16[2,64,512]{2,1,0:T(8,128)(2,1)S(1)} %pad_maximum_fusion.6), channel_id=1, source_target_pairs={{0,14},{1,15},{2,12},{3,13},{4,10},{5,11},{6,8},{7,9},{8,6},{9,7},... | collective-permute-start | bytes 393224 | tf_op jit(solution)/shard_map/ppermute | solution.py:298
  113.9 1.0 copy-start
  117.2 16.2 %copy-start.5 = (bf16[2,64,512]{2,1,0:T(8,128)(2,1)}, bf16[2,64,512]{2,1,0:T(8,128)(2,1)S(1)}, u32[]{:S(2)}) copy-start(bf16[2,64,512]{2,1,0:T(8,128)(2,1)S(1)} %collective-permute-done.3.rest_2_) | copy-start | bytes 393220
  117.2 16.2 %copy-start.6 = (bf16[2,64,512]{2,1,0:T(8,128)(2,1)}, bf16[2,64,512]{2,1,0:T(8,128)(2,1)S(1)}, u32[]{:S(2)}) copy-start(bf16[2,64,512]{2,1,0:T(8,128)(2,1)S(1)} %collective-permute-done.4.rest_3_) | copy-start | bytes 393220
  125.6 7.7 %copy-start.7 = (bf16[2,64,512]{2,1,0:T(8,128)(2,1)}, bf16[2,64,512]{2,1,0:T(8,128)(2,1)S(1)}, u32[]{:S(2)}) copy-start(bf16[2,64,512]{2,1,0:T(8,128)(2,1)S(1)} %collective-permute-done.5.rest_4_) | copy-start | bytes 393220
  131.0 2.3 %copy-start.8 = (bf16[2,64,512]{2,1,0:T(8,128)(2,1)}, bf16[2,64,512]{2,1,0:T(8,128)(2,1)S(1)}, u32[]{:S(2)}) copy-start(bf16[2,64,512]{2,1,0:T(8,128)(2,1)S(1)} %collective-permute-done.6.rest_5_) | copy-start | bytes 393220
  133.3 0.7 copy-start.9

commit v7 on v6

--- a/solution.py
+++ b/solution.py
@@ -234,10 +234,14 @@
     frame_lines(x_ref, fp_ref, fo_ref, we_ref, wc_ref, store)
 
 
-def frame_sort_kernel(x_ref, fp_ref, fo_ref, we_ref, wc_ref, place_ref, out_ref):
+def frame_sort_kernel(x_ref, fp_ref, fo_ref, we_ref, wc_ref, place_ref, own_ref, other_ref):
+    first = place_ref[0] == 0
+
     def store(at, z):
-        for f in range(z.shape[0]):
-            out_ref[place_ref[f % 2], place_ref[2 + f // 2], at, :] = z[f]
+        for f in range(0, z.shape[0], 2):
+            step = place_ref[2 + f // 2]
+            own_ref[step, at, :] = jnp.where(first, z[f], z[f + 1])
+            other_ref[step, at, :] = jnp.where(first, z[f + 1], z[f])
 
     frame_lines(x_ref, fp_ref, fo_ref, we_ref, wc_ref, store)
 
@@ -248,16 +252,15 @@
     copy.wait()
 
 
-def gather_kernel(count, place_ref, own_ref, other_ref, *rest):
-    pieces, out_ref, sems = rest[:-3], rest[-2], rest[-1]
-    size = own_ref.shape[0]
+def gather_kernel(count, nearest, place_ref, *refs):
+    pieces, out_ref, sems = refs[:-3], refs[-2], refs[-1]
+    size = pieces[0].shape[1]
     copies = []
-    for s in range(len(pieces) + 1):
+    for i, piece in enumerate(pieces):
         for c in range(2):
-            owner = 2 * place_ref[2 + s] + place_ref[c]
+            owner = 2 * place_ref[2 + nearest + i] + place_ref[c]
             to = out_ref.at[pl.ds(pl.multiple_of(count + owner * size, SIDE), size)]
-            source = pieces[s - 1].at[c] if s else (own_ref, other_ref)[c]
-            copies.append(pltpu.make_async_copy(source, to, sems.at[2 * s + c]))
+            copies.append(pltpu.make_async_copy(piece.at[c], to, sems.at[2 * i + c]))
     for copy in copies:
         copy.start()
     for copy in copies:
@@ -307,27 +310,30 @@
         unit * 12 * count,
     )
     one = exchange(one).reshape(count * columns, width)
-    two = local_call(
+    own, other = local_call(
         frame_sort_kernel,
-        like(2, chips, share, width),
+        [like(chips, share, width)] * 2,
         (two, *weights, place),
         [VMEM] * 5 + [SMEM],
         unit * 12 * count,
     )
-    other = hop(two[1], 1)
-    pieces = [hop(jnp.stack([two[0, s], other[s]]), 2 * s) for s in range(1, chips)]
+    other = hop(other, 1)
+    pieces = [jnp.stack([own[s], other[s]]) for s in range(chips)]
+    pieces = pieces[:1] + [hop(pieces[s], 2 * s) for s in range(1, chips)]
     whole = like(rows * columns, width)
     result = local_call(head_kernel, whole, (one,), [VMEM], unit, [pltpu.SemaphoreType.DMA], ANY)
-    result = local_call(
-        functools.partial(gather_kernel, count * columns),
-        whole,
-        (place, two[0, 0], other[0], *pieces, result),
-        [SMEM] + [VMEM] * (chips + 1) + [ANY],
-        unit,
-        [pltpu.SemaphoreType.DMA((2 * chips,))],
-        ANY,
-        {chips + 2: 0},
-    )
+    half = chips // 2
+    for nearest in (0, half):
+        result = local_call(
+            functools.partial(gather_kernel, count * columns, nearest),
+            whole,
+            (place, *pieces[nearest : nearest + half], result),
+            [SMEM] + [VMEM] * half + [ANY],
+            unit,
+            [pltpu.SemaphoreType.DMA((2 * half,))],
+            ANY,
+            {half + 1: 0},
+        )
     return result.reshape(latent.shape)
 
 

time: 137 us -> 140 us (1.022)
  the two profiles are of different devices: /device:TPU:18 before, /device:TPU:6 now
where the time goes in v7:
time: 140 us
  Pallas kernels  73.4 us (52%)
  starting transfers between devices  46.4 us (33%)
  waiting for transfers between devices  14 us (10%)
  local copies, waits for them, and re-layouts  4.71 us (3%)
    pallas_call x7, Pallas kernels, local_call(): pl.pallas_call(kernel, out_shape=out_shape, in_specs=specs, out_specs=jax...  73.4 us
    ppermute x8, starting transfers between devices, hop(): return lax.ppermute(block, 'frame', [(i, i ^ step) for i in range(owners)])  26.1 us
    all_to_all x3, starting transfers between devices, exchange(): lax.all_to_all(blocks, 'frame', split_axis=0, concat_axis=0, tiled=True)  20.4 us
    all_to_all x3, waiting for transfers between devices, exchange(): lax.all_to_all(blocks, 'frame', split_axis=0, concat_axis=0, tiled=True)  11.3 us
    unnamed x20, local copies, waits for them, and re-layouts  2.97 us
  transfers between devices with their start and end apart: 11, of which 5 were waited for; matrix products, arithmetic and copies ran while one was open for 2% of the time, Pallas kernels for 38%

profile of v7, /device:TPU:6, one launch (start us, length us, event | category | flops | bytes accessed | tf_op | source)
XLA Modules:
  0.0 139.6 jit_solution(8260425343164486650)
XLA Ops:
  0.0 17.9 %shard_map.93 = bf16[16,64,512]{2,1,0:T(8,128)(2,1)} custom-call(bf16[32,64,512]{2,1,0:T(8,128)(2,1)} %bitcast.14, bf16[512,1536]{1,0:T(8,128)(2,1)} %cp_hbm.3, bf16[512,512]{1,0:T(8,128)(2,1)} %co_hbm.3, bf16[512,1536]{1,0:T(8,128)(2,1)} %rp_hbm.3, bf16[512,512]{1,0:T(8,128)(2,1)} %ro_hbm.3), custom_call_target="tpu_custom_call" | custom-call | flops 5368709120 | bytes 6291456 | tf_op jit(solution)/shard_map/pallas_call | solution.py:146
  17.9 6.4 %all-to-all-start.1 = ((bf16[16,64,512]{2,1,0:T(8,128)(2,1)}), bf16[16,64,512]{2,1,0:T(8,128)(2,1)S(1)}, u32[]{:S(2)}, u32[]{:S(2)}) async-start(bf16[16,64,512]{2,1,0:T(8,128)(2,1)} %shard_map.93), calls=%async_computation.1 | async-start | bytes 2097152 | tf_op jit(solution)/shard_map/all_to_all | solution.py:271
  24.3 18.1 %shard_map.91.rest_0_ = bf16[16,64,512]{2,1,0:T(8,128)(2,1)} custom-call(bf16[32,64,512]{2,1,0:T(8,128)(2,1)} %bitcast.15, bf16[512,1536]{1,0:T(8,128)(2,1)} %cp_hbm.3, bf16[512,512]{1,0:T(8,128)(2,1)} %co_hbm.3, bf16[512,1536]{1,0:T(8,128)(2,1)} %rp_hbm.3, bf16[512,512]{1,0:T(8,128)(2,1)} %ro_hbm.3), custom_call_target="tpu_custom_call" | custom-call | flops 5368709120 | bytes 6291456 | tf_op jit(solution)/shard_map/pallas_call | solution.py:146
  42.4 4.7 %all-to-all-done.1.x_ref = bf16[16,64,512]{2,1,0:T(8,128)(2,1)S(1)} async-done(((bf16[16,64,512]{2,1,0:T(8,128)(2,1)}), bf16[16,64,512]{2,1,0:T(8,128)(2,1)S(1)}, u32[]{:S(2)}, u32[]{:S(2)}) %all-to-all-start.1) | async-done | bytes 1048608 | tf_op jit(solution)/shard_map/all_to_all | solution.py:271
  47.1 7.0 %all-to-all-start = ((bf16[16,64,512]{2,1,0:T(8,128)(2,1)}), bf16[16,64,512]{2,1,0:T(8,128)(2,1)S(1)}, u32[]{:S(2)}, u32[]{:S(2)}) async-start(bf16[16,64,512]{2,1,0:T(8,128)(2,1)} %shard_map.91.rest_0_), calls=%async_computation | async-start | bytes 2097152 | tf_op jit(solution)/shard_map/all_to_all | solution.py:271
  54.1 0.6 stack.67.place_ref
  54.7 15.6 %shard_map.94 = bf16[16,64,512]{2,1,0:T(8,128)(2,1)} custom-call(bf16[16,64,512]{2,1,0:T(8,128)(2,1)} %copy-done.2, bf16[512,1536]{1,0:T(8,128)(2,1)} %fp_ref.3, bf16[512,512]{1,0:T(8,128)(2,1)} %fo_ref.3, bf16[512,2048]{1,0:T(8,128)(2,1)} %we_ref.3, bf16[2048,512]{1,0:T(8,128)(2,1)} %wc_ref.3, bf16[16,64,512]{2,1,0:T(8,128)(2,1)} %shard_map.91.rest_0_), custom_call_target="tpu_custom_call" | custom-call | flops 6442450944 | bytes 8388608 | tf_op jit(solution)/shard_map/pallas_call | solution.py:146
  70.3 6.6 %all-to-all-done.x_ref = bf16[16,64,512]{2,1,0:T(8,128)(2,1)S(1)} async-done(((bf16[16,64,512]{2,1,0:T(8,128)(2,1)}), bf16[16,64,512]{2,1,0:T(8,128)(2,1)S(1)}, u32[]{:S(2)}, u32[]{:S(2)}) %all-to-all-start) | async-done | bytes 1048608 | tf_op jit(solution)/shard_map/all_to_all | solution.py:271
  76.9 7.0 %all-to-all-start.2 = ((bf16[16,64,512]{2,1,0:T(8,128)(2,1)}), bf16[16,64,512]{2,1,0:T(8,128)(2,1)S(1)}, u32[]{:S(2)}, u32[]{:S(2)}) async-start(bf16[16,64,512]{2,1,0:T(8,128)(2,1)} %shard_map.94), calls=%async_computation.2 | async-start | bytes 2097152 | tf_op jit(solution)/shard_map/all_to_all | solution.py:271
  83.9 15.7 %shard_map.92 = (bf16[8,64,512]{2,1,0:T(8,128)(2,1)}, bf16[8,64,512]{2,1,0:T(8,128)(2,1)}) custom-call(bf16[16,64,512]{2,1,0:T(8,128)(2,1)} %copy-done.1, bf16[512,1536]{1,0:T(8,128)(2,1)} %fp_ref.3, bf16[512,512]{1,0:T(8,128)(2,1)} %fo_ref.3, bf16[512,2048]{1,0:T(8,128)(2,1)} %we_ref.3, bf16[2048,512]{1,0:T(8,128)(2,1)} %wc_ref.3, s32[10]{0:T(128)} %stack.67.place_ref), custom_call_target="tpu_custom_call" | custom-call | flops 6442450944 | bytes 7340052 | tf_op jit(solution)/shard_map/pallas_call | solution.py:146
  99.6 0.2 collective-permute-start
  99.8 1.1 fusion
  100.9 0.9 collective-permute-done
  101.8 2.4 %collective-permute-start.1 = (bf16[2,64,512]{2,1,0:T(8,128)(2,1)S(1)}, bf16[2,64,512]{2,1,0:T(8,128)(2,1)S(1)}, u32[]{:S(2)}, u32[]{:S(2)}) collective-permute-start(bf16[2,64,512]{2,1,0:T(8,128)(2,1)S(1)} %pad_maximum_fusion), channel_id=1, source_target_pairs={{0,8},{1,9},{2,10},{3,11},{4,12},{5,13},{6,14},{7,15},{8,0},{9,1},... | collective-permute-start | bytes 393224 | tf_op jit(solution)/shard_map/ppermute | solution.py:301
  104.2 0.2 collective-permute-start.2
  104.5 1.9 %collective-permute-start.5 = (bf16[2,64,512]{2,1,0:T(8,128)(2,1)S(1)}, bf16[2,64,512]{2,1,0:T(8,128)(2,1)S(1)}, u32[]{:S(2)}, u32[]{:S(2)}) collective-permute-start(bf16[2,64,512]{2,1,0:T(8,128)(2,1)S(1)} %pad_maximum_fusion.5), channel_id=1, source_target_pairs={{0,2},{1,3},{2,0},{3,1},{4,6},{5,7},{6,4},{7,5},{8,10},{9,11},{10,... | collective-permute-start | bytes 393224 | tf_op jit(solution)/shard_map/ppermute | solution.py:301
  106.4 1.5 %collective-permute-start.6 = (bf16[2,64,512]{2,1,0:T(8,128)(2,1)S(1)}, bf16[2,64,512]{2,1,0:T(8,128)(2,1)S(1)}, u32[]{:S(2)}, u32[]{:S(2)}) collective-permute-start(bf16[2,64,512]{2,1,0:T(8,128)(2,1)S(1)} %pad_maximum_fusion.6), channel_id=1, source_target_pairs={{0,4},{1,5},{2,6},{3,7},{4,0},{5,1},{6,2},{7,3},{8,12},{9,13},{10,... | collective-permute-start | bytes 393224 | tf_op jit(solution)/shard_map/ppermute | solution.py:301
  108.0 0.2 collective-permute-start.7
  108.2 1.7 %collective-permute-done.5.refs_1_ = bf16[2,64,512]{2,1,0:T(8,128)(2,1)S(1)} collective-permute-done((bf16[2,64,512]{2,1,0:T(8,128)(2,1)S(1)}, bf16[2,64,512]{2,1,0:T(8,128)(2,1)S(1)}, u32[]{:S(2)}, u32[]{:S(2)}) %collective-permute-start.5) | collective-permute-done | bytes 131104 | tf_op jit(solution)/shard_map/ppermute | solution.py:301
  109.9 3.8 %collective-permute-start.3 = (bf16[2,64,512]{2,1,0:T(8,128)(2,1)S(1)}, bf16[2,64,512]{2,1,0:T(8,128)(2,1)S(1)}, u32[]{:S(2)}, u32[]{:S(2)}) collective-permute-start(bf16[2,64,512]{2,1,0:T(8,128)(2,1)S(1)} %pad_maximum_fusion.2), channel_id=1, source_target_pairs={{0,12},{1,13},{2,14},{3,15},{4,8},{5,9},{6,10},{7,11},{8,4},{9,5},... | collective-permute-start | bytes 393224 | tf_op jit(solution)/shard_map/ppermute | solution.py:301
  113.7 0.1 collective-permute-done.6.refs_2_
  113.7 15.8 %collective-permute-start.4 = (bf16[2,64,512]{2,1,0:T(8,128)(2,1)S(1)}, bf16[2,64,512]{2,1,0:T(8,128)(2,1)S(1)}, u32[]{:S(2)}, u32[]{:S(2)}) collective-permute-start(bf16[2,64,512]{2,1,0:T(8,128)(2,1)S(1)} %pad_maximum_fusion.3), channel_id=1, source_target_pairs={{0,14},{1,15},{2,12},{3,13},{4,10},{5,11},{6,8},{7,9},{8,6},{9,7},... | collective-permute-start | bytes 393224 | tf_op jit(solution)/shard_map/ppermute | solution.py:301
  129.6 0.7 pad_maximum_fusion.4.refs_0_
  130.2 1.0 copy-done
  131.2 2.2 %shard_map.95.refs_4_ = bf16[2048,512]{1,0:T(8,128)(2,1)} custom-call(bf16[1024,512]{1,0:T(8,128)(2,1)} %bitcast.13), custom_call_target="tpu_custom_call" | custom-call | flops 33554432 | bytes 1048576 | tf_op jit(solution)/shard_map/pallas_call | solution.py:146
  133.5 0.6 copy-done.9
  134.1 2.0 %shard_map.96.refs_4_ = bf16[2048,512]{1,0:T(8,128)(2,1)} custom-call(s32[10]{0:T(128)} %stack.67.place_ref, bf16[2,64,512]{2,1,0:T(8,128)(2,1)} %pad_maximum_fusion.4.refs_0_, bf16[2,64,512]{2,1,0:T(8,128)(2,1)} %copy-done.5, bf16[2,64,512]{2,1,0:T(8,128)(2,1)} %copy-done.7, bf16[2,64,512]{2,1,0:T(8,128)(2,1)} %copy-done.9, ...), custom_call_target="tpu_custom_call", output_to_operand_aliasing={{}: (5, {})} | custom-call | flops 33554432 | bytes 2621460 | tf_op jit(solution)/shard_map/pallas_call | solution.py:146
  136.1 0.6 copy-done.3
  136.7 0.0 copy-done.4
  136.8 0.1 copy-done.6
  136.8 0.6 copy-done.8
  137.5 2.0 %shard_map.97 = bf16[2048,512]{1,0:T(8,128)(2,1)} custom-call(s32[10]{0:T(128)} %stack.67.place_ref, bf16[2,64,512]{2,1,0:T(8,128)(2,1)} %copy-done.3, bf16[2,64,512]{2,1,0:T(8,128)(2,1)} %copy-done.4, bf16[2,64,512]{2,1,0:T(8,128)(2,1)} %copy-done.6, bf16[2,64,512]{2,1,0:T(8,128)(2,1)} %copy-done.8, ...), custom_call_target="tpu_custom_call", output_to_operand_aliasing={{}: (5, {})} | custom-call | flops 33554432 | bytes 2621460 | tf_op jit(solution)/shard_map/pallas_call | solution.py:146
  (28 shorter events, 0.2 us)
Async XLA Ops:
  17.9 29.2 %all-to-all-start.1 = ((bf16[16,64,512]{2,1,0:T(8,128)(2,1)}), bf16[16,64,512]{2,1,0:T(8,128)(2,1)S(1)}, u32[]{:S(2)}, u32[]{:S(2)}) async-start(bf16[16,64,512]{2,1,0:T(8,128)(2,1)} %shard_map.93), calls=%async_computation.1 | async-start | bytes 2097152 | tf_op jit(solution)/shard_map/all_to_all | solution.py:271
  47.1 7.6 %copy-start.2 = (bf16[16,64,512]{2,1,0:T(8,128)(2,1)}, bf16[16,64,512]{2,1,0:T(8,128)(2,1)S(1)}, u32[]{:S(2)}) copy-start(bf16[16,64,512]{2,1,0:T(8,128)(2,1)S(1)} %all-to-all-done.1.x_ref) | copy-start | bytes 3145732
  47.1 29.8 %all-to-all-start = ((bf16[16,64,512]{2,1,0:T(8,128)(2,1)}), bf16[16,64,512]{2,1,0:T(8,128)(2,1)S(1)}, u32[]{:S(2)}, u32[]{:S(2)}) async-start(bf16[16,64,512]{2,1,0:T(8,128)(2,1)} %shard_map.91.rest_0_), calls=%async_computation | async-start | bytes 2097152 | tf_op jit(solution)/shard_map/all_to_all | solution.py:271
  76.9 7.0 %copy-start.1 = (bf16[16,64,512]{2,1,0:T(8,128)(2,1)}, bf16[16,64,512]{2,1,0:T(8,128)(2,1)S(1)}, u32[]{:S(2)}) copy-start(bf16[16,64,512]{2,1,0:T(8,128)(2,1)S(1)} %all-to-all-done.x_ref) | copy-start | bytes 3145732
  76.9 53.3 %all-to-all-start.2 = ((bf16[16,64,512]{2,1,0:T(8,128)(2,1)}), bf16[16,64,512]{2,1,0:T(8,128)(2,1)S(1)}, u32[]{:S(2)}, u32[]{:S(2)}) async-start(bf16[16,64,512]{2,1,0:T(8,128)(2,1)} %shard_map.94), calls=%async_computation.2 | async-start | bytes 2097152 | tf_op jit(solution)/shard_map/all_to_all | solution.py:271
  99.6 2.1 %collective-permute-start = (bf16[8,64,512]{2,1,0:T(8,128)(2,1)}, bf16[8,64,512]{2,1,0:T(8,128)(2,1)S(1)}, u32[]{:S(2)}, u32[]{:S(2)}) collective-permute-start(bf16[8,64,512]{2,1,0:T(8,128)(2,1)} %get-tuple-element.8), channel_id=1, source_target_pairs={{0,1},{1,0},{2,3},{3,2},{4,5},{5,4},{6,7},{7,6},{8,9},{9,8},{10,11... | collective-permute-start | bytes 1572872 | tf_op jit(solution)/shard_map/ppermute | solution.py:301
  101.8 34.3 %collective-permute-start.1 = (bf16[2,64,512]{2,1,0:T(8,128)(2,1)S(1)}, bf16[2,64,512]{2,1,0:T(8,128)(2,1)S(1)}, u32[]{:S(2)}, u32[]{:S(2)}) collective-permute-start(bf16[2,64,512]{2,1,0:T(8,128)(2,1)S(1)} %pad_maximum_fusion), channel_id=1, source_target_pairs={{0,8},{1,9},{2,10},{3,11},{4,12},{5,13},{6,14},{7,15},{8,0},{9,1},... | collective-permute-start | bytes 393224 | tf_op jit(solution)/shard_map/ppermute | solution.py:301
  104.2 31.9 %collective-permute-start.2 = (bf16[2,64,512]{2,1,0:T(8,128)(2,1)S(1)}, bf16[2,64,512]{2,1,0:T(8,128)(2,1)S(1)}, u32[]{:S(2)}, u32[]{:S(2)}) collective-permute-start(bf16[2,64,512]{2,1,0:T(8,128)(2,1)S(1)} %pad_maximum_fusion.1), channel_id=1, source_target_pairs={{0,10},{1,11},{2,8},{3,9},{4,14},{5,15},{6,12},{7,13},{8,2},{9,3},... | collective-permute-start | bytes 393224 | tf_op jit(solution)/shard_map/ppermute | solution.py:301
  104.5 5.4 %collective-permute-start.5 = (bf16[2,64,512]{2,1,0:T(8,128)(2,1)S(1)}, bf16[2,64,512]{2,1,0:T(8,128)(2,1)S(1)}, u32[]{:S(2)}, u32[]{:S(2)}) collective-permute-start(bf16[2,64,512]{2,1,0:T(8,128)(2,1)S(1)} %pad_maximum_fusion.5), channel_id=1, source_target_pairs={{0,2},{1,3},{2,0},{3,1},{4,6},{5,7},{6,4},{7,5},{8,10},{9,11},{10,... | collective-permute-start | bytes 393224 | tf_op jit(solution)/shard_map/ppermute | solution.py:301
  106.4 7.3 %collective-permute-start.6 = (bf16[2,64,512]{2,1,0:T(8,128)(2,1)S(1)}, bf16[2,64,512]{2,1,0:T(8,128)(2,1)S(1)}, u32[]{:S(2)}, u32[]{:S(2)}) collective-permute-start(bf16[2,64,512]{2,1,0:T(8,128)(2,1)S(1)} %pad_maximum_fusion.6), channel_id=1, source_target_pairs={{0,4},{1,5},{2,6},{3,7},{4,0},{5,1},{6,2},{7,3},{8,12},{9,13},{10,... | collective-permute-start | bytes 393224 | tf_op jit(solution)/shard_map/ppermute | solution.py:301
  108.0 25.5 %collective-permute-start.7 = (bf16[2,64,512]{2,1,0:T(8,128)(2,1)S(1)}, bf16[2,64,512]{2,1,0:T(8,128)(2,1)S(1)}, u32[]{:S(2)}, u32[]{:S(2)}) collective-permute-start(bf16[2,64,512]{2,1,0:T(8,128)(2,1)S(1)} %pad_maximum_fusion.7), channel_id=1, source_target_pairs={{0,6},{1,7},{2,4},{3,5},{4,2},{5,3},{6,0},{7,1},{8,14},{9,15},{10,... | collective-permute-start | bytes 393224 | tf_op jit(solution)/shard_map/ppermute | solution.py:301
  109.9 23.5 %copy-start.5 = (bf16[2,64,512]{2,1,0:T(8,128)(2,1)}, bf16[2,64,512]{2,1,0:T(8,128)(2,1)S(1)}, u32[]{:S(2)}) copy-start(bf16[2,64,512]{2,1,0:T(8,128)(2,1)S(1)} %collective-permute-done.5.refs_1_) | copy-start | bytes 393220
  109.9 26.2 %collective-permute-start.3 = (bf16[2,64,512]{2,1,0:T(8,128)(2,1)S(1)}, bf16[2,64,512]{2,1,0:T(8,128)(2,1)S(1)}, u32[]{:S(2)}, u32[]{:S(2)}) collective-permute-start(bf16[2,64,512]{2,1,0:T(8,128)(2,1)S(1)} %pad_maximum_fusion.2), channel_id=1, source_target_pairs={{0,12},{1,13},{2,14},{3,15},{4,8},{5,9},{6,10},{7,11},{8,4},{9,5},... | collective-permute-start | bytes 393224 | tf_op jit(solution)/shard_map/ppermute | solution.py:301
  113.7 19.7 %copy-start.7 = (bf16[2,64,512]{2,1,0:T(8,128)(2,1)}, bf16[2,64,512]{2,1,0:T(8,128)(2,1)S(1)}, u32[]{:S(2)}) copy-start(bf16[2,64,512]{2,1,0:T(8,128)(2,1)S(1)} %collective-permute-done.6.refs_2_) | copy-start | bytes 393220
  113.7 22.4 %collective-permute-start.4 = (bf16[2,64,512]{2,1,0:T(8,128)(2,1)S(1)}, bf16[2,64,512]{2,1,0:T(8,128)(2,1)S(1)}, u32[]{:S(2)}, u32[]{:S(2)}) collective-permute-start(bf16[2,64,512]{2,1,0:T(8,128)(2,1)S(1)} %pad_maximum_fusion.3), channel_id=1, source_target_pairs={{0,14},{1,15},{2,12},{3,13},{4,10},{5,11},{6,8},{7,9},{8,6},{9,7},... | collective-permute-start | bytes 393224 | tf_op jit(solution)/shard_map/ppermute | solution.py:301
  130.2 1.0 copy-start
  133.4 0.6 copy-start.9
  136.1 0.6 copy-start.3
  136.1 0.7 copy-start.4
  136.1 0.7 copy-start.6
  136.8 0.6 copy-start.8

commit v8 on v6

--- a/solution.py
+++ b/solution.py
@@ -234,10 +234,14 @@
     frame_lines(x_ref, fp_ref, fo_ref, we_ref, wc_ref, store)
 
 
-def frame_sort_kernel(x_ref, fp_ref, fo_ref, we_ref, wc_ref, place_ref, out_ref):
+def frame_sort_kernel(x_ref, fp_ref, fo_ref, we_ref, wc_ref, place_ref, own_ref, other_ref):
+    first = place_ref[0] == 0
+
     def store(at, z):
-        for f in range(z.shape[0]):
-            out_ref[place_ref[f % 2], place_ref[2 + f // 2], at, :] = z[f]
+        for f in range(0, z.shape[0], 2):
+            step = place_ref[2 + f // 2]
+            own_ref[step, at, :] = jnp.where(first, z[f], z[f + 1])
+            other_ref[step, at, :] = jnp.where(first, z[f + 1], z[f])
 
     frame_lines(x_ref, fp_ref, fo_ref, we_ref, wc_ref, store)
 
@@ -307,21 +311,21 @@
         unit * 12 * count,
     )
     one = exchange(one).reshape(count * columns, width)
-    two = local_call(
+    own, other = local_call(
         frame_sort_kernel,
-        like(2, chips, share, width),
+        [like(chips, share, width)] * 2,
         (two, *weights, place),
         [VMEM] * 5 + [SMEM],
         unit * 12 * count,
     )
-    other = hop(two[1], 1)
-    pieces = [hop(jnp.stack([two[0, s], other[s]]), 2 * s) for s in range(1, chips)]
+    other = hop(other, 1)
+    pieces = [hop(jnp.stack([own[s], other[s]]), 2 * s) for s in range(1, chips)]
     whole = like(rows * columns, width)
     result = local_call(head_kernel, whole, (one,), [VMEM], unit, [pltpu.SemaphoreType.DMA], ANY)
     result = local_call(
         functools.partial(gather_kernel, count * columns),
         whole,
-        (place, two[0, 0], other[0], *pieces, result),
+        (place, own[0], other[0], *pieces, result),
         [SMEM] + [VMEM] * (chips + 1) + [ANY],
         unit,
         [pltpu.SemaphoreType.DMA((2 * chips,))],

time: 137 us -> 136 us (level)
    slice x0 -> x1, local copies, waits for them, and re-layouts: none -> 1.73 us  [per_device(): own[s]]
    another operation x1 -> x0, local copies, waits for them, and re-layouts: 1.72 us -> none  [per_device(): jnp.stack([two[0, s], other[s]])]
  transfers between devices with their start and end apart: 11 -> 11, of which waited for: 6 -> 8; matrix products, arithmetic and copies ran while one was open for 3% -> 2% of each run, Pallas kernels for 38% -> 38%
where the time goes in v8:
time: 136 us; the launch traced here: 135 us
  Pallas kernels  71.9 us (53%)
  waiting for transfers between devices  35 us (26%)
  starting transfers between devices  23.5 us (17%)
  local copies, waits for them, and re-layouts  4.71 us (3%)
    pallas_call x6, Pallas kernels, local_call(): pl.pallas_call(kernel, out_shape=out_shape, in_specs=specs, out_specs=jax...  71.9 us
    ppermute x8, waiting for transfers between devices, hop(): return lax.ppermute(block, 'frame', [(i, i ^ step) for i in range(owners)])  19 us
    all_to_all x3, waiting for transfers between devices, exchange(): lax.all_to_all(blocks, 'frame', split_axis=0, concat_axis=0, tiled=True)  16 us
    all_to_all x3, starting transfers between devices, exchange(): lax.all_to_all(blocks, 'frame', split_axis=0, concat_axis=0, tiled=True)  15.5 us
    ppermute x8, starting transfers between devices, hop(): return lax.ppermute(block, 'frame', [(i, i ^ step) for i in range(owners)])  7.99 us
  transfers between devices with their start and end apart: 11, of which 8 were waited for; matrix products, arithmetic and copies ran while one was open for 2% of the time, Pallas kernels for 38%

profile of v8, /device:TPU:18, one launch (start us, length us, event | category | flops | bytes accessed | tf_op | source)
XLA Modules:
  0.0 135.5 jit_solution(15649390262463329816)
XLA Ops:
  0.0 17.9 %shard_map.93 = bf16[16,64,512]{2,1,0:T(8,128)(2,1)} custom-call(bf16[32,64,512]{2,1,0:T(8,128)(2,1)} %bitcast.18, bf16[512,1536]{1,0:T(8,128)(2,1)} %cp_hbm.3, bf16[512,512]{1,0:T(8,128)(2,1)} %co_hbm.3, bf16[512,1536]{1,0:T(8,128)(2,1)} %rp_hbm.3, bf16[512,512]{1,0:T(8,128)(2,1)} %ro_hbm.3), custom_call_target="tpu_custom_call" | custom-call | flops 5368709120 | bytes 6291456 | tf_op jit(solution)/shard_map/pallas_call | solution.py:146
  17.9 6.2 %all-to-all-start.1 = ((bf16[16,64,512]{2,1,0:T(8,128)(2,1)}), bf16[16,64,512]{2,1,0:T(8,128)(2,1)S(1)}, u32[]{:S(2)}, u32[]{:S(2)}) async-start(bf16[16,64,512]{2,1,0:T(8,128)(2,1)} %shard_map.93), calls=%async_computation.1 | async-start | bytes 2097152 | tf_op jit(solution)/shard_map/all_to_all | solution.py:272
  24.1 18.1 %shard_map.91.rest_0_ = bf16[16,64,512]{2,1,0:T(8,128)(2,1)} custom-call(bf16[32,64,512]{2,1,0:T(8,128)(2,1)} %bitcast.19, bf16[512,1536]{1,0:T(8,128)(2,1)} %cp_hbm.3, bf16[512,512]{1,0:T(8,128)(2,1)} %co_hbm.3, bf16[512,1536]{1,0:T(8,128)(2,1)} %rp_hbm.3, bf16[512,512]{1,0:T(8,128)(2,1)} %ro_hbm.3), custom_call_target="tpu_custom_call" | custom-call | flops 5368709120 | bytes 6291456 | tf_op jit(solution)/shard_map/pallas_call | solution.py:146
  42.2 7.0 %all-to-all-done.1.x_ref = bf16[16,64,512]{2,1,0:T(8,128)(2,1)S(1)} async-done(((bf16[16,64,512]{2,1,0:T(8,128)(2,1)}), bf16[16,64,512]{2,1,0:T(8,128)(2,1)S(1)}, u32[]{:S(2)}, u32[]{:S(2)}) %all-to-all-start.1) | async-done | bytes 1048608 | tf_op jit(solution)/shard_map/all_to_all | solution.py:272
  49.3 4.6 %all-to-all-start = ((bf16[16,64,512]{2,1,0:T(8,128)(2,1)}), bf16[16,64,512]{2,1,0:T(8,128)(2,1)S(1)}, u32[]{:S(2)}, u32[]{:S(2)}) async-start(bf16[16,64,512]{2,1,0:T(8,128)(2,1)} %shard_map.91.rest_0_), calls=%async_computation | async-start | bytes 2097152 | tf_op jit(solution)/shard_map/all_to_all | solution.py:272
  53.9 0.6 stack.64.place_ref
  54.6 15.6 %shard_map.94 = bf16[16,64,512]{2,1,0:T(8,128)(2,1)} custom-call(bf16[16,64,512]{2,1,0:T(8,128)(2,1)} %copy-done.2, bf16[512,1536]{1,0:T(8,128)(2,1)} %fp_ref.3, bf16[512,512]{1,0:T(8,128)(2,1)} %fo_ref.3, bf16[512,2048]{1,0:T(8,128)(2,1)} %we_ref.3, bf16[2048,512]{1,0:T(8,128)(2,1)} %wc_ref.3, bf16[16,64,512]{2,1,0:T(8,128)(2,1)} %shard_map.91.rest_0_), custom_call_target="tpu_custom_call" | custom-call | flops 6442450944 | bytes 8388608 | tf_op jit(solution)/shard_map/pallas_call | solution.py:146
  70.2 8.9 %all-to-all-done.x_ref = bf16[16,64,512]{2,1,0:T(8,128)(2,1)S(1)} async-done(((bf16[16,64,512]{2,1,0:T(8,128)(2,1)}), bf16[16,64,512]{2,1,0:T(8,128)(2,1)S(1)}, u32[]{:S(2)}, u32[]{:S(2)}) %all-to-all-start) | async-done | bytes 1048608 | tf_op jit(solution)/shard_map/all_to_all | solution.py:272
  79.1 4.6 %all-to-all-start.2 = ((bf16[16,64,512]{2,1,0:T(8,128)(2,1)}), bf16[16,64,512]{2,1,0:T(8,128)(2,1)S(1)}, u32[]{:S(2)}, u32[]{:S(2)}) async-start(bf16[16,64,512]{2,1,0:T(8,128)(2,1)} %shard_map.94), calls=%async_computation.2 | async-start | bytes 2097152 | tf_op jit(solution)/shard_map/all_to_all | solution.py:272
  83.7 15.7 %shard_map.92 = (bf16[8,64,512]{2,1,0:T(8,128)(2,1)}, bf16[8,64,512]{2,1,0:T(8,128)(2,1)}) custom-call(bf16[16,64,512]{2,1,0:T(8,128)(2,1)} %copy-done.1, bf16[512,1536]{1,0:T(8,128)(2,1)} %fp_ref.3, bf16[512,512]{1,0:T(8,128)(2,1)} %fo_ref.3, bf16[512,2048]{1,0:T(8,128)(2,1)} %we_ref.3, bf16[2048,512]{1,0:T(8,128)(2,1)} %wc_ref.3, s32[10]{0:T(128)} %stack.64.place_ref), custom_call_target="tpu_custom_call" | custom-call | flops 6442450944 | bytes 7340052 | tf_op jit(solution)/shard_map/pallas_call | solution.py:146
  99.4 0.1 collective-permute-start
  99.6 1.7 %fusion = (bf16[1,64,512]{2,1,0:T(8,128)(2,1)S(1)}, bf16[1,64,512]{2,1,0:T(8,128)(2,1)S(1)}, bf16[1,64,512]{2,1,0:T(8,128)(2,1)S(1)}, bf16[1,64,512]{2,1,0:T(8,1...) fusion(bf16[8,64,512]{2,1,0:T(8,128)(2,1)} %get-tuple-element.7), kind=kLoop, calls=%fused_computation.9 | loop fusion | bytes 1048576 | tf_op jit(solution)/shard_map/slice | solution.py:322
  101.3 0.2 collective-permute-done
  101.6 0.7 fusion.1
  102.2 1.5 %collective-permute-start.1 = (bf16[2,64,512]{2,1,0:T(8,128)(2,1)S(1)}, bf16[2,64,512]{2,1,0:T(8,128)(2,1)S(1)}, u32[]{:S(2)}, u32[]{:S(2)}) collective-permute-start(bf16[2,64,512]{2,1,0:T(8,128)(2,1)S(1)} %pad_maximum_fusion), channel_id=1, source_target_pairs={{0,2},{1,3},{2,0},{3,1},{4,6},{5,7},{6,4},{7,5},{8,10},{9,11},{10,... | collective-permute-start | bytes 393224 | tf_op jit(solution)/shard_map/ppermute | solution.py:302
  103.8 1.5 %collective-permute-start.2 = (bf16[2,64,512]{2,1,0:T(8,128)(2,1)S(1)}, bf16[2,64,512]{2,1,0:T(8,128)(2,1)S(1)}, u32[]{:S(2)}, u32[]{:S(2)}) collective-permute-start(bf16[2,64,512]{2,1,0:T(8,128)(2,1)S(1)} %pad_maximum_fusion.1), channel_id=1, source_target_pairs={{0,4},{1,5},{2,6},{3,7},{4,0},{5,1},{6,2},{7,3},{8,12},{9,13},{10,... | collective-permute-start | bytes 393224 | tf_op jit(solution)/shard_map/ppermute | solution.py:302
  105.3 0.6 collective-permute-start.3
  106.0 0.2 collective-permute-start.4
  106.2 3.7 %collective-permute-start.5 = (bf16[2,64,512]{2,1,0:T(8,128)(2,1)S(1)}, bf16[2,64,512]{2,1,0:T(8,128)(2,1)S(1)}, u32[]{:S(2)}, u32[]{:S(2)}) collective-permute-start(bf16[2,64,512]{2,1,0:T(8,128)(2,1)S(1)} %pad_maximum_fusion.4), channel_id=1, source_target_pairs={{0,10},{1,11},{2,8},{3,9},{4,14},{5,15},{6,12},{7,13},{8,2},{9,3},... | collective-permute-start | bytes 393224 | tf_op jit(solution)/shard_map/ppermute | solution.py:302
  110.0 1.4 %collective-permute-done.1.rest_0_ = bf16[2,64,512]{2,1,0:T(8,128)(2,1)S(1)} collective-permute-done((bf16[2,64,512]{2,1,0:T(8,128)(2,1)S(1)}, bf16[2,64,512]{2,1,0:T(8,128)(2,1)S(1)}, u32[]{:S(2)}, u32[]{:S(2)}) %collective-permute-start.1) | collective-permute-done | bytes 131104 | tf_op jit(solution)/shard_map/ppermute | solution.py:302
  111.4 0.2 collective-permute-start.6
  111.6 1.4 %collective-permute-done.2.rest_1_ = bf16[2,64,512]{2,1,0:T(8,128)(2,1)S(1)} collective-permute-done((bf16[2,64,512]{2,1,0:T(8,128)(2,1)S(1)}, bf16[2,64,512]{2,1,0:T(8,128)(2,1)S(1)}, u32[]{:S(2)}, u32[]{:S(2)}) %collective-permute-start.2) | collective-permute-done | bytes 131104 | tf_op jit(solution)/shard_map/ppermute | solution.py:302
  113.1 0.0 collective-permute-start.7
  113.1 0.0 all-to-all-done.2
  113.1 1.0 copy-done
  114.1 2.2 %shard_map.95.rest_7_ = bf16[2048,512]{1,0:T(8,128)(2,1)} custom-call(bf16[1024,512]{1,0:T(8,128)(2,1)} %bitcast.17), custom_call_target="tpu_custom_call" | custom-call | flops 33554432 | bytes 1048576 | tf_op jit(solution)/shard_map/pallas_call | solution.py:146
  116.3 0.0 collective-permute-done.3.rest_2_
  116.4 8.1 %collective-permute-done.5.rest_4_ = bf16[2,64,512]{2,1,0:T(8,128)(2,1)S(1)} collective-permute-done((bf16[2,64,512]{2,1,0:T(8,128)(2,1)S(1)}, bf16[2,64,512]{2,1,0:T(8,128)(2,1)S(1)}, u32[]{:S(2)}, u32[]{:S(2)}) %collective-permute-start.5) | collective-permute-done | bytes 131104 | tf_op jit(solution)/shard_map/ppermute | solution.py:302
  124.5 5.4 %collective-permute-done.6.rest_5_ = bf16[2,64,512]{2,1,0:T(8,128)(2,1)S(1)} collective-permute-done((bf16[2,64,512]{2,1,0:T(8,128)(2,1)S(1)}, bf16[2,64,512]{2,1,0:T(8,128)(2,1)S(1)}, u32[]{:S(2)}, u32[]{:S(2)}) %collective-permute-start.6) | collective-permute-done | bytes 131104 | tf_op jit(solution)/shard_map/ppermute | solution.py:302
  129.9 2.3 %collective-permute-done.7.rest_6_ = bf16[2,64,512]{2,1,0:T(8,128)(2,1)S(1)} collective-permute-done((bf16[2,64,512]{2,1,0:T(8,128)(2,1)S(1)}, bf16[2,64,512]{2,1,0:T(8,128)(2,1)S(1)}, u32[]{:S(2)}, u32[]{:S(2)}) %collective-permute-start.7) | collective-permute-done | bytes 131104 | tf_op jit(solution)/shard_map/ppermute | solution.py:302
  132.3 0.6 copy-done.9
  132.9 2.4 %shard_map.96 = bf16[2048,512]{1,0:T(8,128)(2,1)} custom-call(s32[10]{0:T(128)} %stack.64.place_ref, bf16[64,512]{1,0:T(8,128)(2,1)} %get-tuple-element.16.own_ref, bf16[64,512]{1,0:T(8,128)(2,1)} %get-tuple-element.24.other_ref, bf16[2,64,512]{2,1,0:T(8,128)(2,1)} %copy-done.3, bf16[2,64,512]{2,1,0:T(8,128)(2,1)} %copy-done.4, ...), custom_call_target="tpu_custom_call", output_to_operand_aliasing={{}: (10, {})} | custom-call | flops 33554432 | bytes 3145748 | tf_op jit(solution)/shard_map/pallas_call | solution.py:146
  (26 shorter events, 0.1 us)
Async XLA Ops:
  17.9 31.4 %all-to-all-start.1 = ((bf16[16,64,512]{2,1,0:T(8,128)(2,1)}), bf16[16,64,512]{2,1,0:T(8,128)(2,1)S(1)}, u32[]{:S(2)}, u32[]{:S(2)}) async-start(bf16[16,64,512]{2,1,0:T(8,128)(2,1)} %shard_map.93), calls=%async_computation.1 | async-start | bytes 2097152 | tf_op jit(solution)/shard_map/all_to_all | solution.py:272
  49.3 5.3 %copy-start.2 = (bf16[16,64,512]{2,1,0:T(8,128)(2,1)}, bf16[16,64,512]{2,1,0:T(8,128)(2,1)S(1)}, u32[]{:S(2)}) copy-start(bf16[16,64,512]{2,1,0:T(8,128)(2,1)S(1)} %all-to-all-done.1.x_ref) | copy-start | bytes 3145732
  49.3 29.8 %all-to-all-start = ((bf16[16,64,512]{2,1,0:T(8,128)(2,1)}), bf16[16,64,512]{2,1,0:T(8,128)(2,1)S(1)}, u32[]{:S(2)}, u32[]{:S(2)}) async-start(bf16[16,64,512]{2,1,0:T(8,128)(2,1)} %shard_map.91.rest_0_), calls=%async_computation | async-start | bytes 2097152 | tf_op jit(solution)/shard_map/all_to_all | solution.py:272
  79.1 4.6 %copy-start.1 = (bf16[16,64,512]{2,1,0:T(8,128)(2,1)}, bf16[16,64,512]{2,1,0:T(8,128)(2,1)S(1)}, u32[]{:S(2)}) copy-start(bf16[16,64,512]{2,1,0:T(8,128)(2,1)S(1)} %all-to-all-done.x_ref) | copy-start | bytes 3145732
  79.1 34.0 %all-to-all-start.2 = ((bf16[16,64,512]{2,1,0:T(8,128)(2,1)}), bf16[16,64,512]{2,1,0:T(8,128)(2,1)S(1)}, u32[]{:S(2)}, u32[]{:S(2)}) async-start(bf16[16,64,512]{2,1,0:T(8,128)(2,1)} %shard_map.94), calls=%async_computation.2 | async-start | bytes 2097152 | tf_op jit(solution)/shard_map/all_to_all | solution.py:272
  99.4 2.1 %collective-permute-start = (bf16[8,64,512]{2,1,0:T(8,128)(2,1)}, bf16[8,64,512]{2,1,0:T(8,128)(2,1)S(1)}, u32[]{:S(2)}, u32[]{:S(2)}) collective-permute-start(bf16[8,64,512]{2,1,0:T(8,128)(2,1)} %get-tuple-element.8), channel_id=1, source_target_pairs={{0,1},{1,0},{2,3},{3,2},{4,5},{5,4},{6,7},{7,6},{8,9},{9,8},{10,11... | collective-permute-start | bytes 1572872 | tf_op jit(solution)/shard_map/ppermute | solution.py:302
  102.2 9.2 %collective-permute-start.1 = (bf16[2,64,512]{2,1,0:T(8,128)(2,1)S(1)}, bf16[2,64,512]{2,1,0:T(8,128)(2,1)S(1)}, u32[]{:S(2)}, u32[]{:S(2)}) collective-permute-start(bf16[2,64,512]{2,1,0:T(8,128)(2,1)S(1)} %pad_maximum_fusion), channel_id=1, source_target_pairs={{0,2},{1,3},{2,0},{3,1},{4,6},{5,7},{6,4},{7,5},{8,10},{9,11},{10,... | collective-permute-start | bytes 393224 | tf_op jit(solution)/shard_map/ppermute | solution.py:302
  103.8 9.3 %collective-permute-start.2 = (bf16[2,64,512]{2,1,0:T(8,128)(2,1)S(1)}, bf16[2,64,512]{2,1,0:T(8,128)(2,1)S(1)}, u32[]{:S(2)}, u32[]{:S(2)}) collective-permute-start(bf16[2,64,512]{2,1,0:T(8,128)(2,1)S(1)} %pad_maximum_fusion.1), channel_id=1, source_target_pairs={{0,4},{1,5},{2,6},{3,7},{4,0},{5,1},{6,2},{7,3},{8,12},{9,13},{10,... | collective-permute-start | bytes 393224 | tf_op jit(solution)/shard_map/ppermute | solution.py:302
  105.3 11.0 %collective-permute-start.3 = (bf16[2,64,512]{2,1,0:T(8,128)(2,1)S(1)}, bf16[2,64,512]{2,1,0:T(8,128)(2,1)S(1)}, u32[]{:S(2)}, u32[]{:S(2)}) collective-permute-start(bf16[2,64,512]{2,1,0:T(8,128)(2,1)S(1)} %pad_maximum_fusion.2), channel_id=1, source_target_pairs={{0,6},{1,7},{2,4},{3,5},{4,2},{5,3},{6,0},{7,1},{8,14},{9,15},{10,... | collective-permute-start | bytes 393224 | tf_op jit(solution)/shard_map/ppermute | solution.py:302
  106.0 10.4 %collective-permute-start.4 = (bf16[2,64,512]{2,1,0:T(8,128)(2,1)S(1)}, bf16[2,64,512]{2,1,0:T(8,128)(2,1)S(1)}, u32[]{:S(2)}, u32[]{:S(2)}) collective-permute-start(bf16[2,64,512]{2,1,0:T(8,128)(2,1)S(1)} %pad_maximum_fusion.3), channel_id=1, source_target_pairs={{0,8},{1,9},{2,10},{3,11},{4,12},{5,13},{6,14},{7,15},{8,0},{9,1},... | collective-permute-start | bytes 393224 | tf_op jit(solution)/shard_map/ppermute | solution.py:302
  106.2 18.3 %collective-permute-start.5 = (bf16[2,64,512]{2,1,0:T(8,128)(2,1)S(1)}, bf16[2,64,512]{2,1,0:T(8,128)(2,1)S(1)}, u32[]{:S(2)}, u32[]{:S(2)}) collective-permute-start(bf16[2,64,512]{2,1,0:T(8,128)(2,1)S(1)} %pad_maximum_fusion.4), channel_id=1, source_target_pairs={{0,10},{1,11},{2,8},{3,9},{4,14},{5,15},{6,12},{7,13},{8,2},{9,3},... | collective-permute-start | bytes 393224 | tf_op jit(solution)/shard_map/ppermute | solution.py:302
  111.4 20.8 %copy-start.3 = (bf16[2,64,512]{2,1,0:T(8,128)(2,1)}, bf16[2,64,512]{2,1,0:T(8,128)(2,1)S(1)}, u32[]{:S(2)}) copy-start(bf16[2,64,512]{2,1,0:T(8,128)(2,1)S(1)} %collective-permute-done.1.rest_0_) | copy-start | bytes 393220
  111.4 18.5 %collective-permute-start.6 = (bf16[2,64,512]{2,1,0:T(8,128)(2,1)S(1)}, bf16[2,64,512]{2,1,0:T(8,128)(2,1)S(1)}, u32[]{:S(2)}, u32[]{:S(2)}) collective-permute-start(bf16[2,64,512]{2,1,0:T(8,128)(2,1)S(1)} %pad_maximum_fusion.5), channel_id=1, source_target_pairs={{0,12},{1,13},{2,14},{3,15},{4,8},{5,9},{6,10},{7,11},{8,4},{9,5},... | collective-permute-start | bytes 393224 | tf_op jit(solution)/shard_map/ppermute | solution.py:302
  113.1 19.2 %copy-start.4 = (bf16[2,64,512]{2,1,0:T(8,128)(2,1)}, bf16[2,64,512]{2,1,0:T(8,128)(2,1)S(1)}, u32[]{:S(2)}) copy-start(bf16[2,64,512]{2,1,0:T(8,128)(2,1)S(1)} %collective-permute-done.2.rest_1_) | copy-start | bytes 393220
  113.1 19.2 %collective-permute-start.7 = (bf16[2,64,512]{2,1,0:T(8,128)(2,1)S(1)}, bf16[2,64,512]{2,1,0:T(8,128)(2,1)S(1)}, u32[]{:S(2)}, u32[]{:S(2)}) collective-permute-start(bf16[2,64,512]{2,1,0:T(8,128)(2,1)S(1)} %pad_maximum_fusion.6), channel_id=1, source_target_pairs={{0,14},{1,15},{2,12},{3,13},{4,10},{5,11},{6,8},{7,9},{8,6},{9,7},... | collective-permute-start | bytes 393224 | tf_op jit(solution)/shard_map/ppermute | solution.py:302
  113.1 1.1 copy-start
  116.3 15.9 %copy-start.5 = (bf16[2,64,512]{2,1,0:T(8,128)(2,1)}, bf16[2,64,512]{2,1,0:T(8,128)(2,1)S(1)}, u32[]{:S(2)}) copy-start(bf16[2,64,512]{2,1,0:T(8,128)(2,1)S(1)} %collective-permute-done.3.rest_2_) | copy-start | bytes 393220
  116.4 15.9 %copy-start.6 = (bf16[2,64,512]{2,1,0:T(8,128)(2,1)}, bf16[2,64,512]{2,1,0:T(8,128)(2,1)S(1)}, u32[]{:S(2)}) copy-start(bf16[2,64,512]{2,1,0:T(8,128)(2,1)S(1)} %collective-permute-done.4.rest_3_) | copy-start | bytes 393220
  124.5 7.8 %copy-start.7 = (bf16[2,64,512]{2,1,0:T(8,128)(2,1)}, bf16[2,64,512]{2,1,0:T(8,128)(2,1)S(1)}, u32[]{:S(2)}) copy-start(bf16[2,64,512]{2,1,0:T(8,128)(2,1)S(1)} %collective-permute-done.5.rest_4_) | copy-start | bytes 393220
  129.9 2.4 %copy-start.8 = (bf16[2,64,512]{2,1,0:T(8,128)(2,1)}, bf16[2,64,512]{2,1,0:T(8,128)(2,1)S(1)}, u32[]{:S(2)}) copy-start(bf16[2,64,512]{2,1,0:T(8,128)(2,1)S(1)} %collective-permute-done.6.rest_5_) | copy-start | bytes 393220
  132.3 0.7 copy-start.9
